TPU v7x, 256 devices: a whole 4x4x8 slice. The times are simulated.
256 devices in a mesh: ctx: 8 (over y, core), tp: 32 (over z, x).
Axes of the slice: x: 4, y: 4, z: 8, core: 2. Of those that a mesh axis runs over, the one named last changes fastest.
Arguments:
- query_in: bfloat16 [8192, 8192], P('ctx', 'tp'), may hold values from -6 to 6
- key_in: bfloat16 [8192, 8192], P('ctx', 'tp'), may hold values from -6 to 6
- value_in: bfloat16 [8192, 8192], P('ctx', 'tp'), may hold values from -6 to 6
- short_taps: float32 [3, 7, 8192], P(None, None, 'tp'), may hold values from -2 to 2
- modal_poles: float32 [16, 8192], P(None, 'tp'), may hold values from 0 to 1, as said below
- modal_residues: float32 [16, 8192], P(None, 'tp'), may hold values from -0.5 to 0.5
- out_weight: bfloat16 [8192, 8192], P('tp'), may hold values from -0.0625 to 0.0625
- grad_out: bfloat16 [8192, 8192], P('ctx', 'tp'), may hold values from -6 to 6
Outputs:
- gated: bfloat16 [8192, 8192], P('ctx', 'tp')
- grad_query: bfloat16 [8192, 8192], P('ctx', 'tp')
- grad_key: bfloat16 [8192, 8192], P('ctx', 'tp')
- grad_value: bfloat16 [8192, 8192], P('ctx', 'tp')
Inputs may be any that keep to these rules, and one draw needn't show every extreme that they name: `modal_poles`: every pole lies strictly between 0 and 1.
All inputs are finite; a program needn't handle non-finite values.
Results may differ from a plain program's by a relative error of at most 0.0017.
Values may be sent and summed in bfloat16 or wider, within the bound.
No kernel may reach another device: no remote copies, remote signals or barrier semaphores. Data moves between devices by JAX's collectives and lax.ppermute only.
A program may use at most 128 MiB of HBM per device.

v0:
```python
import functools
import jax
import jax.numpy as jnp
from jax import lax
from jax.experimental import pallas as pl
from jax.experimental.pallas import tpu as pltpu
from jax.sharding import Mesh, PartitionSpec as P

LANES = 128
PARTS = 8
RIM = 8
X_COUNT = 4
TILE = 256
HEAD = 16
SPAN = 32768.0
TINY = 1e-30
LEAST = 1e-37
VMEM_LIMIT = 16 * 1024 * 1024


def power(base, exponent):
    result = None
    while exponent:
        if exponent & 1:
            result = base if result is None else result * base
        exponent >>= 1
        if exponent:
            base = base * base
    return result


def rows_of(ref, lanes):
    return [ref[m : m + 1, lanes] for m in range(ref.shape[0])]


def spread(row):
    return jnp.broadcast_to(row, (PARTS, LANES))


def lane_blocks(width):
    return [(n, pl.ds(n * LANES, LANES)) for n in range(width // LANES)]


def short_filters(q_ref, k_ref, v_ref, prior_ref, taps_ref, poles_ref, qs_ref, ks_ref, vs_ref, ends_ref, own_ref, natural):
    tokens, width = q_ref.shape
    tap_count = taps_ref.shape[1]
    modes = poles_ref.shape[0]
    steps = tokens // PARTS
    for which, (source, target) in enumerate(((q_ref, qs_ref), (k_ref, ks_ref), (v_ref, vs_ref))):
        for block, lanes in lane_blocks(width):
            natural[block, 0:RIM, :] = prior_ref[which, :, lanes].astype(jnp.float32)[prior_ref.shape[1] - RIM :]
            natural[block, RIM:, :] = source[:, lanes].astype(jnp.float32)
        for block, lanes in lane_blocks(width):
            taps = [spread(taps_ref[which, j : j + 1, lanes]) for j in range(tap_count)]

            def tap_step(i, window):
                fresh = natural[block, pl.ds(RIM + i, PARTS, stride=steps), :]
                window = (fresh,) + window
                total = taps[0] * window[0]
                for j in range(1, tap_count):
                    total = total + taps[j] * window[j]
                target[pl.ds(pl.multiple_of(i * PARTS, PARTS), PARTS), lanes] = total
                return window[:-1]

            before = tuple(
                natural[block, pl.ds(RIM - 1 - d, PARTS, stride=steps), :] for d in range(tap_count - 1)
            )
            lax.fori_loop(0, steps, tap_step, before, unroll=8)
    for block, lanes in lane_blocks(width):
        poles = [spread(row) for row in rows_of(poles_ref, lanes)]

        def state_step(i, states):
            rows = pl.ds(pl.multiple_of(i * PARTS, PARTS), PARTS)
            fresh = ks_ref[rows, lanes] * vs_ref[rows, lanes]
            return tuple(p * s + fresh for p, s in zip(poles, states))

        zero = jnp.zeros((PARTS, LANES), jnp.float32)
        states = lax.fori_loop(0, steps, state_step, (zero,) * modes, unroll=4)
        for m in range(modes):
            ends_ref[m, :, lanes] = states[m]
    part_decay = power(poles_ref[...], steps)
    own = ends_ref[:, 0, :]
    for c in range(1, PARTS):
        own = part_decay * own + ends_ref[:, c, :]
    own_ref[...] = own


def long_forward(qs_ref, ks_ref, vs_ref, ends_ref, before_ref, poles_ref, residues_ref, long_ref, gated_ref, first, natural):
    tokens, width = qs_ref.shape
    modes = poles_ref.shape[0]
    steps = tokens // PARTS
    part_decay = power(poles_ref[...], steps)
    entering = before_ref[...]
    for c in range(PARTS):
        first[:, c, :] = entering
        if c < PARTS - 1:
            entering = part_decay * entering + ends_ref[:, c, :]
    for block, lanes in lane_blocks(width):
        poles = [spread(row) for row in rows_of(poles_ref, lanes)]
        residues = [spread(row) for row in rows_of(residues_ref, lanes)]

        def step(i, states):
            rows = pl.ds(pl.multiple_of(i * PARTS, PARTS), PARTS)
            fresh = ks_ref[rows, lanes] * vs_ref[rows, lanes]
            states = tuple(p * s + fresh for p, s in zip(poles, states))
            total = mixed(residues, states)
            long_ref[rows, lanes] = total
            natural[block, pl.ds(i, PARTS, stride=steps), :] = total * qs_ref[rows, lanes]
            return states

        lax.fori_loop(0, steps, step, tuple(first[m, :, lanes] for m in range(modes)), unroll=4)
    for block, lanes in lane_blocks(width):
        gated_ref[:, lanes] = natural[block].astype(gated_ref.dtype)


def mixed(residues, states):
    return added([r * s for r, s in zip(residues, states)])


def added(terms):
    while len(terms) > 1:
        terms = [a + b for a, b in zip(terms[::2], terms[1::2])] + list(terms[len(terms) // 2 * 2 :])
    return terms[0]


def back_states(kept_ref, one_ref, three_ref, qs_ref, long_ref, poles_ref, mixed_ref, starts_ref, own_ref, rim_ref, rim_starts, natural):
    tokens, width = qs_ref.shape
    modes = poles_ref.shape[0]
    steps = tokens // PARTS
    for block, lanes in lane_blocks(width):
        poles = [spread(row) for row in rows_of(poles_ref, lanes)]

        def add_step(n, carry):
            piece = 64
            row = pl.multiple_of(n * piece, piece)
            tile, inside = row // TILE, pl.multiple_of(row % TILE, piece)
            total = kept_ref[pl.ds(row, piece), lanes]
            for ref in (one_ref, three_ref):
                start = pl.multiple_of(tile * (TILE + HEAD), HEAD)
                total = total + decoded(ref, start, pl.ds(inside, piece), lanes)
            natural[block, pl.ds(row, piece), :] = total
            return carry

        lax.fori_loop(0, tokens // 64, add_step, 0)

        def step(back, states):
            i = steps - 1 - back
            rows = pl.ds(pl.multiple_of(i * PARTS, PARTS), PARTS)
            here = natural[block, pl.ds(i, PARTS, stride=steps), :]
            mixed_ref[rows, lanes] = here
            fresh = here * qs_ref[rows, lanes]
            return tuple(p * s + fresh for p, s in zip(poles, states))

        zero = jnp.zeros((PARTS, LANES), jnp.float32)
        states = lax.fori_loop(0, steps - RIM, step, (zero,) * modes, unroll=4)
        for m in range(modes):
            rim_starts[m, :, lanes] = states[m]
        states = lax.fori_loop(steps - RIM, steps, step, states, unroll=4)
        for m in range(modes):
            starts_ref[m, :, lanes] = states[m]
    part_decay = power(poles_ref[...], steps)
    own = starts_ref[:, PARTS - 1, :]
    for c in range(PARTS - 2, 0, -1):
        own = part_decay * own + starts_ref[:, c, :]
    own_ref[...] = part_decay * own + starts_ref[:, 0, :]
    rim_ref[0:modes, :] = power(poles_ref[...], steps - RIM) * own + rim_starts[:, 0, :]
    for i in range(RIM):
        here = mixed_ref[i * PARTS : i * PARTS + 1, :]
        rim_ref[modes + i : modes + i + 1, :] = here * qs_ref[i * PARTS : i * PARTS + 1, :]
        rim_ref[modes + RIM + i : modes + RIM + i + 1, :] = here * long_ref[i * PARTS : i * PARTS + 1, :]


def back_local(mixed_ref, qs_ref, poles_ref, residues_ref, local_ref):
    tokens, width = qs_ref.shape
    modes = poles_ref.shape[0]
    steps = tokens // PARTS
    for block, lanes in lane_blocks(width):
        poles = [spread(row) for row in rows_of(poles_ref, lanes)]
        residues = [spread(row) for row in rows_of(residues_ref, lanes)]

        def step(back, states):
            i = steps - 1 - back
            rows = pl.ds(pl.multiple_of(i * PARTS, PARTS), PARTS)
            fresh = mixed_ref[rows, lanes] * qs_ref[rows, lanes]
            states = tuple(p * s + fresh for p, s in zip(poles, states))
            local_ref[rows, lanes] = mixed(residues, states)
            return states

        zero = jnp.zeros((PARTS, LANES), jnp.float32)
        lax.fori_loop(0, steps, step, (zero,) * modes, unroll=4)


def short_back(value, rim, taps_ref, which, target, natural):
    tokens, width = target.shape
    tap_count = taps_ref.shape[1]
    steps = tokens // PARTS
    bottom = lax.broadcasted_iota(jnp.int32, (PARTS, LANES), 0) == PARTS - 1
    for block, lanes in lane_blocks(width):
        taps = [spread(taps_ref[which, j : j + 1, lanes]) for j in range(tap_count)]

        def tap_step(back, window):
            i = steps - 1 - back
            window = (value(pl.ds(pl.multiple_of(i * PARTS, PARTS), PARTS), lanes),) + window
            total = taps[0] * window[0]
            for j in range(1, tap_count):
                total = total + taps[j] * window[j]
            natural[block, pl.ds(i, PARTS, stride=steps), :] = total
            return window[:-1]

        after = tuple(
            jnp.where(
                bottom,
                spread(rim(d, lanes)),
                pltpu.roll(value(pl.ds(d * PARTS, PARTS), lanes), PARTS - 1, 0),
            )
            for d in range(tap_count - 1)
        )
        lax.fori_loop(0, steps, tap_step, after, unroll=8)
    for block, lanes in lane_blocks(width):
        target[:, lanes] = natural[block].astype(target.dtype)


def back_query(mixed_ref, long_ref, next_ref, taps_ref, gq_ref, natural):
    first = next_ref.shape[0] - RIM
    short_back(
        lambda rows, lanes: mixed_ref[rows, lanes] * long_ref[rows, lanes],
        lambda d, lanes: next_ref[first + d : first + d + 1, lanes],
        taps_ref, 0, gq_ref, natural,
    )


def back_filters(local_ref, ks_ref, vs_ref, starts_ref, next_ref, beyond_ref, next_kv_ref, taps_ref, poles_ref, residues_ref, gk_ref, gv_ref, last, product, natural, rims):
    tokens, width = ks_ref.shape
    modes = poles_ref.shape[0]
    steps = tokens // PARTS
    poles_all = poles_ref[...]
    residues_all = residues_ref[...]
    entering = next_ref[0:modes, :] + power(poles_all, tokens - RIM) * beyond_ref[...]
    for i in range(RIM - 1, -1, -1):
        entering = poles_all * entering + next_ref[modes + i : modes + i + 1, :]
        here = jnp.sum(residues_all * entering, axis=0, keepdims=True)
        rims[0, i : i + 1, :] = here * next_kv_ref[1, i : i + 1, :]
        rims[1, i : i + 1, :] = here * next_kv_ref[0, i : i + 1, :]
    part_decay = power(poles_all, steps)
    for c in range(PARTS - 1, -1, -1):
        last[:, c, :] = residues_all * entering
        if c:
            entering = part_decay * entering + starts_ref[:, c, :]
    for block, lanes in lane_blocks(width):
        poles = [spread(row) for row in rows_of(poles_ref, lanes)]

        def step(back, fading):
            i = steps - 1 - back
            rows = pl.ds(pl.multiple_of(i * PARTS, PARTS), PARTS)
            fading = tuple(p * s for p, s in zip(poles, fading))
            product[rows, lanes] = local_ref[rows, lanes] + added(fading)
            return fading

        lax.fori_loop(0, steps, step, tuple(last[m, :, lanes] for m in range(modes)), unroll=4)
    for which, other, target in ((1, vs_ref, gk_ref), (2, ks_ref, gv_ref)):
        short_back(
            lambda rows, lanes: product[rows, lanes] * other[rows, lanes],
            lambda d, lanes: rims[which - 1, d : d + 1, lanes],
            taps_ref, which, target, natural,
        )


def pick_shares(place_ref, weight_ref, up_ref, down_ref, arrived):
    rows = weight_ref.shape[0] // 2
    blocks = arrived.shape[2]
    depth = up_ref.shape[1]
    width = depth // blocks
    count = weight_ref.shape[1] // depth
    first = pl.multiple_of(place_ref[2] * rows, rows)
    copies = []
    for side, (message_ref, step) in enumerate(((up_ref, 1), (down_ref, count - 1))):
        for part, (x, begin, size, target) in enumerate(
            (
                (lax.rem(place_ref[0] + step, count), 0, rows, 0),
                (lax.rem(place_ref[0] + 2, count), side * (rows // 2), rows // 2, rows),
            )
        ):
            for z in range(blocks):
                column = pl.multiple_of((z * count + x) * width, width)
                copies.append(
                    pltpu.make_async_copy(
                        weight_ref.at[pl.ds(first + begin, size), pl.ds(column, width)],
                        message_ref.at[pl.ds(target, size), pl.ds(z * width, width)],
                        arrived.at[side, part, z],
                    )
                )
    for copy in copies:
        copy.start()
    for copy in copies:
        copy.wait()


def join_shares(place_ref, share_ref, other_ref, j, weight):
    rows = share_ref.shape[1]
    core = place_ref[2]
    weight[pl.ds(pl.multiple_of(core * rows, rows), rows), :] = share_ref[j]
    weight[pl.ds(pl.multiple_of((1 - core) * rows, rows), rows), :] = other_ref[j]


def ring_product(target_ref, ring, weight_ref, column_of):
    tokens, width = target_ref.shape
    rows = tokens // 2
    first = True
    for n, refs in ring:
        for half in range(2):
            target_rows = pl.ds(half * rows, rows)
            features = refs[half][...] if len(refs) == 2 else refs[0][target_rows, :]
            term = lax.dot_general(
                features,
                weight_ref[:, pl.ds(column_of(n), width)],
                (((1,), (1,)), ((), ())),
                preferred_element_type=jnp.float32,
            )
            target_ref[target_rows, :] = term if first else target_ref[target_rows, :] + term
        first = False


def in_places(early_ref, left_ref, right_ref, *middle):
    count = early_ref.shape[0] + 3
    ring = [(n % count, (early_ref.at[n + 2],)) for n in range(-2, 3)]
    ring += [(3, (left_ref,)), (count - 3, (right_ref,))]
    return ring + [(count // 2, middle)] if middle else ring


def collect(*refs):
    *block_refs, early_ref, arrived = refs
    copies = [
        pltpu.make_async_copy(ref, early_ref.at[n], arrived.at[n]) for n, ref in enumerate(block_refs)
    ]
    for copy in copies:
        copy.start()
    for copy in copies:
        copy.wait()


def encode_tile(total, coded_ref, tile):
    largest = jnp.max(jnp.abs(total), axis=0, keepdims=True) * 1.01
    largest = jnp.maximum(largest, TINY).astype(jnp.bfloat16)
    scaled = total * (SPAN / largest.astype(jnp.float32))
    square = scaled * scaled
    fourth = square * square
    eighth = fourth * fourth
    code = jnp.where(scaled < 0, -eighth, eighth)
    start = pl.multiple_of(tile * (TILE + HEAD), HEAD)
    coded_ref[pl.ds(start, HEAD), :] = jnp.broadcast_to(largest, (HEAD, largest.shape[1]))
    coded_ref[pl.ds(start + HEAD, TILE), :] = code.astype(jnp.bfloat16)


def column_on_ring(place_ref, count, width):
    return lambda n: pl.multiple_of(lax.rem(place_ref[3] + n, count) * width, width)


def far_start(place_ref, *refs):
    *ring_refs, shares_ref, other_ref, far_ref, weight = refs
    width = far_ref.shape[1]
    join_shares(place_ref, shares_ref, other_ref, 1, weight)
    column_of = column_on_ring(place_ref, weight.shape[1] // width, width)
    ring_product(far_ref, in_places(*ring_refs), weight, column_of)


def far_finish(place_ref, far_ref, middle_up_ref, middle_down_ref, shares_ref, other_ref, up_ref, down_ref, weight):
    half, width = middle_up_ref.shape
    count = weight.shape[1] // width
    join_shares(place_ref, shares_ref, other_ref, 1, weight)
    column = column_on_ring(place_ref, count, width)(count // 2)
    for side, (features_ref, coded_ref) in enumerate(((middle_up_ref, up_ref), (middle_down_ref, down_ref))):

        def tile_step(t, carry):
            row = pl.multiple_of(t * TILE, TILE)
            term = lax.dot_general(
                features_ref[pl.ds(row, TILE), :],
                weight[:, pl.ds(column, width)],
                (((1,), (1,)), ((), ())),
                preferred_element_type=jnp.float32,
            )
            encode_tile(far_ref[pl.ds(pl.multiple_of(side * half + row, TILE), TILE), :] + term, coded_ref, t)
            return carry

        lax.fori_loop(0, half // TILE, tile_step, 0)


def near_products(place_ref, *refs):
    *ring_refs, shares_ref, other_ref, next_ref, last_ref, weight = refs
    width = next_ref.shape[1]
    column_of = column_on_ring(place_ref, weight.shape[1] // width, width)
    for j, target in ((0, next_ref), (2, last_ref)):
        join_shares(place_ref, shares_ref, other_ref, j, weight)
        ring_product(target, in_places(*ring_refs), weight, column_of)


def keep_product(place_ref, *refs):
    *ring_refs, weight_ref, kept_ref = refs
    width = kept_ref.shape[1]
    count = ring_refs[0].shape[0] + 3
    along_x = weight_ref.shape[1] // (count * width)

    def column_of(n):
        block = lax.rem(place_ref[3] + n, count) * along_x + place_ref[0]
        return pl.multiple_of(block * width, width)

    ring_product(kept_ref, in_places(*ring_refs), weight_ref, column_of)


def send_near(next_ref, last_ref, up_ref, down_ref, next_coded_ref, last_coded_ref):
    tokens, width = next_ref.shape
    tiles = tokens // TILE
    half = tiles // 2
    everything = pl.ds(0, width)

    for t in range(tiles):
        rows = pl.ds(t * TILE, TILE)
        start = t % half * (TILE + HEAD)
        after, before = next_ref[rows, :], last_ref[rows, :]
        if t < half:
            after = after + decoded(up_ref, start, pl.ds(0, TILE), everything)
        else:
            before = before + decoded(down_ref, start, pl.ds(0, TILE), everything)
        encode_tile(after, next_coded_ref, t)
        encode_tile(before, last_coded_ref, t)


def decoded(coded_ref, start, rows, lanes):
    largest = coded_ref[pl.ds(start, HEAD), lanes].astype(jnp.float32)[0:1]
    code = coded_ref[pl.ds(start + HEAD + rows.start, rows.size), lanes].astype(jnp.float32)
    size = jnp.exp2(jnp.log2(jnp.maximum(jnp.abs(code), LEAST)) * 0.125)
    value = jnp.where(code < 0, -size, size) * (largest * (1.0 / SPAN))
    return jnp.where(code == 0, 0.0, value)


def local_call(kernel, outs, scratch, operands, cost):
    whole = pl.BlockSpec(memory_space=pltpu.VMEM)
    return pl.pallas_call(
        kernel,
        out_shape=outs,
        in_specs=[whole if o.ndim > 1 else pl.BlockSpec(memory_space=pltpu.SMEM) for o in operands],
        out_specs=[whole] * len(outs),
        scratch_shapes=scratch,
        compiler_params=pltpu.CompilerParams(vmem_limit_bytes=VMEM_LIMIT),
        cost_estimate=pl.CostEstimate(flops=cost, bytes_accessed=cost // 64, transcendentals=0),
    )(*operands)


def floats(*shape):
    return jax.ShapeDtypeStruct(shape, jnp.float32)


def shift(block, axis, distance, size):
    return lax.ppermute(block, axis, [(i, (i + distance) % size) for i in range(size)])


def from_behind(block, axis, distance, size):
    return lax.ppermute(
        block, axis, [(i - distance, i) for i in range(size) if 0 <= i - distance < size]
    )


def shards(
    sizes, query_in, key_in, value_in, short_taps, modal_poles, modal_residues, out_weight, grad_out
):
    ctx_count, z_count, x_count = sizes
    tokens, width = query_in.shape
    modes = modal_poles.shape[0]
    slab = floats(tokens, width)
    rounded = jax.ShapeDtypeStruct((tokens, width), jnp.bfloat16)
    per_part = floats(modes, PARTS, width)
    state = floats(modes, width)
    slab_scratch = pltpu.VMEM((tokens, width), jnp.float32)
    natural_scratch = pltpu.VMEM((width // LANES, tokens, LANES), jnp.float32)
    part_scratch = pltpu.VMEM((modes, PARTS, width), jnp.float32)
    together = lax.optimization_barrier
    decay_1 = power(modal_poles, tokens)
    decay_2 = decay_1 * decay_1

    ctx = lax.axis_index("ctx")
    place = jnp.stack([lax.axis_index("x"), ctx // 2, ctx % 2, lax.axis_index("z")])

    right_1 = shift(grad_out, "z", 1, z_count)
    left_1 = shift(grad_out, "z", -1, z_count)
    tails = jnp.stack([a[tokens - 16 :] for a in (query_in, key_in, value_in)])
    prior = from_behind(tails, "ctx", 1, ctx_count)
    place, prior = together((place, prior))
    message = jax.ShapeDtypeStruct((width // 4 * 3, z_count * width), jnp.bfloat16)
    up, down = pl.pallas_call(
        pick_shares,
        out_shape=[message] * 2,
        in_specs=[pl.BlockSpec(memory_space=pltpu.SMEM), pl.BlockSpec(memory_space=pltpu.HBM)],
        out_specs=[pl.BlockSpec(memory_space=pltpu.VMEM)] * 2,
        scratch_shapes=[pltpu.SemaphoreType.DMA((2, 2, z_count))],
        compiler_params=pltpu.CompilerParams(vmem_limit_bytes=VMEM_LIMIT),
    )(place, out_weight)
    up = shift(up, "x", 1, x_count)
    down = shift(down, "x", -1, x_count)
    q_short, k_short, v_short, ends, own_end = local_call(
        short_filters,
        [slab, slab, slab, per_part, state],
        [pltpu.VMEM((width // LANES, tokens + RIM, LANES), jnp.float32)],
        (query_in, key_in, value_in, prior, short_taps, modal_poles),
        tokens * width * 80,
    )
    right_2 = shift(right_1, "z", 1, z_count)
    left_2 = shift(left_1, "z", -1, z_count)
    one = from_behind(own_end, "ctx", 1, ctx_count)
    right_2, left_2, one, up, down = together((right_2, left_2, one, up, down))

    right_3 = shift(right_2, "z", 1, z_count)
    left_3 = shift(left_2, "z", -1, z_count)
    rows = width // 2
    far_up = shift(up[rows:], "x", 1, x_count)
    far_down = shift(down[rows:], "x", -1, x_count)
    anywhere = pl.BlockSpec(memory_space=pl.ANY)
    blocks = (right_2, right_1, grad_out, left_1, left_2)
    early = pl.pallas_call(
        collect,
        out_shape=jax.ShapeDtypeStruct((len(blocks), tokens, width), jnp.bfloat16),
        in_specs=[anywhere] * len(blocks),
        out_specs=pl.BlockSpec(memory_space=pltpu.VMEM),
        scratch_shapes=[pltpu.SemaphoreType.DMA((len(blocks),))],
        compiler_params=pltpu.CompilerParams(vmem_limit_bytes=VMEM_LIMIT),
    )(*blocks)
    right_3, left_3, far_up, far_down, early = together((right_3, left_3, far_up, far_down, early))

    middle_up = shift(right_3[: tokens // 2], "z", 1, z_count)
    middle_down = shift(left_3[tokens // 2 :], "z", -1, z_count)
    shares = jnp.stack([down[:rows], jnp.concatenate([far_up, far_down]), up[:rows]])
    other = lax.ppermute(shares, "ctx", [(i, i ^ 1) for i in range(ctx_count)])

    weight_scratch = pltpu.VMEM((width, z_count * width), jnp.bfloat16)
    product_cost = tokens * width * z_count * width * 2
    half_code = jax.ShapeDtypeStruct((tokens // TILE // 2 * (TILE + HEAD), width), jnp.bfloat16)
    code = jax.ShapeDtypeStruct((tokens // TILE * (TILE + HEAD), width), jnp.bfloat16)
    (far,) = local_call(
        far_start,
        [slab],
        [weight_scratch],
        (place, early, left_3, right_3, shares, other),
        product_cost,
    )
    middle_up, middle_down, far = together((middle_up, middle_down, far))
    on_ring = (early, left_3, right_3, middle_up, middle_down)
    up, down = local_call(
        far_finish,
        [half_code, half_code],
        [weight_scratch],
        (place, far, middle_up, middle_down, shares, other),
        product_cost // z_count,
    )
    up = shift(up, "x", 1, x_count)
    down = shift(down, "x", -1, x_count)
    after, last = local_call(
        near_products,
        [slab, slab],
        [weight_scratch],
        (place, *on_ring, shares, other),
        2 * product_cost,
    )
    pair = own_end + decay_1 * one
    two = from_behind(pair, "ctx", 2, ctx_count)
    up, down, after, last, two = together((up, down, after, last, two))
    after, last = local_call(
        send_near, [code, code], [], (after, last, up, down), tokens * width * 64
    )
    after = shift(after, "x", 1, x_count)
    last = shift(last, "x", -1, x_count)
    four = from_behind(pair + decay_2 * two, "ctx", 4, ctx_count)
    before = one + decay_1 * two + decay_2 * decay_1 * four
    first_kv = jnp.stack([k_short[: RIM * PARTS : PARTS], v_short[: RIM * PARTS : PARTS]])
    next_kv = from_behind(first_kv, "ctx", -1, ctx_count)
    (kept,) = local_call(
        keep_product, [slab], [], (place, *on_ring, out_weight), product_cost
    )
    long_out, gated = local_call(
        long_forward,
        [slab, rounded],
        [part_scratch, natural_scratch],
        (q_short, k_short, v_short, ends, before, modal_poles, modal_residues),
        tokens * width * 70,
    )
    after, last, gated, kept, next_kv = together((after, last, gated, kept, next_kv))
    mixed_steps, starts, own_start, rim = local_call(
        back_states,
        [slab, per_part, state, floats(modes + 2 * RIM, width)],
        [part_scratch, natural_scratch],
        (kept, after, last, q_short, long_out, modal_poles),
        tokens * width * 40,
    )

    near = from_behind(jnp.concatenate([rim, own_start]), "ctx", -1, ctx_count)
    (local,) = local_call(
        back_local, [slab], [], (mixed_steps, q_short, modal_poles, modal_residues), tokens * width * 64
    )
    two = from_behind(own_start, "ctx", -2, ctx_count)
    near, two, local = together((near, two, local))
    rim_size = modes + 2 * RIM
    near_rim = near[:rim_size]
    triple = own_start + decay_1 * near[rim_size:] + decay_2 * two
    triple_2 = from_behind(triple, "ctx", -2, ctx_count)
    triple_5 = from_behind(triple, "ctx", -5, ctx_count)
    (grad_query,) = local_call(
        back_query,
        [rounded],
        [natural_scratch],
        (mixed_steps, long_out, near_rim, short_taps),
        tokens * width * 20,
    )
    triple_2, triple_5, grad_query = together((triple_2, triple_5, grad_query))
    beyond = triple_2 + decay_2 * decay_1 * triple_5
    grad_key, grad_value = local_call(
        back_filters,
        [rounded, rounded],
        [part_scratch, slab_scratch, natural_scratch, pltpu.VMEM((2, RIM, width), jnp.float32)],
        (
            local, k_short, v_short, starts, near_rim, beyond, next_kv,
            short_taps, modal_poles, modal_residues,
        ),
        tokens * width * 80,
    )
    return gated, grad_query, grad_key, grad_value


def solution(mesh):
    ctx_count, tp_count = mesh.shape["ctx"], mesh.shape["tp"]
    sizes = (ctx_count, tp_count // X_COUNT, X_COUNT)
    grid = Mesh(mesh.devices.reshape(sizes), ("ctx", "z", "x"))
    tp = ("z", "x")
    placed = (
        P("ctx", tp),
        P("ctx", tp),
        P("ctx", tp),
        P(None, None, tp),
        P(None, tp),
        P(None, tp),
        P(tp, None),
        P("ctx", tp),
    )
    return jax.shard_map(
        functools.partial(shards, sizes),
        mesh=grid,
        in_specs=placed,
        out_specs=(P("ctx", tp),) * 4,
        check_vma=False,
    )
```

profile of v0, /device:TPU:1, one launch (start us, length us, event | category | flops | bytes accessed | tf_op | source)
XLA Modules:
  0.0 119.7 jit_solution(14640796668778884775)
XLA Ops:
  0.6 2.5 %collective-permute-start.1 = (bf16[1024,256]{1,0:T(8,128)(2,1)}, bf16[1024,256]{1,0:T(8,128)(2,1)S(1)}, u32[]{:S(2)}, u32[]{:S(2)}) collective-permute-start(bf16[1024,256]{1,0:T(8,128)(2,1)} %refs_2_.1), channel_id=1, source_target_pairs={{0,4},{4,8},{8,12},{12,16},{16,20},{20,24},{24,28},{28,0},{1,5},{5... | collective-permute-start | bytes 1572872 | tf_op jit(solution)/shard_map/ppermute | solution.py:453
  3.2 4.0 %collective-permute-start.3 = (bf16[1024,256]{1,0:T(8,128)(2,1)}, bf16[1024,256]{1,0:T(8,128)(2,1)S(1)}, u32[]{:S(2)}, u32[]{:S(2)}) collective-permute-start(bf16[1024,256]{1,0:T(8,128)(2,1)} %refs_2_.1), channel_id=1, source_target_pairs={{0,28},{4,0},{8,4},{12,8},{16,12},{20,16},{24,20},{28,24},{1,29},{... | collective-permute-start | bytes 1572872 | tf_op jit(solution)/shard_map/ppermute | solution.py:453
  8.6 4.0 %collective-permute-start = (bf16[3,16,256]{2,1,0:T(8,128)(2,1)S(1)}, bf16[3,16,256]{2,1,0:T(8,128)(2,1)S(1)}, u32[]{:S(2)}, u32[]{:S(2)}) collective-permute-start(bf16[3,16,256]{2,1,0:T(8,128)(2,1)S(1)} %pad_maximum_fusion.2), channel_id=1, source_target_pairs={{0,32},{32,64},{64,96},{96,128},{128,160},{160,192},{192,224},{1,3... | collective-permute-start | bytes 73736 | tf_op jit(solution)/shard_map/ppermute | solution.py:457
  19.8 2.7 %collective-permute-start.4 = (bf16[1024,256]{1,0:T(8,128)(2,1)S(1)}, bf16[1024,256]{1,0:T(8,128)(2,1)S(1)}, u32[]{:S(2)}, u32[]{:S(2)}) collective-permute-start(bf16[1024,256]{1,0:T(8,128)(2,1)S(1)} %collective-permute-done.3.refs_3_), channel_id=1, source_target_pairs={{0,28},{4,0},{8,4},{12,8},{16,12},{20,16},{24,20},{28,24},{1,29},{... | collective-permute-start | bytes 1572872 | tf_op jit(solution)/shard_map/ppermute | solution.py:453
  22.5 4.7 %shard_map.111 = (f32[1024,256]{1,0:T(8,128)S(1)}, f32[1024,256]{1,0:T(8,128)S(1)}, f32[1024,256]{1,0:T(8,128)S(1)}, f32[16,8,256]{2,1,0:T(8,128)S(1)}, f32[16,256]{1,0:T(8,128)S(1)}) custom-call(bf16[1024,256]{1,0:T(8,128)(2,1)S(1)} %copy-done.12, bf16[1024,256]{1,0:T(8,128)(2,1)S(1)} %copy-done.13, bf16[1024,256]{1,0:T(8,128)(2,1)S(1)} %copy-done.14, ...), custom_call_target="tpu_custom_call" | custom-call | flops 20971520 | bytes 327680 | tf_op jit(solution)/shard_map/pallas_call | solution.py:437
  28.2 5.3 %collective-permute-start.5 = (f32[16,256]{1,0:T(8,128)S(1)}, f32[16,256]{1,0:T(8,128)S(1)}, u32[]{:S(2)}, u32[]{:S(2)}) collective-permute-start(f32[16,256]{1,0:T(8,128)S(1)} %get-tuple-element.58), channel_id=1, source_target_pairs={{0,32},{32,64},{64,96},{96,128},{128,160},{160,192},{192,224},{1,3... | collective-permute-start | bytes 49160 | tf_op jit(solution)/shard_map/ppermute | solution.py:457
  36.6 2.7 %collective-permute-start.9 = (bf16[1024,256]{1,0:T(8,128)(2,1)S(1)}, bf16[1024,256]{1,0:T(8,128)(2,1)S(1)}, u32[]{:S(2)}, u32[]{:S(2)}) collective-permute-start(bf16[1024,256]{1,0:T(8,128)(2,1)S(1)} %collective-permute-done.4.refs_4_), channel_id=1, source_target_pairs={{0,28},{4,0},{8,4},{12,8},{16,12},{20,16},{24,20},{28,24},{1,29},{... | collective-permute-start | bytes 1572872 | tf_op jit(solution)/shard_map/ppermute | solution.py:453
  44.6 3.7 %collective-permute-done.10 = bf16[64,2048]{1,0:T(8,128)(2,1)S(1)} collective-permute-done((bf16[64,2048]{1,0:T(8,128)(2,1)S(1)}, bf16[64,2048]{1,0:T(8,128)(2,1)S(1)}, u32[]{:S(2)}, u32[]{:S(2)}) %collective-permute-start.10) | collective-permute-done | bytes 262176 | tf_op jit(solution)/shard_map/ppermute | solution.py:453
  48.3 3.3 %collective-permute-done.8.refs_2_ = bf16[1024,256]{1,0:T(8,128)(2,1)S(1)} collective-permute-done((bf16[1024,256]{1,0:T(8,128)(2,1)S(1)}, bf16[1024,256]{1,0:T(8,128)(2,1)S(1)}, u32[]{:S(2)}, u32[]{:S(2)}) %collective-permute-start.8) | collective-permute-done | bytes 524320 | tf_op jit(solution)/shard_map/ppermute | solution.py:453
  55.0 2.7 %collective-permute-start.13 = (bf16[512,256]{1,0:T(8,128)(2,1)}, bf16[512,256]{1,0:T(8,128)(2,1)}, u32[]{:S(2)}, u32[]{:S(2)}) collective-permute-start(bf16[512,256]{1,0:T(8,128)(2,1)} %slice.45), channel_id=1, source_target_pairs={{0,28},{4,0},{8,4},{12,8},{16,12},{20,16},{24,20},{28,24},{1,29},{... | collective-permute-start | bytes 786440 | tf_op jit(solution)/shard_map/ppermute | solution.py:453
  60.4 3.1 %shard_map.114.far_ref = f32[1024,256]{1,0:T(8,128)S(1)} custom-call(s32[4]{0:T(128)S(1)} %pad_add_fusion.place_ref, bf16[5,1024,256]{2,1,0:T(8,128)(2,1)S(1)} %shard_map.113.refs_0_, bf16[1024,256]{1,0:T(8,128)(2,1)S(1)} %copy-done.9, bf16[1024,256]{1,0:T(8,128)(2,1)S(1)} %collective-permute-done.8.refs_2_, ...), custom_call_target="tpu_custom_call" | custom-call | flops 1073741824 | bytes 16777216 | tf_op jit(solution)/shard_map/pallas_call | solution.py:437
  64.0 3.4 %shard_map.115 = (bf16[544,256]{1,0:T(8,128)(2,1)S(1)}, bf16[544,256]{1,0:T(8,128)(2,1)S(1)}) custom-call(s32[4]{0:T(128)S(1)} %pad_add_fusion.place_ref, f32[1024,256]{1,0:T(8,128)S(1)} %shard_map.114.far_ref, bf16[512,256]{1,0:T(8,128)(2,1)S(1)} %collective-permute-done.12.middle_up_ref.refs_3_, ...), custom_call_target="tpu_custom_call" | custom-call | flops 134217728 | bytes 2097152 | tf_op jit(solution)/shard_map/pallas_call | solution.py:437
  70.1 3.1 %collective-permute-start.17 = (f32[16,256]{1,0:T(8,128)S(1)}, f32[16,256]{1,0:T(8,128)S(1)}, u32[]{:S(2)}, u32[]{:S(2)}) collective-permute-start(f32[16,256]{1,0:T(8,128)S(1)} %multiply_add_fusion.2), channel_id=1, source_target_pairs={{0,64},{32,96},{64,128},{96,160},{128,192},{160,224},{1,65},{33,97... | collective-permute-start | bytes 49160 | tf_op jit(solution)/shard_map/ppermute | solution.py:457
  73.2 4.6 %shard_map.116 = (f32[1024,256]{1,0:T(8,128)S(1)}, f32[1024,256]{1,0:T(8,128)S(1)}) custom-call(s32[4]{0:T(128)S(1)} %pad_add_fusion.place_ref, bf16[5,1024,256]{2,1,0:T(8,128)(2,1)S(1)} %shard_map.113.refs_0_, bf16[1024,256]{1,0:T(8,128)(2,1)S(1)} %copy-done.10, bf16[1024,256]{1,0:T(8,128)(2,1)S(1)} %collective-permute-done.8.refs_2_, ...), custom_call_target="tpu_custom_call" | custom-call | flops 2147483648 | bytes 33554432 | tf_op jit(solution)/shard_map/pallas_call | solution.py:437
  79.1 2.7 %collective-permute-start.19 = (bf16[1088,256]{1,0:T(8,128)(2,1)S(1)}, bf16[1088,256]{1,0:T(8,128)(2,1)S(1)}, u32[]{:S(2)}, u32[]{:S(2)}) collective-permute-start(bf16[1088,256]{1,0:T(8,128)(2,1)S(1)} %get-tuple-element.83), channel_id=1, source_target_pairs={{0,3},{1,0},{2,1},{3,2},{4,7},{5,4},{6,5},{7,6},{8,11},{9,8},{10,9... | collective-permute-start | bytes 1671176 | tf_op jit(solution)/shard_map/ppermute | solution.py:453
  81.8 4.1 %collective-permute-start.21 = (f32[2,8,256]{2,1,0:T(8,128)S(1)}, f32[2,8,256]{2,1,0:T(8,128)S(1)}, u32[]{:S(2)}, u32[]{:S(2)}) collective-permute-start(f32[2,8,256]{2,1,0:T(8,128)S(1)} %pad_maximum_fusion.3), channel_id=1, source_target_pairs={{32,0},{64,32},{96,64},{128,96},{160,128},{192,160},{224,192},{33,... | collective-permute-start | bytes 49160 | tf_op jit(solution)/shard_map/ppermute | solution.py:457
  86.0 2.9 %collective-permute-start.20 = (f32[16,256]{1,0:T(8,128)S(1)}, f32[16,256]{1,0:T(8,128)S(1)}, u32[]{:S(2)}, u32[]{:S(2)}) collective-permute-start(f32[16,256]{1,0:T(8,128)S(1)} %fusion), channel_id=1, source_target_pairs={{0,128},{32,160},{64,192},{96,224},{1,129},{33,161},{65,193},{97,2... | collective-permute-start | bytes 49160 | tf_op jit(solution)/shard_map/ppermute | solution.py:457
  88.9 2.2 %shard_map.119.kept_ref = f32[1024,256]{1,0:T(8,128)S(1)} custom-call(s32[4]{0:T(128)S(1)} %pad_add_fusion.place_ref, bf16[5,1024,256]{2,1,0:T(8,128)(2,1)S(1)} %shard_map.113.refs_0_, bf16[1024,256]{1,0:T(8,128)(2,1)S(1)} %copy-done.10, bf16[1024,256]{1,0:T(8,128)(2,1)S(1)} %collective-permute-done.8.refs_2_, ...), custom_call_target="tpu_custom_call" | custom-call | flops 1073741824 | bytes 16777216 | tf_op jit(solution)/shard_map/pallas_call | solution.py:437
  91.2 3.8 %shard_map.118 = (f32[1024,256]{1,0:T(8,128)S(1)}, bf16[1024,256]{1,0:T(8,128)(2,1)}) custom-call(f32[1024,256]{1,0:T(8,128)S(1)} %copy-done.3, f32[1024,256]{1,0:T(8,128)S(1)} %copy-done.5, f32[1024,256]{1,0:T(8,128)S(1)} %copy-done.7, f32[16,8,256]{2,1,0:T(8,128)S(1)} %copy-done.23, f32[16,256]{1,0:T(8,128)S(1)} %multiply_add_fusion.1.before_ref, ...), custom_call_target="tpu_custom_call" | custom-call | flops 18350080 | bytes 286720 | tf_op jit(solution)/shard_map/pallas_call | solution.py:437
  95.1 3.7 %shard_map.120 = (f32[1024,256]{1,0:T(8,128)S(1)}, f32[16,8,256]{2,1,0:T(8,128)S(1)}, f32[16,256]{1,0:T(8,128)S(1)}, f32[32,256]{1,0:T(8,128)S(1)}) custom-call(f32[1024,256]{1,0:T(8,128)S(1)} %shard_map.119.kept_ref, bf16[1088,256]{1,0:T(8,128)(2,1)S(1)} %collective-permute-done.18.one_ref, bf16[1088,256]{1,0:T(8,128)(2,1)S(1)} %collective-permute-done.19.three_ref, ...), custom_call_target="tpu_custom_call" | custom-call | flops 10485760 | bytes 163840 | tf_op jit(solution)/shard_map/pallas_call | solution.py:437
  102.3 2.6 %shard_map.121.local_ref = f32[1024,256]{1,0:T(8,128)S(1)} custom-call(f32[1024,256]{1,0:T(8,128)S(1)} %get-tuple-element.97.mixed_ref, f32[1024,256]{1,0:T(8,128)S(1)} %copy-done.3, f32[16,256]{1,0:T(8,128)S(1)} %copy-done.11, f32[16,256]{1,0:T(8,128)S(1)} %copy-done.21), custom_call_target="tpu_custom_call" | custom-call | flops 16777216 | bytes 262144 | tf_op jit(solution)/shard_map/pallas_call | solution.py:437
  108.2 2.2 %shard_map.122 = bf16[1024,256]{1,0:T(8,128)(2,1)} custom-call(f32[1024,256]{1,0:T(8,128)S(1)} %get-tuple-element.97.mixed_ref, f32[1024,256]{1,0:T(8,128)S(1)} %get-tuple-element.94.long_ref, f32[32,256]{1,0:T(8,128)S(1)} %slice.51.next_ref, f32[3,7,256]{2,1,0:T(8,128)S(1)} %copy-done.20), custom_call_target="tpu_custom_call" | custom-call | flops 5242880 | bytes 81920 | tf_op jit(solution)/shard_map/pallas_call | solution.py:437
  110.4 4.0 %collective-permute-done.25 = f32[16,256]{1,0:T(8,128)S(1)} collective-permute-done((f32[16,256]{1,0:T(8,128)S(1)}, f32[16,256]{1,0:T(8,128)S(1)}, u32[]{:S(2)}, u32[]{:S(2)}) %collective-permute-start.25) | collective-permute-done | bytes 16416 | tf_op jit(solution)/shard_map/ppermute | solution.py:457
  114.5 5.2 %shard_map.123 = (bf16[1024,256]{1,0:T(8,128)(2,1)}, bf16[1024,256]{1,0:T(8,128)(2,1)}) custom-call(f32[1024,256]{1,0:T(8,128)S(1)} %shard_map.121.local_ref, f32[1024,256]{1,0:T(8,128)S(1)} %copy-done.5, f32[1024,256]{1,0:T(8,128)S(1)} %copy-done.7, f32[16,8,256]{2,1,0:T(8,128)S(1)} %get-tuple-element.102.starts_ref, f32[32,256]{1,0:T(8,128)S(1)} %slice.51.next_ref, ...), custom_call_target="tpu_custom_call" | custom-call | flops 20971520 | bytes 327680 | tf_op jit(solution)/shard_map/pallas_call | solution.py:437
  (111 shorter events, 35.2 us)
Async XLA Ops:
  0.6 19.1 %collective-permute-start.1 = (bf16[1024,256]{1,0:T(8,128)(2,1)}, bf16[1024,256]{1,0:T(8,128)(2,1)S(1)}, u32[]{:S(2)}, u32[]{:S(2)}) collective-permute-start(bf16[1024,256]{1,0:T(8,128)(2,1)} %refs_2_.1), channel_id=1, source_target_pairs={{0,4},{4,8},{8,12},{12,16},{16,20},{20,24},{24,28},{28,0},{1,5},{5... | collective-permute-start | bytes 1572872 | tf_op jit(solution)/shard_map/ppermute | solution.py:453
  3.2 16.6 %collective-permute-start.3 = (bf16[1024,256]{1,0:T(8,128)(2,1)}, bf16[1024,256]{1,0:T(8,128)(2,1)S(1)}, u32[]{:S(2)}, u32[]{:S(2)}) collective-permute-start(bf16[1024,256]{1,0:T(8,128)(2,1)} %refs_2_.1), channel_id=1, source_target_pairs={{0,28},{4,0},{8,4},{12,8},{16,12},{20,16},{24,20},{28,24},{1,29},{... | collective-permute-start | bytes 1572872 | tf_op jit(solution)/shard_map/ppermute | solution.py:453
  8.6 5.0 %collective-permute-start = (bf16[3,16,256]{2,1,0:T(8,128)(2,1)S(1)}, bf16[3,16,256]{2,1,0:T(8,128)(2,1)S(1)}, u32[]{:S(2)}, u32[]{:S(2)}) collective-permute-start(bf16[3,16,256]{2,1,0:T(8,128)(2,1)S(1)} %pad_maximum_fusion.2), channel_id=1, source_target_pairs={{0,32},{32,64},{64,96},{96,128},{128,160},{160,192},{192,224},{1,3... | collective-permute-start | bytes 73736 | tf_op jit(solution)/shard_map/ppermute | solution.py:457
  17.0 19.3 %collective-permute-start.6 = (bf16[192,2048]{1,0:T(8,128)(2,1)S(1)}, bf16[192,2048]{1,0:T(8,128)(2,1)S(1)}, u32[]{:S(2)}, u32[]{:S(2)}) collective-permute-start(bf16[192,2048]{1,0:T(8,128)(2,1)S(1)} %get-tuple-element.59), channel_id=1, source_target_pairs={{0,1},{1,2},{2,3},{3,0},{4,5},{5,6},{6,7},{7,4},{8,9},{9,10},{10,1... | collective-permute-start | bytes 2359304 | tf_op jit(solution)/shard_map/ppermute | solution.py:453
  18.3 18.3 %collective-permute-start.7 = (bf16[192,2048]{1,0:T(8,128)(2,1)S(1)}, bf16[192,2048]{1,0:T(8,128)(2,1)S(1)}, u32[]{:S(2)}, u32[]{:S(2)}) collective-permute-start(bf16[192,2048]{1,0:T(8,128)(2,1)S(1)} %get-tuple-element.60), channel_id=1, source_target_pairs={{0,3},{1,0},{2,1},{3,2},{4,7},{5,4},{6,5},{7,6},{8,11},{9,8},{10,9... | collective-permute-start | bytes 2359304 | tf_op jit(solution)/shard_map/ppermute | solution.py:453
  19.8 16.8 %collective-permute-start.2 = (bf16[1024,256]{1,0:T(8,128)(2,1)S(1)}, bf16[1024,256]{1,0:T(8,128)(2,1)S(1)}, u32[]{:S(2)}, u32[]{:S(2)}) collective-permute-start(bf16[1024,256]{1,0:T(8,128)(2,1)S(1)} %collective-permute-done.1.refs_1_), channel_id=1, source_target_pairs={{0,4},{4,8},{8,12},{12,16},{16,20},{20,24},{24,28},{28,0},{1,5},{5... | collective-permute-start | bytes 1572872 | tf_op jit(solution)/shard_map/ppermute | solution.py:453
  19.8 16.8 %collective-permute-start.4 = (bf16[1024,256]{1,0:T(8,128)(2,1)S(1)}, bf16[1024,256]{1,0:T(8,128)(2,1)S(1)}, u32[]{:S(2)}, u32[]{:S(2)}) collective-permute-start(bf16[1024,256]{1,0:T(8,128)(2,1)S(1)} %collective-permute-done.3.refs_3_), channel_id=1, source_target_pairs={{0,28},{4,0},{8,4},{12,8},{16,12},{20,16},{24,20},{28,24},{1,29},{... | collective-permute-start | bytes 1572872 | tf_op jit(solution)/shard_map/ppermute | solution.py:453
  28.2 6.2 %collective-permute-start.5 = (f32[16,256]{1,0:T(8,128)S(1)}, f32[16,256]{1,0:T(8,128)S(1)}, u32[]{:S(2)}, u32[]{:S(2)}) collective-permute-start(f32[16,256]{1,0:T(8,128)S(1)} %get-tuple-element.58), channel_id=1, source_target_pairs={{0,32},{32,64},{64,96},{96,128},{128,160},{160,192},{192,224},{1,3... | collective-permute-start | bytes 49160 | tf_op jit(solution)/shard_map/ppermute | solution.py:457
  36.6 15.0 %collective-permute-start.8 = (bf16[1024,256]{1,0:T(8,128)(2,1)S(1)}, bf16[1024,256]{1,0:T(8,128)(2,1)S(1)}, u32[]{:S(2)}, u32[]{:S(2)}) collective-permute-start(bf16[1024,256]{1,0:T(8,128)(2,1)S(1)} %collective-permute-done.2.refs_0_), channel_id=1, source_target_pairs={{0,4},{4,8},{8,12},{12,16},{16,20},{20,24},{24,28},{28,0},{1,5},{5... | collective-permute-start | bytes 1572872 | tf_op jit(solution)/shard_map/ppermute | solution.py:453
  36.6 15.0 %collective-permute-start.9 = (bf16[1024,256]{1,0:T(8,128)(2,1)S(1)}, bf16[1024,256]{1,0:T(8,128)(2,1)S(1)}, u32[]{:S(2)}, u32[]{:S(2)}) collective-permute-start(bf16[1024,256]{1,0:T(8,128)(2,1)S(1)} %collective-permute-done.4.refs_4_), channel_id=1, source_target_pairs={{0,28},{4,0},{8,4},{12,8},{16,12},{20,16},{24,20},{28,24},{1,29},{... | collective-permute-start | bytes 1572872 | tf_op jit(solution)/shard_map/ppermute | solution.py:453
  39.4 8.9 %collective-permute-start.10 = (bf16[64,2048]{1,0:T(8,128)(2,1)S(1)}, bf16[64,2048]{1,0:T(8,128)(2,1)S(1)}, u32[]{:S(2)}, u32[]{:S(2)}) collective-permute-start(bf16[64,2048]{1,0:T(8,128)(2,1)S(1)} %slice.42), channel_id=1, source_target_pairs={{0,1},{1,2},{2,3},{3,0},{4,5},{5,6},{6,7},{7,4},{8,9},{9,10},{10,1... | collective-permute-start | bytes 786440 | tf_op jit(solution)/shard_map/ppermute | solution.py:453
  40.7 7.6 %collective-permute-start.11 = (bf16[64,2048]{1,0:T(8,128)(2,1)S(1)}, bf16[64,2048]{1,0:T(8,128)(2,1)S(1)}, u32[]{:S(2)}, u32[]{:S(2)}) collective-permute-start(bf16[64,2048]{1,0:T(8,128)(2,1)S(1)} %slice.43), channel_id=1, source_target_pairs={{0,3},{1,0},{2,1},{3,2},{4,7},{5,4},{6,5},{7,6},{8,11},{9,8},{10,9... | collective-permute-start | bytes 786440 | tf_op jit(solution)/shard_map/ppermute | solution.py:453
  53.0 6.4 %collective-permute-start.14 = (bf16[3,128,2048]{2,1,0:T(8,128)(2,1)}, bf16[3,128,2048]{2,1,0:T(8,128)(2,1)}, u32[]{:S(2)}, u32[]{:S(2)}) collective-permute-start(bf16[3,128,2048]{2,1,0:T(8,128)(2,1)} %pad_maximum_fusion.refs_3_.shares_ref.refs_5_), channel_id=1, source_target_pairs={{0,32},{32,0},{64,96},{96,64},{128,160},{160,128},{192,224},{224,1... | collective-permute-start | bytes 4718600 | tf_op jit(solution)/shard_map/ppermute | solution.py:530
  54.3 9.4 %collective-permute-start.12 = (bf16[512,256]{1,0:T(8,128)(2,1)}, bf16[512,256]{1,0:T(8,128)(2,1)S(1)}, u32[]{:S(2)}, u32[]{:S(2)}) collective-permute-start(bf16[512,256]{1,0:T(8,128)(2,1)} %slice.44), channel_id=1, source_target_pairs={{0,4},{4,8},{8,12},{12,16},{16,20},{20,24},{24,28},{28,0},{1,5},{5... | collective-permute-start | bytes 786440 | tf_op jit(solution)/shard_map/ppermute | solution.py:453
  55.0 9.0 %collective-permute-start.13 = (bf16[512,256]{1,0:T(8,128)(2,1)}, bf16[512,256]{1,0:T(8,128)(2,1)}, u32[]{:S(2)}, u32[]{:S(2)}) collective-permute-start(bf16[512,256]{1,0:T(8,128)(2,1)} %slice.45), channel_id=1, source_target_pairs={{0,28},{4,0},{8,4},{12,8},{16,12},{20,16},{24,20},{28,24},{1,29},{... | collective-permute-start | bytes 786440 | tf_op jit(solution)/shard_map/ppermute | solution.py:453
  67.4 10.5 %collective-permute-start.15 = (bf16[544,256]{1,0:T(8,128)(2,1)S(1)}, bf16[544,256]{1,0:T(8,128)(2,1)S(1)}, u32[]{:S(2)}, u32[]{:S(2)}) collective-permute-start(bf16[544,256]{1,0:T(8,128)(2,1)S(1)} %get-tuple-element.73), channel_id=1, source_target_pairs={{0,1},{1,2},{2,3},{3,0},{4,5},{5,6},{6,7},{7,4},{8,9},{9,10},{10,1... | collective-permute-start | bytes 835592 | tf_op jit(solution)/shard_map/ppermute | solution.py:453
  68.4 9.4 %collective-permute-start.16 = (bf16[544,256]{1,0:T(8,128)(2,1)S(1)}, bf16[544,256]{1,0:T(8,128)(2,1)S(1)}, u32[]{:S(2)}, u32[]{:S(2)}) collective-permute-start(bf16[544,256]{1,0:T(8,128)(2,1)S(1)} %get-tuple-element.74), channel_id=1, source_target_pairs={{0,3},{1,0},{2,1},{3,2},{4,7},{5,4},{6,5},{7,6},{8,11},{9,8},{10,9... | collective-permute-start | bytes 835592 | tf_op jit(solution)/shard_map/ppermute | solution.py:453
  70.1 7.7 %collective-permute-start.17 = (f32[16,256]{1,0:T(8,128)S(1)}, f32[16,256]{1,0:T(8,128)S(1)}, u32[]{:S(2)}, u32[]{:S(2)}) collective-permute-start(f32[16,256]{1,0:T(8,128)S(1)} %multiply_add_fusion.2), channel_id=1, source_target_pairs={{0,64},{32,96},{64,128},{96,160},{128,192},{160,224},{1,65},{33,97... | collective-permute-start | bytes 49160 | tf_op jit(solution)/shard_map/ppermute | solution.py:457
  79.0 16.1 %collective-permute-start.18 = (bf16[1088,256]{1,0:T(8,128)(2,1)S(1)}, bf16[1088,256]{1,0:T(8,128)(2,1)S(1)}, u32[]{:S(2)}, u32[]{:S(2)}) collective-permute-start(bf16[1088,256]{1,0:T(8,128)(2,1)S(1)} %get-tuple-element.82), channel_id=1, source_target_pairs={{0,1},{1,2},{2,3},{3,0},{4,5},{5,6},{6,7},{7,4},{8,9},{9,10},{10,1... | collective-permute-start | bytes 1671176 | tf_op jit(solution)/shard_map/ppermute | solution.py:453
  79.1 16.0 %collective-permute-start.19 = (bf16[1088,256]{1,0:T(8,128)(2,1)S(1)}, bf16[1088,256]{1,0:T(8,128)(2,1)S(1)}, u32[]{:S(2)}, u32[]{:S(2)}) collective-permute-start(bf16[1088,256]{1,0:T(8,128)(2,1)S(1)} %get-tuple-element.83), channel_id=1, source_target_pairs={{0,3},{1,0},{2,1},{3,2},{4,7},{5,4},{6,5},{7,6},{8,11},{9,8},{10,9... | collective-permute-start | bytes 1671176 | tf_op jit(solution)/shard_map/ppermute | solution.py:453
  81.8 13.3 %collective-permute-start.21 = (f32[2,8,256]{2,1,0:T(8,128)S(1)}, f32[2,8,256]{2,1,0:T(8,128)S(1)}, u32[]{:S(2)}, u32[]{:S(2)}) collective-permute-start(f32[2,8,256]{2,1,0:T(8,128)S(1)} %pad_maximum_fusion.3), channel_id=1, source_target_pairs={{32,0},{64,32},{96,64},{128,96},{160,128},{192,160},{224,192},{33,... | collective-permute-start | bytes 49160 | tf_op jit(solution)/shard_map/ppermute | solution.py:457
  86.0 5.2 %collective-permute-start.20 = (f32[16,256]{1,0:T(8,128)S(1)}, f32[16,256]{1,0:T(8,128)S(1)}, u32[]{:S(2)}, u32[]{:S(2)}) collective-permute-start(f32[16,256]{1,0:T(8,128)S(1)} %fusion), channel_id=1, source_target_pairs={{0,128},{32,160},{64,192},{96,224},{1,129},{33,161},{65,193},{97,2... | collective-permute-start | bytes 49160 | tf_op jit(solution)/shard_map/ppermute | solution.py:457
  98.8 6.7 %collective-permute-start.22 = (f32[48,256]{1,0:T(8,128)S(1)}, f32[48,256]{1,0:T(8,128)S(1)}, u32[]{:S(2)}, u32[]{:S(2)}) collective-permute-start(f32[48,256]{1,0:T(8,128)S(1)} %pad_maximum_fusion.1), channel_id=1, source_target_pairs={{32,0},{64,32},{96,64},{128,96},{160,128},{192,160},{224,192},{33,... | collective-permute-start | bytes 147464 | tf_op jit(solution)/shard_map/ppermute | solution.py:457
  106.8 7.6 %collective-permute-start.25 = (f32[16,256]{1,0:T(8,128)S(1)}, f32[16,256]{1,0:T(8,128)S(1)}, u32[]{:S(2)}, u32[]{:S(2)}) collective-permute-start(f32[16,256]{1,0:T(8,128)S(1)} %fusion.1), channel_id=1, source_target_pairs={{160,0},{192,32},{224,64},{161,1},{193,33},{225,65},{162,2},{194,3... | collective-permute-start | bytes 49160 | tf_op jit(solution)/shard_map/ppermute | solution.py:457
  (26 other events, 208.0 us)
where the time goes:
time: 121 us; the launch traced here: 120 us
  starting transfers between devices  51.8 us (43%)
  Pallas kernels  38.2 us (32%)
  waiting for transfers between devices  15.9 us (13%)
  local copies, waits for them, and re-layouts  11 us (9%)
  other arithmetic  1.56 us (1%)
    pallas_call x11, Pallas kernels, local_call(): pl.pallas_call(kernel, out_shape=outs, in_specs=[whole if o.ndim > 1 else...  36.8 us
    ppermute x16, starting transfers between devices, shift(): lax.ppermute(block, axis, [(i, (i + distance) % size) for i in range(size)])  25.7 us
    ppermute x9, starting transfers between devices, from_behind(): lax.ppermute(block, axis, [(i - distance, i) for i in range(size) if 0 <=...  25.5 us
    ppermute x16, waiting for transfers between devices, shift(): lax.ppermute(block, axis, [(i, (i + distance) % size) for i in range(size)])  9.61 us
    unnamed x48, local copies, waits for them, and re-layouts  6.36 us
    ppermute x9, waiting for transfers between devices, from_behind(): lax.ppermute(block, axis, [(i - distance, i) for i in range(size) if 0 <=...  6.34 us
  transfers between devices with their start and end apart: 26, of which 10 were waited for; matrix products, arithmetic and copies ran while one was open for 4% of the time, Pallas kernels for 21%

commit v1 on v0

--- a/solution.py
+++ b/solution.py
@@ -10,6 +10,7 @@
 PARTS = 8
 RIM = 8
 X_COUNT = 4
+RING = 8
 TILE = 256
 HEAD = 16
 SPAN = 32768.0
@@ -41,7 +42,7 @@
     return [(n, pl.ds(n * LANES, LANES)) for n in range(width // LANES)]
 
 
-def short_filters(q_ref, k_ref, v_ref, prior_ref, taps_ref, poles_ref, qs_ref, ks_ref, vs_ref, ends_ref, own_ref, natural):
+def short_filters(q_ref, k_ref, v_ref, prior_ref, taps_ref, poles_ref, qs_ref, ks_ref, vs_ref, ends_ref, own_ref, first_ref, natural):
     tokens, width = q_ref.shape
     tap_count = taps_ref.shape[1]
     modes = poles_ref.shape[0]
@@ -83,6 +84,9 @@
     for c in range(1, PARTS):
         own = part_decay * own + ends_ref[:, c, :]
     own_ref[...] = own
+    for i in range(RIM):
+        first_ref[0, i : i + 1, :] = ks_ref[i * PARTS : i * PARTS + 1, :]
+        first_ref[1, i : i + 1, :] = vs_ref[i * PARTS : i * PARTS + 1, :]
 
 
 def long_forward(qs_ref, ks_ref, vs_ref, ends_ref, before_ref, poles_ref, residues_ref, long_ref, gated_ref, first, natural):
@@ -123,25 +127,28 @@
     return terms[0]
 
 
-def back_states(kept_ref, one_ref, three_ref, qs_ref, long_ref, poles_ref, mixed_ref, starts_ref, own_ref, rim_ref, rim_starts, natural):
+def back_states(kept_ref, one_up_ref, one_down_ref, three_up_ref, three_down_ref, qs_ref, long_ref, poles_ref, mixed_ref, starts_ref, own_ref, rim_ref, rim_starts, natural):
     tokens, width = qs_ref.shape
     modes = poles_ref.shape[0]
     steps = tokens // PARTS
     for block, lanes in lane_blocks(width):
         poles = [spread(row) for row in rows_of(poles_ref, lanes)]
 
-        def add_step(n, carry):
-            piece = 64
-            row = pl.multiple_of(n * piece, piece)
-            tile, inside = row // TILE, pl.multiple_of(row % TILE, piece)
-            total = kept_ref[pl.ds(row, piece), lanes]
-            for ref in (one_ref, three_ref):
-                start = pl.multiple_of(tile * (TILE + HEAD), HEAD)
-                total = total + decoded(ref, start, pl.ds(inside, piece), lanes)
-            natural[block, pl.ds(row, piece), :] = total
-            return carry
-
-        lax.fori_loop(0, tokens // 64, add_step, 0)
+        for half, refs in enumerate(((one_up_ref, three_up_ref), (one_down_ref, three_down_ref))):
+
+            def add_step(n, carry):
+                piece = 64
+                row = pl.multiple_of(n * piece, piece)
+                tile, inside = row // TILE, pl.multiple_of(row % TILE, piece)
+                there = pl.ds(pl.multiple_of(half * (tokens // 2) + row, piece), piece)
+                total = kept_ref[there, lanes]
+                for ref in refs:
+                    start = pl.multiple_of(tile * (TILE + HEAD), HEAD)
+                    total = total + decoded(ref, start, pl.ds(inside, piece), lanes)
+                natural[block, there, :] = total
+                return carry
+
+            lax.fori_loop(0, tokens // 128, add_step, 0)
 
         def step(back, states):
             i = steps - 1 - back
@@ -295,17 +302,16 @@
         copy.wait()
 
 
-def join_shares(place_ref, share_ref, other_ref, j, weight):
-    rows = share_ref.shape[1]
+def join_shares(place_ref, share, other, weight):
+    rows = share.shape[0]
     core = place_ref[2]
-    weight[pl.ds(pl.multiple_of(core * rows, rows), rows), :] = share_ref[j]
-    weight[pl.ds(pl.multiple_of((1 - core) * rows, rows), rows), :] = other_ref[j]
-
-
-def ring_product(target_ref, ring, weight_ref, column_of):
+    weight[pl.ds(pl.multiple_of(core * rows, rows), rows), :] = share
+    weight[pl.ds(pl.multiple_of((1 - core) * rows, rows), rows), :] = other
+
+
+def ring_product(target_ref, ring, weight_ref, column_of, first=True):
     tokens, width = target_ref.shape
     rows = tokens // 2
-    first = True
     for n, refs in ring:
         for half in range(2):
             target_rows = pl.ds(half * rows, rows)
@@ -320,15 +326,30 @@
         first = False
 
 
-def in_places(early_ref, left_ref, right_ref, *middle):
+def early_places(early_ref):
     count = early_ref.shape[0] + 3
-    ring = [(n % count, (early_ref.at[n + 2],)) for n in range(-2, 3)]
-    ring += [(3, (left_ref,)), (count - 3, (right_ref,))]
+    return [(n % count, (early_ref.at[n + 2],)) for n in range(-2, 3)]
+
+
+def late_places(count, left_ref, right_ref, *middle):
+    ring = [(3, (left_ref,)), (count - 3, (right_ref,))]
     return ring + [(count // 2, middle)] if middle else ring
 
 
-def collect(*refs):
-    *block_refs, early_ref, arrived = refs
+def in_places(early_ref, *late_refs):
+    return early_places(early_ref) + late_places(early_ref.shape[0] + 3, *late_refs)
+
+
+def own_columns(place_ref, count, along_x, width):
+    def column_of(n):
+        block = lax.rem(place_ref[3] + n, count) * along_x + place_ref[0]
+        return pl.multiple_of(block * width, width)
+
+    return column_of
+
+
+def keep_start(place_ref, weight_ref, *refs):
+    *block_refs, early_ref, kept_ref, arrived = refs
     copies = [
         pltpu.make_async_copy(ref, early_ref.at[n], arrived.at[n]) for n, ref in enumerate(block_refs)
     ]
@@ -336,6 +357,19 @@
         copy.start()
     for copy in copies:
         copy.wait()
+    width = kept_ref.shape[1]
+    count = early_ref.shape[0] + 3
+    column_of = own_columns(place_ref, count, weight_ref.shape[1] // (count * width), width)
+    ring_product(kept_ref, early_places(early_ref), weight_ref, column_of)
+
+
+def keep_finish(place_ref, weight_ref, started_ref, *refs):
+    *late_refs, kept_ref = refs
+    width = kept_ref.shape[1]
+    count = RING
+    column_of = own_columns(place_ref, count, weight_ref.shape[1] // (count * width), width)
+    kept_ref[...] = started_ref[...]
+    ring_product(kept_ref, late_places(count, *late_refs), weight_ref, column_of, False)
 
 
 def encode_tile(total, coded_ref, tile):
@@ -356,70 +390,59 @@
 
 
 def far_start(place_ref, *refs):
-    *ring_refs, shares_ref, other_ref, far_ref, weight = refs
+    *ring_refs, share_ref, other_ref, far_ref, weight = refs
     width = far_ref.shape[1]
-    join_shares(place_ref, shares_ref, other_ref, 1, weight)
+    join_shares(place_ref, share_ref[...], other_ref[...], weight)
     column_of = column_on_ring(place_ref, weight.shape[1] // width, width)
     ring_product(far_ref, in_places(*ring_refs), weight, column_of)
 
 
-def far_finish(place_ref, far_ref, middle_up_ref, middle_down_ref, shares_ref, other_ref, up_ref, down_ref, weight):
+def far_finish(place_ref, far_ref, middle_up_ref, middle_down_ref, share_ref, other_ref, up_ref, down_ref, weight):
     half, width = middle_up_ref.shape
-    count = weight.shape[1] // width
-    join_shares(place_ref, shares_ref, other_ref, 1, weight)
-    column = column_on_ring(place_ref, count, width)(count // 2)
+    count = share_ref.shape[1] // width
+    column = pl.ds(column_on_ring(place_ref, count, width)(count // 2), width)
+    join_shares(place_ref, share_ref[:, column], other_ref[:, column], weight)
     for side, (features_ref, coded_ref) in enumerate(((middle_up_ref, up_ref), (middle_down_ref, down_ref))):
-
-        def tile_step(t, carry):
-            row = pl.multiple_of(t * TILE, TILE)
+        for t in range(half // TILE):
             term = lax.dot_general(
-                features_ref[pl.ds(row, TILE), :],
-                weight[:, pl.ds(column, width)],
+                features_ref[t * TILE : (t + 1) * TILE, :],
+                weight[...],
                 (((1,), (1,)), ((), ())),
                 preferred_element_type=jnp.float32,
             )
-            encode_tile(far_ref[pl.ds(pl.multiple_of(side * half + row, TILE), TILE), :] + term, coded_ref, t)
-            return carry
-
-        lax.fori_loop(0, half // TILE, tile_step, 0)
+            row = side * half + t * TILE
+            encode_tile(far_ref[row : row + TILE, :] + term, coded_ref, t)
 
 
 def near_products(place_ref, *refs):
     *ring_refs, shares_ref, other_ref, next_ref, last_ref, weight = refs
     width = next_ref.shape[1]
     column_of = column_on_ring(place_ref, weight.shape[1] // width, width)
-    for j, target in ((0, next_ref), (2, last_ref)):
-        join_shares(place_ref, shares_ref, other_ref, j, weight)
+    for j, target in enumerate((next_ref, last_ref)):
+        join_shares(place_ref, shares_ref[j], other_ref[j], weight)
         ring_product(target, in_places(*ring_refs), weight, column_of)
 
 
-def keep_product(place_ref, *refs):
-    *ring_refs, weight_ref, kept_ref = refs
-    width = kept_ref.shape[1]
-    count = ring_refs[0].shape[0] + 3
-    along_x = weight_ref.shape[1] // (count * width)
-
-    def column_of(n):
-        block = lax.rem(place_ref[3] + n, count) * along_x + place_ref[0]
-        return pl.multiple_of(block * width, width)
-
-    ring_product(kept_ref, in_places(*ring_refs), weight_ref, column_of)
-
-
-def send_near(next_ref, last_ref, up_ref, down_ref, next_coded_ref, last_coded_ref):
-    tokens, width = next_ref.shape
-    tiles = tokens // TILE
+def send_half(next_ref, last_ref, next_coded_ref, last_coded_ref):
+    tiles = next_ref.shape[0] // TILE
     half = tiles // 2
-    everything = pl.ds(0, width)
-
-    for t in range(tiles):
-        rows = pl.ds(t * TILE, TILE)
-        start = t % half * (TILE + HEAD)
-        after, before = next_ref[rows, :], last_ref[rows, :]
-        if t < half:
-            after = after + decoded(up_ref, start, pl.ds(0, TILE), everything)
-        else:
-            before = before + decoded(down_ref, start, pl.ds(0, TILE), everything)
+    for t in range(half):
+        start = (half + t) * TILE
+        encode_tile(next_ref[start : start + TILE, :], next_coded_ref, t)
+        encode_tile(last_ref[t * TILE : (t + 1) * TILE, :], last_coded_ref, t)
+
+
+def send_joined(next_ref, last_ref, up_ref, down_ref, next_coded_ref, last_coded_ref):
+    tiles = next_ref.shape[0] // TILE
+    half = tiles // 2
+    everything = pl.ds(0, next_ref.shape[1])
+    for t in range(half):
+        coded = t * (TILE + HEAD)
+        start = (half + t) * TILE
+        after = next_ref[t * TILE : (t + 1) * TILE, :]
+        before = last_ref[start : start + TILE, :]
+        after = after + decoded(up_ref, coded, pl.ds(0, TILE), everything)
+        before = before + decoded(down_ref, coded, pl.ds(0, TILE), everything)
         encode_tile(after, next_coded_ref, t)
         encode_tile(before, last_coded_ref, t)
 
@@ -495,9 +518,9 @@
     )(place, out_weight)
     up = shift(up, "x", 1, x_count)
     down = shift(down, "x", -1, x_count)
-    q_short, k_short, v_short, ends, own_end = local_call(
+    q_short, k_short, v_short, ends, own_end, first_kv = local_call(
         short_filters,
-        [slab, slab, slab, per_part, state],
+        [slab, slab, slab, per_part, state, floats(2, RIM, width)],
         [pltpu.VMEM((width // LANES, tokens + RIM, LANES), jnp.float32)],
         (query_in, key_in, value_in, prior, short_taps, modal_poles),
         tokens * width * 80,
@@ -505,7 +528,10 @@
     right_2 = shift(right_1, "z", 1, z_count)
     left_2 = shift(left_1, "z", -1, z_count)
     one = from_behind(own_end, "ctx", 1, ctx_count)
-    right_2, left_2, one, up, down = together((right_2, left_2, one, up, down))
+    two = from_behind(own_end, "ctx", 2, ctx_count)
+    seven = from_behind(own_end, "ctx", 7, ctx_count)
+    triple = own_end + decay_1 * one + decay_2 * two
+    right_2, left_2, triple, up, down = together((right_2, left_2, triple, up, down))
 
     right_3 = shift(right_2, "z", 1, z_count)
     left_3 = shift(left_2, "z", -1, z_count)
@@ -513,31 +539,51 @@
     far_up = shift(up[rows:], "x", 1, x_count)
     far_down = shift(down[rows:], "x", -1, x_count)
     anywhere = pl.BlockSpec(memory_space=pl.ANY)
+    in_vmem = pl.BlockSpec(memory_space=pltpu.VMEM)
     blocks = (right_2, right_1, grad_out, left_1, left_2)
-    early = pl.pallas_call(
-        collect,
-        out_shape=jax.ShapeDtypeStruct((len(blocks), tokens, width), jnp.bfloat16),
-        in_specs=[anywhere] * len(blocks),
-        out_specs=pl.BlockSpec(memory_space=pltpu.VMEM),
+    early, kept = pl.pallas_call(
+        keep_start,
+        out_shape=[jax.ShapeDtypeStruct((len(blocks), tokens, width), jnp.bfloat16), slab],
+        in_specs=[pl.BlockSpec(memory_space=pltpu.SMEM), in_vmem] + [anywhere] * len(blocks),
+        out_specs=[in_vmem] * 2,
         scratch_shapes=[pltpu.SemaphoreType.DMA((len(blocks),))],
         compiler_params=pltpu.CompilerParams(vmem_limit_bytes=VMEM_LIMIT),
-    )(*blocks)
-    right_3, left_3, far_up, far_down, early = together((right_3, left_3, far_up, far_down, early))
+        cost_estimate=pl.CostEstimate(
+            flops=tokens * width * width * 10, bytes_accessed=tokens * width * 24, transcendentals=0
+        ),
+    )(place, out_weight, *blocks)
+    near_shares, triple, kept = together((jnp.stack([down[:rows], up[:rows]]), triple, kept))
+    other_near = lax.ppermute(near_shares, "ctx", [(i, i ^ 1) for i in range(ctx_count)])
+    decay_3 = decay_2 * decay_1
+    before = (
+        from_behind(triple, "ctx", 1, ctx_count)
+        + decay_3 * from_behind(triple, "ctx", 4, ctx_count)
+        + decay_3 * decay_3 * seven
+    )
+    long_out, gated = local_call(
+        long_forward,
+        [slab, rounded],
+        [part_scratch, natural_scratch],
+        (q_short, k_short, v_short, ends, before, modal_poles, modal_residues),
+        tokens * width * 70,
+    )
+    right_3, left_3, far_up, far_down, early, kept, gated, other_near = together(
+        (right_3, left_3, far_up, far_down, early, kept, gated, other_near)
+    )
 
     middle_up = shift(right_3[: tokens // 2], "z", 1, z_count)
     middle_down = shift(left_3[tokens // 2 :], "z", -1, z_count)
-    shares = jnp.stack([down[:rows], jnp.concatenate([far_up, far_down]), up[:rows]])
-    other = lax.ppermute(shares, "ctx", [(i, i ^ 1) for i in range(ctx_count)])
+    far_share = jnp.concatenate([far_up, far_down])
+    other_far = lax.ppermute(far_share, "ctx", [(i, i ^ 1) for i in range(ctx_count)])
 
     weight_scratch = pltpu.VMEM((width, z_count * width), jnp.bfloat16)
     product_cost = tokens * width * z_count * width * 2
     half_code = jax.ShapeDtypeStruct((tokens // TILE // 2 * (TILE + HEAD), width), jnp.bfloat16)
-    code = jax.ShapeDtypeStruct((tokens // TILE * (TILE + HEAD), width), jnp.bfloat16)
     (far,) = local_call(
         far_start,
         [slab],
         [weight_scratch],
-        (place, early, left_3, right_3, shares, other),
+        (place, early, left_3, right_3, far_share, other_far),
         product_cost,
     )
     middle_up, middle_down, far = together((middle_up, middle_down, far))
@@ -545,8 +591,8 @@
     up, down = local_call(
         far_finish,
         [half_code, half_code],
-        [weight_scratch],
-        (place, far, middle_up, middle_down, shares, other),
+        [pltpu.VMEM((width, width), jnp.bfloat16)],
+        (place, far, middle_up, middle_down, far_share, other_far),
         product_cost // z_count,
     )
     up = shift(up, "x", 1, x_count)
@@ -555,37 +601,28 @@
         near_products,
         [slab, slab],
         [weight_scratch],
-        (place, *on_ring, shares, other),
+        (place, *on_ring, near_shares, other_near),
         2 * product_cost,
     )
-    pair = own_end + decay_1 * one
-    two = from_behind(pair, "ctx", 2, ctx_count)
-    up, down, after, last, two = together((up, down, after, last, two))
-    after, last = local_call(
-        send_near, [code, code], [], (after, last, up, down), tokens * width * 64
-    )
-    after = shift(after, "x", 1, x_count)
-    last = shift(last, "x", -1, x_count)
-    four = from_behind(pair + decay_2 * two, "ctx", 4, ctx_count)
-    before = one + decay_1 * two + decay_2 * decay_1 * four
-    first_kv = jnp.stack([k_short[: RIM * PARTS : PARTS], v_short[: RIM * PARTS : PARTS]])
-    next_kv = from_behind(first_kv, "ctx", -1, ctx_count)
+    after_2, last_1 = local_call(
+        send_half, [half_code, half_code], [], (after, last), tokens * width * 16
+    )
+    after_2 = shift(after_2, "x", 1, x_count)
+    last_1 = shift(last_1, "x", -1, x_count)
+    after_1, last_2 = local_call(
+        send_joined, [half_code, half_code], [], (after, last, up, down), tokens * width * 32
+    )
+    after_1 = shift(after_1, "x", 1, x_count)
+    last_2 = shift(last_2, "x", -1, x_count)
     (kept,) = local_call(
-        keep_product, [slab], [], (place, *on_ring, out_weight), product_cost
-    )
-    long_out, gated = local_call(
-        long_forward,
-        [slab, rounded],
-        [part_scratch, natural_scratch],
-        (q_short, k_short, v_short, ends, before, modal_poles, modal_residues),
-        tokens * width * 70,
-    )
-    after, last, gated, kept, next_kv = together((after, last, gated, kept, next_kv))
+        keep_finish, [slab], [], (place, out_weight, kept, *on_ring[1:]), product_cost // 2
+    )
+    after_1, after_2, last_1, last_2, kept = together((after_1, after_2, last_1, last_2, kept))
     mixed_steps, starts, own_start, rim = local_call(
         back_states,
         [slab, per_part, state, floats(modes + 2 * RIM, width)],
         [part_scratch, natural_scratch],
-        (kept, after, last, q_short, long_out, modal_poles),
+        (kept, after_1, after_2, last_1, last_2, q_short, long_out, modal_poles),
         tokens * width * 40,
     )
 
@@ -594,7 +631,8 @@
         back_local, [slab], [], (mixed_steps, q_short, modal_poles, modal_residues), tokens * width * 64
     )
     two = from_behind(own_start, "ctx", -2, ctx_count)
-    near, two, local = together((near, two, local))
+    next_kv = from_behind(first_kv, "ctx", -1, ctx_count)
+    near, two, local, next_kv = together((near, two, local, next_kv))
     rim_size = modes + 2 * RIM
     near_rim = near[:rim_size]
     triple = own_start + decay_1 * near[rim_size:] + decay_2 * two

time: 121 us -> 127 us (1.050)
  starting transfers between devices: 51.8 us -> 61.9 us
  waiting for transfers between devices: 15.9 us -> 21.1 us
  Pallas kernels: 38.2 us -> 33.6 us
  local copies, waits for them, and re-layouts: 11 us -> 6.94 us
  other arithmetic: 1.56 us -> 0.26 us
    ppermute x9 -> x11, starting transfers between devices: 25.5 us -> 33.8 us  [from_behind(): lax.ppermute(block, axis, [(i - distance, i) for i in range(size) if 0 <=...]
    ppermute x16 -> x18, waiting for transfers between devices: 9.61 us -> 16.6 us  [shift(): lax.ppermute(block, axis, [(i, (i + distance) % size) for i in range(size)])]
    pallas_call x11 -> x12, Pallas kernels: 36.8 us -> 30.7 us  [local_call(): pl.pallas_call(kernel, out_shape=outs, in_specs=[whole if o.ndim > 1 else...]
    ppermute x16 -> x18, starting transfers between devices: 25.7 us -> 27.5 us  [shift(): lax.ppermute(block, axis, [(i, (i + distance) % size) for i in range(size)])]
    ppermute x9 -> x11, waiting for transfers between devices: 6.34 us -> 4.56 us  [from_behind(): lax.ppermute(block, axis, [(i - distance, i) for i in range(size) if 0 <=...]
    slice x2 -> x0, local copies, waits for them, and re-layouts: 1.7 us -> none  [the longest x1 0.85 us: shards(): v_short[:RIM * PARTS:PARTS]]
    pallas_call x1, Pallas kernels: 0.23 us -> 1.65 us  [shards(): pl.pallas_call(keep_start, out_shape=[jax.ShapeDtypeStruct((len(blocks),...]
    another operation x3 -> x1, other arithmetic: 1.38 us -> 0.1 us  [shards(): jnp.stack([down[:rows], up[:rows]])]
  transfers between devices with their start and end apart: 26 -> 31, of which waited for: 10 -> 10; matrix products, arithmetic and copies ran while one was open for 4% -> 1% of each run, Pallas kernels for 21% -> 17%
where the time goes in v1:
time: 127 us; the launch traced here: 125 us
  starting transfers between devices  61.9 us (49%)
  Pallas kernels  33.6 us (26%)
  waiting for transfers between devices  21.1 us (17%)
  local copies, waits for them, and re-layouts  6.94 us (5%)
    ppermute x11, starting transfers between devices, from_behind(): lax.ppermute(block, axis, [(i - distance, i) for i in range(size) if 0 <=...  33.8 us
    pallas_call x12, Pallas kernels, local_call(): pl.pallas_call(kernel, out_shape=outs, in_specs=[whole if o.ndim > 1 else...  30.7 us
    ppermute x18, starting transfers between devices, shift(): lax.ppermute(block, axis, [(i, (i + distance) % size) for i in range(size)])  27.5 us
    ppermute x18, waiting for transfers between devices, shift(): lax.ppermute(block, axis, [(i, (i + distance) % size) for i in range(size)])  16.6 us
    unnamed x19, local copies, waits for them, and re-layouts  5.35 us
    ppermute x11, waiting for transfers between devices, from_behind(): lax.ppermute(block, axis, [(i - distance, i) for i in range(size) if 0 <=...  4.56 us
  transfers between devices with their start and end apart: 31, of which 10 were waited for; matrix products, arithmetic and copies ran while one was open for 1% of the time, Pallas kernels for 17%

profile of v1, /device:TPU:1, one launch (start us, length us, event | category | flops | bytes accessed | tf_op | source)
XLA Modules:
  0.0 124.9 jit_solution(327356408997034068)
XLA Ops:
  0.7 2.5 %collective-permute-start = (bf16[1024,256]{1,0:T(8,128)(2,1)}, bf16[1024,256]{1,0:T(8,128)(2,1)S(1)}, u32[]{:S(2)}, u32[]{:S(2)}) collective-permute-start(bf16[1024,256]{1,0:T(8,128)(2,1)} %refs_2_.1), channel_id=1, source_target_pairs={{0,4},{4,8},{8,12},{12,16},{16,20},{20,24},{24,28},{28,0},{1,5},{5... | collective-permute-start | bytes 1572872 | tf_op jit(solution)/shard_map/ppermute | solution.py:476
  3.2 4.0 %collective-permute-start.2 = (bf16[1024,256]{1,0:T(8,128)(2,1)}, bf16[1024,256]{1,0:T(8,128)(2,1)S(1)}, u32[]{:S(2)}, u32[]{:S(2)}) collective-permute-start(bf16[1024,256]{1,0:T(8,128)(2,1)} %refs_2_.1), channel_id=1, source_target_pairs={{0,28},{4,0},{8,4},{12,8},{16,12},{20,16},{24,20},{28,24},{1,29},{... | collective-permute-start | bytes 1572872 | tf_op jit(solution)/shard_map/ppermute | solution.py:476
  8.6 4.0 %collective-permute-start.4 = (bf16[3,16,256]{2,1,0:T(8,128)(2,1)S(1)}, bf16[3,16,256]{2,1,0:T(8,128)(2,1)S(1)}, u32[]{:S(2)}, u32[]{:S(2)}) collective-permute-start(bf16[3,16,256]{2,1,0:T(8,128)(2,1)S(1)} %pad_maximum_fusion.2), channel_id=1, source_target_pairs={{0,32},{32,64},{64,96},{96,128},{128,160},{160,192},{192,224},{1,3... | collective-permute-start | bytes 73736 | tf_op jit(solution)/shard_map/ppermute | solution.py:480
  19.8 2.7 %collective-permute-start.3 = (bf16[1024,256]{1,0:T(8,128)(2,1)S(1)}, bf16[1024,256]{1,0:T(8,128)(2,1)S(1)}, u32[]{:S(2)}, u32[]{:S(2)}) collective-permute-start(bf16[1024,256]{1,0:T(8,128)(2,1)S(1)} %collective-permute-done.2.refs_3_), channel_id=1, source_target_pairs={{0,28},{4,0},{8,4},{12,8},{16,12},{20,16},{24,20},{28,24},{1,29},{... | collective-permute-start | bytes 1572872 | tf_op jit(solution)/shard_map/ppermute | solution.py:476
  25.6 4.7 %shard_map.111 = (f32[1024,256]{1,0:T(8,128)S(1)}, f32[1024,256]{1,0:T(8,128)S(1)}, f32[1024,256]{1,0:T(8,128)S(1)}, f32[16,8,256]{2,1,0:T(8,128)S(1)}, f32[16,256]{1,0:T(8,128)S(1)}, /*index=5*/f32[2,8,256]{2,1,0:T(8,128)S(1)}) custom-call(bf16[1024,256]{1,0:T(8,128)(2,1)S(1)} %copy-done.3, bf16[1024,256]{1,0:T(8,128)(2,1)S(1)} %copy-done.4, ...), custom_call_target="tpu_custom_call" | custom-call | flops 20971520 | bytes 327680 | tf_op jit(solution)/shard_map/pallas_call | solution.py:460
  30.3 3.2 %collective-permute-start.6 = (f32[16,256]{1,0:T(8,128)S(1)}, f32[16,256]{1,0:T(8,128)S(1)}, u32[]{:S(2)}, u32[]{:S(2)}) collective-permute-start(f32[16,256]{1,0:T(8,128)S(1)} %get-tuple-element.64), channel_id=1, source_target_pairs={{0,64},{32,96},{64,128},{96,160},{128,192},{160,224},{1,65},{33,97... | collective-permute-start | bytes 49160 | tf_op jit(solution)/shard_map/ppermute | solution.py:480
  34.4 6.9 %collective-permute-start.5 = (f32[16,256]{1,0:T(8,128)S(1)}, f32[16,256]{1,0:T(8,128)S(1)}, u32[]{:S(2)}, u32[]{:S(2)}) collective-permute-start(f32[16,256]{1,0:T(8,128)S(1)} %get-tuple-element.64), channel_id=1, source_target_pairs={{0,32},{32,64},{64,96},{96,128},{128,160},{160,192},{192,224},{1,3... | collective-permute-start | bytes 49160 | tf_op jit(solution)/shard_map/ppermute | solution.py:480
  44.3 2.7 %collective-permute-start.10 = (bf16[1024,256]{1,0:T(8,128)(2,1)S(1)}, bf16[1024,256]{1,0:T(8,128)(2,1)S(1)}, u32[]{:S(2)}, u32[]{:S(2)}) collective-permute-start(bf16[1024,256]{1,0:T(8,128)(2,1)S(1)} %collective-permute-done.3.refs_4_), channel_id=1, source_target_pairs={{0,28},{4,0},{8,4},{12,8},{16,12},{20,16},{24,20},{28,24},{1,29},{... | collective-permute-start | bytes 1572872 | tf_op jit(solution)/shard_map/ppermute | solution.py:476
  47.6 5.9 %collective-permute-start.14 = (f32[16,256]{1,0:T(8,128)S(1)}, f32[16,256]{1,0:T(8,128)S(1)}, u32[]{:S(2)}, u32[]{:S(2)}) collective-permute-start(f32[16,256]{1,0:T(8,128)S(1)} %fusion), channel_id=1, source_target_pairs={{0,128},{32,160},{64,192},{96,224},{1,129},{33,161},{65,193},{97,2... | collective-permute-start | bytes 49160 | tf_op jit(solution)/shard_map/ppermute | solution.py:480
  53.5 3.1 %collective-permute-start.13 = (f32[16,256]{1,0:T(8,128)S(1)}, f32[16,256]{1,0:T(8,128)S(1)}, u32[]{:S(2)}, u32[]{:S(2)}) collective-permute-start(f32[16,256]{1,0:T(8,128)S(1)} %fusion), channel_id=1, source_target_pairs={{0,32},{32,64},{64,96},{96,128},{128,160},{160,192},{192,224},{1,3... | collective-permute-start | bytes 49160 | tf_op jit(solution)/shard_map/ppermute | solution.py:480
  58.2 3.9 %shard_map.114 = (f32[1024,256]{1,0:T(8,128)S(1)}, bf16[1024,256]{1,0:T(8,128)(2,1)}) custom-call(f32[1024,256]{1,0:T(8,128)S(1)} %get-tuple-element.76.qs_ref, f32[1024,256]{1,0:T(8,128)S(1)} %get-tuple-element.77.ks_ref, f32[1024,256]{1,0:T(8,128)S(1)} %get-tuple-element.78.vs_ref, f32[16,8,256]{2,1,0:T(8,128)S(1)} %get-tuple-element.79.ends_ref, ...), custom_call_target="tpu_custom_call" | custom-call | flops 18350080 | bytes 286720 | tf_op jit(solution)/shard_map/pallas_call | solution.py:460
  62.1 2.7 %collective-permute-done.12 = bf16[64,2048]{1,0:T(8,128)(2,1)S(1)} collective-permute-done((bf16[64,2048]{1,0:T(8,128)(2,1)S(1)}, bf16[64,2048]{1,0:T(8,128)(2,1)S(1)}, u32[]{:S(2)}, u32[]{:S(2)}) %collective-permute-start.12) | collective-permute-done | bytes 262176 | tf_op jit(solution)/shard_map/ppermute | solution.py:476
  64.8 2.7 %collective-permute-done.11 = bf16[64,2048]{1,0:T(8,128)(2,1)S(1)} collective-permute-done((bf16[64,2048]{1,0:T(8,128)(2,1)S(1)}, bf16[64,2048]{1,0:T(8,128)(2,1)S(1)}, u32[]{:S(2)}, u32[]{:S(2)}) %collective-permute-start.11) | collective-permute-done | bytes 262176 | tf_op jit(solution)/shard_map/ppermute | solution.py:476
  68.4 2.7 %collective-permute-start.18 = (bf16[512,256]{1,0:T(8,128)(2,1)S(1)}, bf16[512,256]{1,0:T(8,128)(2,1)S(1)}, u32[]{:S(2)}, u32[]{:S(2)}) collective-permute-start(bf16[512,256]{1,0:T(8,128)(2,1)S(1)} %slice.41), channel_id=1, source_target_pairs={{0,28},{4,0},{8,4},{12,8},{16,12},{20,16},{24,20},{28,24},{1,29},{... | collective-permute-start | bytes 786440 | tf_op jit(solution)/shard_map/ppermute | solution.py:476
  72.9 4.6 %collective-permute-done.17.refs_3_.middle_up_ref.refs_2_ = bf16[512,256]{1,0:T(8,128)(2,1)S(1)} collective-permute-done((bf16[512,256]{1,0:T(8,128)(2,1)S(1)}, bf16[512,256]{1,0:T(8,128)(2,1)S(1)}, u32[]{:S(2)}, u32[]{:S(2)}) %collective-permute-start.17) | collective-permute-done | bytes 262176 | tf_op jit(solution)/shard_map/ppermute | solution.py:476
  78.8 2.7 %collective-permute-start.21 = (bf16[544,256]{1,0:T(8,128)(2,1)S(1)}, bf16[544,256]{1,0:T(8,128)(2,1)S(1)}, u32[]{:S(2)}, u32[]{:S(2)}) collective-permute-start(bf16[544,256]{1,0:T(8,128)(2,1)S(1)} %get-tuple-element.96), channel_id=1, source_target_pairs={{0,3},{1,0},{2,1},{3,2},{4,7},{5,4},{6,5},{7,6},{8,11},{9,8},{10,9... | collective-permute-start | bytes 835592 | tf_op jit(solution)/shard_map/ppermute | solution.py:476
  81.5 3.0 %shard_map.116 = (f32[1024,256]{1,0:T(8,128)S(1)}, f32[1024,256]{1,0:T(8,128)S(1)}) custom-call(s32[4]{0:T(128)S(1)} %pad_add_fusion.place_ref, bf16[5,1024,256]{2,1,0:T(8,128)(2,1)S(1)} %get-tuple-element.84.refs_0_, bf16[1024,256]{1,0:T(8,128)(2,1)S(1)} %collective-permute-done.10.refs_1_.refs_0_, ...), custom_call_target="tpu_custom_call" | custom-call | flops 2147483648 | bytes 33554432 | tf_op jit(solution)/shard_map/pallas_call | solution.py:460
  85.0 2.7 %collective-permute-start.24 = (bf16[544,256]{1,0:T(8,128)(2,1)S(1)}, bf16[544,256]{1,0:T(8,128)(2,1)S(1)}, u32[]{:S(2)}, u32[]{:S(2)}) collective-permute-start(bf16[544,256]{1,0:T(8,128)(2,1)S(1)} %get-tuple-element.99), channel_id=1, source_target_pairs={{0,3},{1,0},{2,1},{3,2},{4,7},{5,4},{6,5},{7,6},{8,11},{9,8},{10,9... | collective-permute-start | bytes 835592 | tf_op jit(solution)/shard_map/ppermute | solution.py:476
  88.6 2.7 %collective-permute-start.25 = (bf16[544,256]{1,0:T(8,128)(2,1)S(1)}, bf16[544,256]{1,0:T(8,128)(2,1)S(1)}, u32[]{:S(2)}, u32[]{:S(2)}) collective-permute-start(bf16[544,256]{1,0:T(8,128)(2,1)S(1)} %get-tuple-element.100), channel_id=1, source_target_pairs={{0,3},{1,0},{2,1},{3,2},{4,7},{5,4},{6,5},{7,6},{8,11},{9,8},{10,9... | collective-permute-start | bytes 835592 | tf_op jit(solution)/shard_map/ppermute | solution.py:476
  93.0 6.0 %collective-permute-done.22.one_up_ref = bf16[544,256]{1,0:T(8,128)(2,1)S(1)} collective-permute-done((bf16[544,256]{1,0:T(8,128)(2,1)S(1)}, bf16[544,256]{1,0:T(8,128)(2,1)S(1)}, u32[]{:S(2)}, u32[]{:S(2)}) %collective-permute-start.22) | collective-permute-done | bytes 278560 | tf_op jit(solution)/shard_map/ppermute | solution.py:476
  98.9 3.7 %shard_map.121 = (f32[1024,256]{1,0:T(8,128)S(1)}, f32[16,8,256]{2,1,0:T(8,128)S(1)}, f32[16,256]{1,0:T(8,128)S(1)}, f32[32,256]{1,0:T(8,128)S(1)}) custom-call(f32[1024,256]{1,0:T(8,128)S(1)} %shard_map.120.kept_ref, bf16[544,256]{1,0:T(8,128)(2,1)S(1)} %collective-permute-done.22.one_up_ref, bf16[544,256]{1,0:T(8,128)(2,1)S(1)} %collective-permute-done.23.one_down_ref, ...), custom_call_target="tpu_custom_call" | custom-call | flops 10485760 | bytes 163840 | tf_op jit(solution)/shard_map/pallas_call | solution.py:460
  102.7 4.2 %collective-permute-start.26 = (f32[48,256]{1,0:T(8,128)S(1)}, f32[48,256]{1,0:T(8,128)S(1)}, u32[]{:S(2)}, u32[]{:S(2)}) collective-permute-start(f32[48,256]{1,0:T(8,128)S(1)} %pad_maximum_fusion.1), channel_id=1, source_target_pairs={{32,0},{64,32},{96,64},{128,96},{160,128},{192,160},{224,192},{33,... | collective-permute-start | bytes 147464 | tf_op jit(solution)/shard_map/ppermute | solution.py:480
  110.1 2.6 %shard_map.122.local_ref = f32[1024,256]{1,0:T(8,128)S(1)} custom-call(f32[1024,256]{1,0:T(8,128)S(1)} %get-tuple-element.110.mixed_ref, f32[1024,256]{1,0:T(8,128)S(1)} %get-tuple-element.76.qs_ref, f32[16,256]{1,0:T(8,128)S(1)} %copy-done.2, f32[16,256]{1,0:T(8,128)S(1)} %copy-done.8), custom_call_target="tpu_custom_call" | custom-call | flops 16777216 | bytes 262144 | tf_op jit(solution)/shard_map/pallas_call | solution.py:460
  119.6 5.2 %shard_map.124 = (bf16[1024,256]{1,0:T(8,128)(2,1)}, bf16[1024,256]{1,0:T(8,128)(2,1)}) custom-call(f32[1024,256]{1,0:T(8,128)S(1)} %shard_map.122.local_ref, f32[1024,256]{1,0:T(8,128)S(1)} %get-tuple-element.77.ks_ref, f32[1024,256]{1,0:T(8,128)S(1)} %get-tuple-element.78.vs_ref, f32[16,8,256]{2,1,0:T(8,128)S(1)} %get-tuple-element.116.starts_ref, ...), custom_call_target="tpu_custom_call" | custom-call | flops 20971520 | bytes 327680 | tf_op jit(solution)/shard_map/pallas_call | solution.py:460
  (89 shorter events, 34.8 us)
Async XLA Ops:
  0.7 19.1 %collective-permute-start = (bf16[1024,256]{1,0:T(8,128)(2,1)}, bf16[1024,256]{1,0:T(8,128)(2,1)S(1)}, u32[]{:S(2)}, u32[]{:S(2)}) collective-permute-start(bf16[1024,256]{1,0:T(8,128)(2,1)} %refs_2_.1), channel_id=1, source_target_pairs={{0,4},{4,8},{8,12},{12,16},{16,20},{20,24},{24,28},{28,0},{1,5},{5... | collective-permute-start | bytes 1572872 | tf_op jit(solution)/shard_map/ppermute | solution.py:476
  3.2 16.6 %collective-permute-start.2 = (bf16[1024,256]{1,0:T(8,128)(2,1)}, bf16[1024,256]{1,0:T(8,128)(2,1)S(1)}, u32[]{:S(2)}, u32[]{:S(2)}) collective-permute-start(bf16[1024,256]{1,0:T(8,128)(2,1)} %refs_2_.1), channel_id=1, source_target_pairs={{0,28},{4,0},{8,4},{12,8},{16,12},{20,16},{24,20},{28,24},{1,29},{... | collective-permute-start | bytes 1572872 | tf_op jit(solution)/shard_map/ppermute | solution.py:476
  17.0 25.1 %collective-permute-start.7 = (bf16[192,2048]{1,0:T(8,128)(2,1)S(1)}, bf16[192,2048]{1,0:T(8,128)(2,1)S(1)}, u32[]{:S(2)}, u32[]{:S(2)}) collective-permute-start(bf16[192,2048]{1,0:T(8,128)(2,1)S(1)} %get-tuple-element.66), channel_id=1, source_target_pairs={{0,1},{1,2},{2,3},{3,0},{4,5},{5,6},{6,7},{7,4},{8,9},{9,10},{10,1... | collective-permute-start | bytes 2359304 | tf_op jit(solution)/shard_map/ppermute | solution.py:476
  18.3 23.9 %collective-permute-start.8 = (bf16[192,2048]{1,0:T(8,128)(2,1)S(1)}, bf16[192,2048]{1,0:T(8,128)(2,1)S(1)}, u32[]{:S(2)}, u32[]{:S(2)}) collective-permute-start(bf16[192,2048]{1,0:T(8,128)(2,1)S(1)} %get-tuple-element.67), channel_id=1, source_target_pairs={{0,3},{1,0},{2,1},{3,2},{4,7},{5,4},{6,5},{7,6},{8,11},{9,8},{10,9... | collective-permute-start | bytes 2359304 | tf_op jit(solution)/shard_map/ppermute | solution.py:476
  19.8 22.4 %collective-permute-start.1 = (bf16[1024,256]{1,0:T(8,128)(2,1)S(1)}, bf16[1024,256]{1,0:T(8,128)(2,1)S(1)}, u32[]{:S(2)}, u32[]{:S(2)}) collective-permute-start(bf16[1024,256]{1,0:T(8,128)(2,1)S(1)} %collective-permute-done.refs_1_), channel_id=1, source_target_pairs={{0,4},{4,8},{8,12},{12,16},{16,20},{20,24},{24,28},{28,0},{1,5},{5... | collective-permute-start | bytes 1572872 | tf_op jit(solution)/shard_map/ppermute | solution.py:476
  19.8 22.4 %collective-permute-start.3 = (bf16[1024,256]{1,0:T(8,128)(2,1)S(1)}, bf16[1024,256]{1,0:T(8,128)(2,1)S(1)}, u32[]{:S(2)}, u32[]{:S(2)}) collective-permute-start(bf16[1024,256]{1,0:T(8,128)(2,1)S(1)} %collective-permute-done.2.refs_3_), channel_id=1, source_target_pairs={{0,28},{4,0},{8,4},{12,8},{16,12},{20,16},{24,20},{28,24},{1,29},{... | collective-permute-start | bytes 1572872 | tf_op jit(solution)/shard_map/ppermute | solution.py:476
  34.4 7.8 %collective-permute-start.5 = (f32[16,256]{1,0:T(8,128)S(1)}, f32[16,256]{1,0:T(8,128)S(1)}, u32[]{:S(2)}, u32[]{:S(2)}) collective-permute-start(f32[16,256]{1,0:T(8,128)S(1)} %get-tuple-element.64), channel_id=1, source_target_pairs={{0,32},{32,64},{64,96},{96,128},{128,160},{160,192},{192,224},{1,3... | collective-permute-start | bytes 49160 | tf_op jit(solution)/shard_map/ppermute | solution.py:480
  44.1 23.4 %collective-permute-start.16 = (bf16[2,128,2048]{2,1,0:T(8,128)(2,1)S(1)}, bf16[2,128,2048]{2,1,0:T(8,128)(2,1)S(1)}, u32[]{:S(2)}, u32[]{:S(2)}) collective-permute-start(bf16[2,128,2048]{2,1,0:T(8,128)(2,1)S(1)} %pad_maximum_fusion.refs_5_), channel_id=1, source_target_pairs={{0,32},{32,0},{64,96},{96,64},{128,160},{160,128},{192,224},{224,1... | collective-permute-start | bytes 3145736 | tf_op jit(solution)/shard_map/ppermute | solution.py:556
  44.2 23.3 %collective-permute-start.9 = (bf16[1024,256]{1,0:T(8,128)(2,1)S(1)}, bf16[1024,256]{1,0:T(8,128)(2,1)S(1)}, u32[]{:S(2)}, u32[]{:S(2)}) collective-permute-start(bf16[1024,256]{1,0:T(8,128)(2,1)S(1)} %collective-permute-done.1.refs_0_), channel_id=1, source_target_pairs={{0,4},{4,8},{8,12},{12,16},{16,20},{20,24},{24,28},{28,0},{1,5},{5... | collective-permute-start | bytes 1572872 | tf_op jit(solution)/shard_map/ppermute | solution.py:476
  44.3 23.2 %collective-permute-start.10 = (bf16[1024,256]{1,0:T(8,128)(2,1)S(1)}, bf16[1024,256]{1,0:T(8,128)(2,1)S(1)}, u32[]{:S(2)}, u32[]{:S(2)}) collective-permute-start(bf16[1024,256]{1,0:T(8,128)(2,1)S(1)} %collective-permute-done.3.refs_4_), channel_id=1, source_target_pairs={{0,28},{4,0},{8,4},{12,8},{16,12},{20,16},{24,20},{28,24},{1,29},{... | collective-permute-start | bytes 1572872 | tf_op jit(solution)/shard_map/ppermute | solution.py:476
  46.9 6.5 %collective-permute-start.15 = (f32[16,256]{1,0:T(8,128)S(1)}, f32[16,256]{1,0:T(8,128)S(1)}, u32[]{:S(2)}, u32[]{:S(2)}) collective-permute-start(f32[16,256]{1,0:T(8,128)S(1)} %get-tuple-element.64), channel_id=1, source_target_pairs={{0,224},{1,225},{2,226},{3,227},{4,228},{5,229},{6,230},{7,231},{8... | collective-permute-start | bytes 49160 | tf_op jit(solution)/shard_map/ppermute | solution.py:480
  47.6 9.0 %collective-permute-start.14 = (f32[16,256]{1,0:T(8,128)S(1)}, f32[16,256]{1,0:T(8,128)S(1)}, u32[]{:S(2)}, u32[]{:S(2)}) collective-permute-start(f32[16,256]{1,0:T(8,128)S(1)} %fusion), channel_id=1, source_target_pairs={{0,128},{32,160},{64,192},{96,224},{1,129},{33,161},{65,193},{97,2... | collective-permute-start | bytes 49160 | tf_op jit(solution)/shard_map/ppermute | solution.py:480
  56.7 8.2 %collective-permute-start.12 = (bf16[64,2048]{1,0:T(8,128)(2,1)S(1)}, bf16[64,2048]{1,0:T(8,128)(2,1)S(1)}, u32[]{:S(2)}, u32[]{:S(2)}) collective-permute-start(bf16[64,2048]{1,0:T(8,128)(2,1)S(1)} %slice.37), channel_id=1, source_target_pairs={{0,3},{1,0},{2,1},{3,2},{4,7},{5,4},{6,5},{7,6},{8,11},{9,8},{10,9... | collective-permute-start | bytes 786440 | tf_op jit(solution)/shard_map/ppermute | solution.py:476
  58.0 9.5 %collective-permute-start.11 = (bf16[64,2048]{1,0:T(8,128)(2,1)S(1)}, bf16[64,2048]{1,0:T(8,128)(2,1)S(1)}, u32[]{:S(2)}, u32[]{:S(2)}) collective-permute-start(bf16[64,2048]{1,0:T(8,128)(2,1)S(1)} %slice.36), channel_id=1, source_target_pairs={{0,1},{1,2},{2,3},{3,0},{4,5},{5,6},{6,7},{7,4},{8,9},{9,10},{10,1... | collective-permute-start | bytes 786440 | tf_op jit(solution)/shard_map/ppermute | solution.py:476
  68.2 9.3 %collective-permute-start.17 = (bf16[512,256]{1,0:T(8,128)(2,1)S(1)}, bf16[512,256]{1,0:T(8,128)(2,1)S(1)}, u32[]{:S(2)}, u32[]{:S(2)}) collective-permute-start(bf16[512,256]{1,0:T(8,128)(2,1)S(1)} %slice.40), channel_id=1, source_target_pairs={{0,4},{4,8},{8,12},{12,16},{16,20},{20,24},{24,28},{28,0},{1,5},{5... | collective-permute-start | bytes 786440 | tf_op jit(solution)/shard_map/ppermute | solution.py:476
  68.4 9.1 %collective-permute-start.18 = (bf16[512,256]{1,0:T(8,128)(2,1)S(1)}, bf16[512,256]{1,0:T(8,128)(2,1)S(1)}, u32[]{:S(2)}, u32[]{:S(2)}) collective-permute-start(bf16[512,256]{1,0:T(8,128)(2,1)S(1)} %slice.41), channel_id=1, source_target_pairs={{0,28},{4,0},{8,4},{12,8},{16,12},{20,16},{24,20},{28,24},{1,29},{... | collective-permute-start | bytes 786440 | tf_op jit(solution)/shard_map/ppermute | solution.py:476
  78.8 8.9 %collective-permute-start.20 = (bf16[544,256]{1,0:T(8,128)(2,1)S(1)}, bf16[544,256]{1,0:T(8,128)(2,1)S(1)}, u32[]{:S(2)}, u32[]{:S(2)}) collective-permute-start(bf16[544,256]{1,0:T(8,128)(2,1)S(1)} %get-tuple-element.95), channel_id=1, source_target_pairs={{0,1},{1,2},{2,3},{3,0},{4,5},{5,6},{6,7},{7,4},{8,9},{9,10},{10,1... | collective-permute-start | bytes 835592 | tf_op jit(solution)/shard_map/ppermute | solution.py:476
  78.8 8.9 %collective-permute-start.21 = (bf16[544,256]{1,0:T(8,128)(2,1)S(1)}, bf16[544,256]{1,0:T(8,128)(2,1)S(1)}, u32[]{:S(2)}, u32[]{:S(2)}) collective-permute-start(bf16[544,256]{1,0:T(8,128)(2,1)S(1)} %get-tuple-element.96), channel_id=1, source_target_pairs={{0,3},{1,0},{2,1},{3,2},{4,7},{5,4},{6,5},{7,6},{8,11},{9,8},{10,9... | collective-permute-start | bytes 835592 | tf_op jit(solution)/shard_map/ppermute | solution.py:476
  84.9 8.0 %collective-permute-start.23 = (bf16[544,256]{1,0:T(8,128)(2,1)S(1)}, bf16[544,256]{1,0:T(8,128)(2,1)S(1)}, u32[]{:S(2)}, u32[]{:S(2)}) collective-permute-start(bf16[544,256]{1,0:T(8,128)(2,1)S(1)} %get-tuple-element.98), channel_id=1, source_target_pairs={{0,1},{1,2},{2,3},{3,0},{4,5},{5,6},{6,7},{7,4},{8,9},{9,10},{10,1... | collective-permute-start | bytes 835592 | tf_op jit(solution)/shard_map/ppermute | solution.py:476
  85.0 7.9 %collective-permute-start.24 = (bf16[544,256]{1,0:T(8,128)(2,1)S(1)}, bf16[544,256]{1,0:T(8,128)(2,1)S(1)}, u32[]{:S(2)}, u32[]{:S(2)}) collective-permute-start(bf16[544,256]{1,0:T(8,128)(2,1)S(1)} %get-tuple-element.99), channel_id=1, source_target_pairs={{0,3},{1,0},{2,1},{3,2},{4,7},{5,4},{6,5},{7,6},{8,11},{9,8},{10,9... | collective-permute-start | bytes 835592 | tf_op jit(solution)/shard_map/ppermute | solution.py:476
  88.5 10.4 %collective-permute-start.22 = (bf16[544,256]{1,0:T(8,128)(2,1)S(1)}, bf16[544,256]{1,0:T(8,128)(2,1)S(1)}, u32[]{:S(2)}, u32[]{:S(2)}) collective-permute-start(bf16[544,256]{1,0:T(8,128)(2,1)S(1)} %get-tuple-element.97), channel_id=1, source_target_pairs={{0,1},{1,2},{2,3},{3,0},{4,5},{5,6},{6,7},{7,4},{8,9},{9,10},{10,1... | collective-permute-start | bytes 835592 | tf_op jit(solution)/shard_map/ppermute | solution.py:476
  88.6 10.3 %collective-permute-start.25 = (bf16[544,256]{1,0:T(8,128)(2,1)S(1)}, bf16[544,256]{1,0:T(8,128)(2,1)S(1)}, u32[]{:S(2)}, u32[]{:S(2)}) collective-permute-start(bf16[544,256]{1,0:T(8,128)(2,1)S(1)} %get-tuple-element.100), channel_id=1, source_target_pairs={{0,3},{1,0},{2,1},{3,2},{4,7},{5,4},{6,5},{7,6},{8,11},{9,8},{10,9... | collective-permute-start | bytes 835592 | tf_op jit(solution)/shard_map/ppermute | solution.py:476
  102.7 10.7 %collective-permute-start.26 = (f32[48,256]{1,0:T(8,128)S(1)}, f32[48,256]{1,0:T(8,128)S(1)}, u32[]{:S(2)}, u32[]{:S(2)}) collective-permute-start(f32[48,256]{1,0:T(8,128)S(1)} %pad_maximum_fusion.1), channel_id=1, source_target_pairs={{32,0},{64,32},{96,64},{128,96},{160,128},{192,160},{224,192},{33,... | collective-permute-start | bytes 147464 | tf_op jit(solution)/shard_map/ppermute | solution.py:480
  113.4 6.3 %collective-permute-start.30 = (f32[16,256]{1,0:T(8,128)S(1)}, f32[16,256]{1,0:T(8,128)S(1)}, u32[]{:S(2)}, u32[]{:S(2)}) collective-permute-start(f32[16,256]{1,0:T(8,128)S(1)} %fusion.1), channel_id=1, source_target_pairs={{160,0},{192,32},{224,64},{161,1},{193,33},{225,65},{162,2},{194,3... | collective-permute-start | bytes 49160 | tf_op jit(solution)/shard_map/ppermute | solution.py:480
  (16 other events, 140.5 us)

commit v2 on v1

--- a/solution.py
+++ b/solution.py
@@ -528,16 +528,26 @@
     right_2 = shift(right_1, "z", 1, z_count)
     left_2 = shift(left_1, "z", -1, z_count)
     one = from_behind(own_end, "ctx", 1, ctx_count)
-    two = from_behind(own_end, "ctx", 2, ctx_count)
-    seven = from_behind(own_end, "ctx", 7, ctx_count)
-    triple = own_end + decay_1 * one + decay_2 * two
-    right_2, left_2, triple, up, down = together((right_2, left_2, triple, up, down))
+    pair = own_end + decay_1 * one
+    two = from_behind(pair, "ctx", 2, ctx_count)
+    right_2, left_2, two, up, down = together((right_2, left_2, two, up, down))
 
     right_3 = shift(right_2, "z", 1, z_count)
     left_3 = shift(left_2, "z", -1, z_count)
     rows = width // 2
     far_up = shift(up[rows:], "x", 1, x_count)
     far_down = shift(down[rows:], "x", -1, x_count)
+    near_shares = jnp.stack([down[:rows], up[:rows]])
+    other_near = lax.ppermute(near_shares, "ctx", [(i, i ^ 1) for i in range(ctx_count)])
+    four = from_behind(pair + decay_2 * two, "ctx", 4, ctx_count)
+    before = one + decay_1 * two + decay_2 * decay_1 * four
+    long_out, gated = local_call(
+        long_forward,
+        [slab, rounded],
+        [part_scratch, natural_scratch],
+        (q_short, k_short, v_short, ends, before, modal_poles, modal_residues),
+        tokens * width * 70,
+    )
     anywhere = pl.BlockSpec(memory_space=pl.ANY)
     in_vmem = pl.BlockSpec(memory_space=pltpu.VMEM)
     blocks = (right_2, right_1, grad_out, left_1, left_2)
@@ -552,21 +562,6 @@
             flops=tokens * width * width * 10, bytes_accessed=tokens * width * 24, transcendentals=0
         ),
     )(place, out_weight, *blocks)
-    near_shares, triple, kept = together((jnp.stack([down[:rows], up[:rows]]), triple, kept))
-    other_near = lax.ppermute(near_shares, "ctx", [(i, i ^ 1) for i in range(ctx_count)])
-    decay_3 = decay_2 * decay_1
-    before = (
-        from_behind(triple, "ctx", 1, ctx_count)
-        + decay_3 * from_behind(triple, "ctx", 4, ctx_count)
-        + decay_3 * decay_3 * seven
-    )
-    long_out, gated = local_call(
-        long_forward,
-        [slab, rounded],
-        [part_scratch, natural_scratch],
-        (q_short, k_short, v_short, ends, before, modal_poles, modal_residues),
-        tokens * width * 70,
-    )
     right_3, left_3, far_up, far_down, early, kept, gated, other_near = together(
         (right_3, left_3, far_up, far_down, early, kept, gated, other_near)
     )

time: 127 us -> 118 us (0.929)
  waiting for transfers between devices: 21.1 us -> 17.9 us
  local copies, waits for them, and re-layouts: 6.94 us -> 3.83 us
  starting transfers between devices: 61.9 us -> 59.8 us
    ppermute x11 -> x9, starting transfers between devices: 33.8 us -> 28.1 us  [from_behind(): lax.ppermute(block, axis, [(i - distance, i) for i in range(size) if 0 <=...]
    ppermute x18, waiting for transfers between devices: 16.6 us -> 13.3 us  [shift(): lax.ppermute(block, axis, [(i, (i + distance) % size) for i in range(size)])]
    unnamed x19, local copies, waits for them, and re-layouts: 5.35 us -> 2.24 us
    ppermute x1, starting transfers between devices: 0.09 us -> 2.05 us  [shards(): lax.ppermute(near_shares, 'ctx', [(i, i ^ 1) for i in range(ctx_count)])]
    ppermute x1, starting transfers between devices: 0.53 us -> 2.2 us  [shards(): lax.ppermute(far_share, 'ctx', [(i, i ^ 1) for i in range(ctx_count)])]
    ppermute x11 -> x9, waiting for transfers between devices: 4.56 us -> 4.56 us  [from_behind(): lax.ppermute(block, axis, [(i - distance, i) for i in range(size) if 0 <=...]
  transfers between devices with their start and end apart: 31 -> 29, of which waited for: 10 -> 9; matrix products, arithmetic and copies ran while one was open for 1% -> 1% of each run, Pallas kernels for 17% -> 20%
where the time goes in v2:
time: 118 us; the launch traced here: 116 us
  starting transfers between devices  59.8 us (51%)
  Pallas kernels  33.6 us (28%)
  waiting for transfers between devices  17.9 us (15%)
  local copies, waits for them, and re-layouts  3.83 us (3%)
    pallas_call x12, Pallas kernels, local_call(): pl.pallas_call(kernel, out_shape=outs, in_specs=[whole if o.ndim > 1 else...  30.7 us
    ppermute x9, starting transfers between devices, from_behind(): lax.ppermute(block, axis, [(i - distance, i) for i in range(size) if 0 <=...  28.1 us
    ppermute x18, starting transfers between devices, shift(): lax.ppermute(block, axis, [(i, (i + distance) % size) for i in range(size)])  27.4 us
    ppermute x18, waiting for transfers between devices, shift(): lax.ppermute(block, axis, [(i, (i + distance) % size) for i in range(size)])  13.3 us
    ppermute x9, waiting for transfers between devices, from_behind(): lax.ppermute(block, axis, [(i - distance, i) for i in range(size) if 0 <=...  4.56 us
  transfers between devices with their start and end apart: 29, of which 9 were waited for; matrix products, arithmetic and copies ran while one was open for 1% of the time, Pallas kernels for 20%

profile of v2, /device:TPU:1, one launch (start us, length us, event | category | flops | bytes accessed | tf_op | source)
XLA Modules:
  0.0 116.4 jit_solution(5252472232797870153)
XLA Ops:
  0.7 2.5 %collective-permute-start = (bf16[1024,256]{1,0:T(8,128)(2,1)}, bf16[1024,256]{1,0:T(8,128)(2,1)S(1)}, u32[]{:S(2)}, u32[]{:S(2)}) collective-permute-start(bf16[1024,256]{1,0:T(8,128)(2,1)} %refs_2_.1), channel_id=1, source_target_pairs={{0,4},{4,8},{8,12},{12,16},{16,20},{20,24},{24,28},{28,0},{1,5},{5... | collective-permute-start | bytes 1572872 | tf_op jit(solution)/shard_map/ppermute | solution.py:476
  3.2 4.0 %collective-permute-start.2 = (bf16[1024,256]{1,0:T(8,128)(2,1)}, bf16[1024,256]{1,0:T(8,128)(2,1)S(1)}, u32[]{:S(2)}, u32[]{:S(2)}) collective-permute-start(bf16[1024,256]{1,0:T(8,128)(2,1)} %refs_2_.1), channel_id=1, source_target_pairs={{0,28},{4,0},{8,4},{12,8},{16,12},{20,16},{24,20},{28,24},{1,29},{... | collective-permute-start | bytes 1572872 | tf_op jit(solution)/shard_map/ppermute | solution.py:476
  8.6 4.0 %collective-permute-start.4 = (bf16[3,16,256]{2,1,0:T(8,128)(2,1)S(1)}, bf16[3,16,256]{2,1,0:T(8,128)(2,1)S(1)}, u32[]{:S(2)}, u32[]{:S(2)}) collective-permute-start(bf16[3,16,256]{2,1,0:T(8,128)(2,1)S(1)} %pad_maximum_fusion.2), channel_id=1, source_target_pairs={{0,32},{32,64},{64,96},{96,128},{128,160},{160,192},{192,224},{1,3... | collective-permute-start | bytes 73736 | tf_op jit(solution)/shard_map/ppermute | solution.py:480
  13.6 2.2 %copy-done = bf16[256,8192]{1,0:T(8,128)(2,1)S(1)} copy-done((bf16[256,8192]{1,0:T(8,128)(2,1)S(1)}, bf16[256,8192]{1,0:T(8,128)(2,1)}, u32[]{:S(2)}) %copy-start) | copy-done | bytes 4194328
  19.8 2.7 %collective-permute-start.3 = (bf16[1024,256]{1,0:T(8,128)(2,1)S(1)}, bf16[1024,256]{1,0:T(8,128)(2,1)S(1)}, u32[]{:S(2)}, u32[]{:S(2)}) collective-permute-start(bf16[1024,256]{1,0:T(8,128)(2,1)S(1)} %collective-permute-done.2.refs_3_), channel_id=1, source_target_pairs={{0,28},{4,0},{8,4},{12,8},{16,12},{20,16},{24,20},{28,24},{1,29},{... | collective-permute-start | bytes 1572872 | tf_op jit(solution)/shard_map/ppermute | solution.py:476
  22.5 4.7 %shard_map.111 = (f32[1024,256]{1,0:T(8,128)S(1)}, f32[1024,256]{1,0:T(8,128)S(1)}, f32[1024,256]{1,0:T(8,128)S(1)}, f32[16,8,256]{2,1,0:T(8,128)S(1)}, f32[16,256]{1,0:T(8,128)S(1)}, /*index=5*/f32[2,8,256]{2,1,0:T(8,128)S(1)}) custom-call(bf16[1024,256]{1,0:T(8,128)(2,1)S(1)} %copy-done.3, bf16[1024,256]{1,0:T(8,128)(2,1)S(1)} %copy-done.4, ...), custom_call_target="tpu_custom_call" | custom-call | flops 20971520 | bytes 327680 | tf_op jit(solution)/shard_map/pallas_call | solution.py:460
  27.2 5.3 %collective-permute-start.5 = (f32[16,256]{1,0:T(8,128)S(1)}, f32[16,256]{1,0:T(8,128)S(1)}, u32[]{:S(2)}, u32[]{:S(2)}) collective-permute-start(f32[16,256]{1,0:T(8,128)S(1)} %get-tuple-element.61), channel_id=1, source_target_pairs={{0,32},{32,64},{64,96},{96,128},{128,160},{160,192},{192,224},{1,3... | collective-permute-start | bytes 49160 | tf_op jit(solution)/shard_map/ppermute | solution.py:480
  33.5 3.2 %collective-permute-start.6 = (f32[16,256]{1,0:T(8,128)S(1)}, f32[16,256]{1,0:T(8,128)S(1)}, u32[]{:S(2)}, u32[]{:S(2)}) collective-permute-start(f32[16,256]{1,0:T(8,128)S(1)} %multiply_add_fusion.2), channel_id=1, source_target_pairs={{0,64},{32,96},{64,128},{96,160},{128,192},{160,224},{1,65},{33,97... | collective-permute-start | bytes 49160 | tf_op jit(solution)/shard_map/ppermute | solution.py:480
  39.8 2.7 %collective-permute-start.10 = (bf16[1024,256]{1,0:T(8,128)(2,1)S(1)}, bf16[1024,256]{1,0:T(8,128)(2,1)S(1)}, u32[]{:S(2)}, u32[]{:S(2)}) collective-permute-start(bf16[1024,256]{1,0:T(8,128)(2,1)S(1)} %collective-permute-done.3.refs_4_), channel_id=1, source_target_pairs={{0,28},{4,0},{8,4},{12,8},{16,12},{20,16},{24,20},{28,24},{1,29},{... | collective-permute-start | bytes 1572872 | tf_op jit(solution)/shard_map/ppermute | solution.py:476
  42.5 5.5 %collective-permute-start.13 = (f32[16,256]{1,0:T(8,128)S(1)}, f32[16,256]{1,0:T(8,128)S(1)}, u32[]{:S(2)}, u32[]{:S(2)}) collective-permute-start(f32[16,256]{1,0:T(8,128)S(1)} %fusion), channel_id=1, source_target_pairs={{0,128},{32,160},{64,192},{96,224},{1,129},{33,161},{65,193},{97,2... | collective-permute-start | bytes 49160 | tf_op jit(solution)/shard_map/ppermute | solution.py:480
  51.4 3.9 %shard_map.114 = (f32[1024,256]{1,0:T(8,128)S(1)}, bf16[1024,256]{1,0:T(8,128)(2,1)}) custom-call(f32[1024,256]{1,0:T(8,128)S(1)} %get-tuple-element.71.qs_ref, f32[1024,256]{1,0:T(8,128)S(1)} %get-tuple-element.72.ks_ref, f32[1024,256]{1,0:T(8,128)S(1)} %get-tuple-element.73.vs_ref, f32[16,8,256]{2,1,0:T(8,128)S(1)} %get-tuple-element.74.ends_ref, ...), custom_call_target="tpu_custom_call" | custom-call | flops 18350080 | bytes 286720 | tf_op jit(solution)/shard_map/pallas_call | solution.py:460
  57.3 2.2 %collective-permute-start.17 = (bf16[128,2048]{1,0:T(8,128)(2,1)S(1)}, bf16[128,2048]{1,0:T(8,128)(2,1)S(1)}, u32[]{:S(2)}, u32[]{:S(2)}) collective-permute-start(bf16[128,2048]{1,0:T(8,128)(2,1)S(1)} %constant_dynamic-update-slice_fusion.refs_3_.share_ref), channel_id=1, source_target_pairs={{0,32},{32,0},{64,96},{96,64},{128,160},{160,128},{192,224},{224,1... | collective-permute-start | bytes 1572872 | tf_op jit(solution)/shard_map/ppermute | solution.py:572
  59.9 2.7 %collective-permute-start.16 = (bf16[512,256]{1,0:T(8,128)(2,1)S(1)}, bf16[512,256]{1,0:T(8,128)(2,1)S(1)}, u32[]{:S(2)}, u32[]{:S(2)}) collective-permute-start(bf16[512,256]{1,0:T(8,128)(2,1)S(1)} %slice.41), channel_id=1, source_target_pairs={{0,28},{4,0},{8,4},{12,8},{16,12},{20,16},{24,20},{28,24},{1,29},{... | collective-permute-start | bytes 786440 | tf_op jit(solution)/shard_map/ppermute | solution.py:476
  64.3 4.7 %collective-permute-done.15.refs_3_.middle_up_ref.refs_2_ = bf16[512,256]{1,0:T(8,128)(2,1)S(1)} collective-permute-done((bf16[512,256]{1,0:T(8,128)(2,1)S(1)}, bf16[512,256]{1,0:T(8,128)(2,1)S(1)}, u32[]{:S(2)}, u32[]{:S(2)}) %collective-permute-start.15) | collective-permute-done | bytes 262176 | tf_op jit(solution)/shard_map/ppermute | solution.py:476
  70.3 2.7 %collective-permute-start.19 = (bf16[544,256]{1,0:T(8,128)(2,1)S(1)}, bf16[544,256]{1,0:T(8,128)(2,1)S(1)}, u32[]{:S(2)}, u32[]{:S(2)}) collective-permute-start(bf16[544,256]{1,0:T(8,128)(2,1)S(1)} %get-tuple-element.90), channel_id=1, source_target_pairs={{0,3},{1,0},{2,1},{3,2},{4,7},{5,4},{6,5},{7,6},{8,11},{9,8},{10,9... | collective-permute-start | bytes 835592 | tf_op jit(solution)/shard_map/ppermute | solution.py:476
  73.0 3.0 %shard_map.116 = (f32[1024,256]{1,0:T(8,128)S(1)}, f32[1024,256]{1,0:T(8,128)S(1)}) custom-call(s32[4]{0:T(128)S(1)} %pad_add_fusion.place_ref, bf16[5,1024,256]{2,1,0:T(8,128)(2,1)S(1)} %get-tuple-element.78.refs_0_, bf16[1024,256]{1,0:T(8,128)(2,1)S(1)} %collective-permute-done.10.refs_1_.refs_0_, ...), custom_call_target="tpu_custom_call" | custom-call | flops 2147483648 | bytes 33554432 | tf_op jit(solution)/shard_map/pallas_call | solution.py:460
  76.5 2.7 %collective-permute-start.22 = (bf16[544,256]{1,0:T(8,128)(2,1)S(1)}, bf16[544,256]{1,0:T(8,128)(2,1)S(1)}, u32[]{:S(2)}, u32[]{:S(2)}) collective-permute-start(bf16[544,256]{1,0:T(8,128)(2,1)S(1)} %get-tuple-element.93), channel_id=1, source_target_pairs={{0,3},{1,0},{2,1},{3,2},{4,7},{5,4},{6,5},{7,6},{8,11},{9,8},{10,9... | collective-permute-start | bytes 835592 | tf_op jit(solution)/shard_map/ppermute | solution.py:476
  80.1 2.7 %collective-permute-start.23 = (bf16[544,256]{1,0:T(8,128)(2,1)S(1)}, bf16[544,256]{1,0:T(8,128)(2,1)S(1)}, u32[]{:S(2)}, u32[]{:S(2)}) collective-permute-start(bf16[544,256]{1,0:T(8,128)(2,1)S(1)} %get-tuple-element.94), channel_id=1, source_target_pairs={{0,3},{1,0},{2,1},{3,2},{4,7},{5,4},{6,5},{7,6},{8,11},{9,8},{10,9... | collective-permute-start | bytes 835592 | tf_op jit(solution)/shard_map/ppermute | solution.py:476
  84.5 6.0 %collective-permute-done.20.one_up_ref = bf16[544,256]{1,0:T(8,128)(2,1)S(1)} collective-permute-done((bf16[544,256]{1,0:T(8,128)(2,1)S(1)}, bf16[544,256]{1,0:T(8,128)(2,1)S(1)}, u32[]{:S(2)}, u32[]{:S(2)}) %collective-permute-start.20) | collective-permute-done | bytes 278560 | tf_op jit(solution)/shard_map/ppermute | solution.py:476
  90.5 3.7 %shard_map.121 = (f32[1024,256]{1,0:T(8,128)S(1)}, f32[16,8,256]{2,1,0:T(8,128)S(1)}, f32[16,256]{1,0:T(8,128)S(1)}, f32[32,256]{1,0:T(8,128)S(1)}) custom-call(f32[1024,256]{1,0:T(8,128)S(1)} %shard_map.120.kept_ref, bf16[544,256]{1,0:T(8,128)(2,1)S(1)} %collective-permute-done.20.one_up_ref, bf16[544,256]{1,0:T(8,128)(2,1)S(1)} %collective-permute-done.21.one_down_ref, ...), custom_call_target="tpu_custom_call" | custom-call | flops 10485760 | bytes 163840 | tf_op jit(solution)/shard_map/pallas_call | solution.py:460
  94.2 4.2 %collective-permute-start.24 = (f32[48,256]{1,0:T(8,128)S(1)}, f32[48,256]{1,0:T(8,128)S(1)}, u32[]{:S(2)}, u32[]{:S(2)}) collective-permute-start(f32[48,256]{1,0:T(8,128)S(1)} %pad_maximum_fusion.1), channel_id=1, source_target_pairs={{32,0},{64,32},{96,64},{128,96},{160,128},{192,160},{224,192},{33,... | collective-permute-start | bytes 147464 | tf_op jit(solution)/shard_map/ppermute | solution.py:480
  101.6 2.6 %shard_map.122.local_ref = f32[1024,256]{1,0:T(8,128)S(1)} custom-call(f32[1024,256]{1,0:T(8,128)S(1)} %get-tuple-element.104.mixed_ref, f32[1024,256]{1,0:T(8,128)S(1)} %get-tuple-element.71.qs_ref, f32[16,256]{1,0:T(8,128)S(1)} %copy-done.2, f32[16,256]{1,0:T(8,128)S(1)} %copy-done.8), custom_call_target="tpu_custom_call" | custom-call | flops 16777216 | bytes 262144 | tf_op jit(solution)/shard_map/pallas_call | solution.py:460
  107.5 2.2 %shard_map.123 = bf16[1024,256]{1,0:T(8,128)(2,1)} custom-call(f32[1024,256]{1,0:T(8,128)S(1)} %get-tuple-element.104.mixed_ref, f32[1024,256]{1,0:T(8,128)S(1)} %get-tuple-element.101.long_ref, f32[32,256]{1,0:T(8,128)S(1)} %slice.43.next_ref, f32[3,7,256]{2,1,0:T(8,128)S(1)} %copy-done.7), custom_call_target="tpu_custom_call" | custom-call | flops 5242880 | bytes 81920 | tf_op jit(solution)/shard_map/pallas_call | solution.py:460
  111.1 5.2 %shard_map.124 = (bf16[1024,256]{1,0:T(8,128)(2,1)}, bf16[1024,256]{1,0:T(8,128)(2,1)}) custom-call(f32[1024,256]{1,0:T(8,128)S(1)} %shard_map.122.local_ref, f32[1024,256]{1,0:T(8,128)S(1)} %get-tuple-element.72.ks_ref, f32[1024,256]{1,0:T(8,128)S(1)} %get-tuple-element.73.vs_ref, f32[16,8,256]{2,1,0:T(8,128)S(1)} %get-tuple-element.110.starts_ref, ...), custom_call_target="tpu_custom_call" | custom-call | flops 20971520 | bytes 327680 | tf_op jit(solution)/shard_map/pallas_call | solution.py:460
  (86 shorter events, 30.1 us)
Async XLA Ops:
  0.7 19.2 %collective-permute-start = (bf16[1024,256]{1,0:T(8,128)(2,1)}, bf16[1024,256]{1,0:T(8,128)(2,1)S(1)}, u32[]{:S(2)}, u32[]{:S(2)}) collective-permute-start(bf16[1024,256]{1,0:T(8,128)(2,1)} %refs_2_.1), channel_id=1, source_target_pairs={{0,4},{4,8},{8,12},{12,16},{16,20},{20,24},{24,28},{28,0},{1,5},{5... | collective-permute-start | bytes 1572872 | tf_op jit(solution)/shard_map/ppermute | solution.py:476
  3.2 16.6 %collective-permute-start.2 = (bf16[1024,256]{1,0:T(8,128)(2,1)}, bf16[1024,256]{1,0:T(8,128)(2,1)S(1)}, u32[]{:S(2)}, u32[]{:S(2)}) collective-permute-start(bf16[1024,256]{1,0:T(8,128)(2,1)} %refs_2_.1), channel_id=1, source_target_pairs={{0,28},{4,0},{8,4},{12,8},{16,12},{20,16},{24,20},{28,24},{1,29},{... | collective-permute-start | bytes 1572872 | tf_op jit(solution)/shard_map/ppermute | solution.py:476
  17.0 20.5 %collective-permute-start.7 = (bf16[192,2048]{1,0:T(8,128)(2,1)S(1)}, bf16[192,2048]{1,0:T(8,128)(2,1)S(1)}, u32[]{:S(2)}, u32[]{:S(2)}) collective-permute-start(bf16[192,2048]{1,0:T(8,128)(2,1)S(1)} %get-tuple-element.63), channel_id=1, source_target_pairs={{0,1},{1,2},{2,3},{3,0},{4,5},{5,6},{6,7},{7,4},{8,9},{9,10},{10,1... | collective-permute-start | bytes 2359304 | tf_op jit(solution)/shard_map/ppermute | solution.py:476
  18.3 19.2 %collective-permute-start.8 = (bf16[192,2048]{1,0:T(8,128)(2,1)S(1)}, bf16[192,2048]{1,0:T(8,128)(2,1)S(1)}, u32[]{:S(2)}, u32[]{:S(2)}) collective-permute-start(bf16[192,2048]{1,0:T(8,128)(2,1)S(1)} %get-tuple-element.64), channel_id=1, source_target_pairs={{0,3},{1,0},{2,1},{3,2},{4,7},{5,4},{6,5},{7,6},{8,11},{9,8},{10,9... | collective-permute-start | bytes 2359304 | tf_op jit(solution)/shard_map/ppermute | solution.py:476
  19.8 17.7 %collective-permute-start.1 = (bf16[1024,256]{1,0:T(8,128)(2,1)S(1)}, bf16[1024,256]{1,0:T(8,128)(2,1)S(1)}, u32[]{:S(2)}, u32[]{:S(2)}) collective-permute-start(bf16[1024,256]{1,0:T(8,128)(2,1)S(1)} %collective-permute-done.refs_1_), channel_id=1, source_target_pairs={{0,4},{4,8},{8,12},{12,16},{16,20},{20,24},{24,28},{28,0},{1,5},{5... | collective-permute-start | bytes 1572872 | tf_op jit(solution)/shard_map/ppermute | solution.py:476
  19.8 17.7 %collective-permute-start.3 = (bf16[1024,256]{1,0:T(8,128)(2,1)S(1)}, bf16[1024,256]{1,0:T(8,128)(2,1)S(1)}, u32[]{:S(2)}, u32[]{:S(2)}) collective-permute-start(bf16[1024,256]{1,0:T(8,128)(2,1)S(1)} %collective-permute-done.2.refs_3_), channel_id=1, source_target_pairs={{0,28},{4,0},{8,4},{12,8},{16,12},{20,16},{24,20},{28,24},{1,29},{... | collective-permute-start | bytes 1572872 | tf_op jit(solution)/shard_map/ppermute | solution.py:476
  27.2 6.2 %collective-permute-start.5 = (f32[16,256]{1,0:T(8,128)S(1)}, f32[16,256]{1,0:T(8,128)S(1)}, u32[]{:S(2)}, u32[]{:S(2)}) collective-permute-start(f32[16,256]{1,0:T(8,128)S(1)} %get-tuple-element.61), channel_id=1, source_target_pairs={{0,32},{32,64},{64,96},{96,128},{128,160},{160,192},{192,224},{1,3... | collective-permute-start | bytes 49160 | tf_op jit(solution)/shard_map/ppermute | solution.py:480
  37.7 19.5 %collective-permute-start.14 = (bf16[2,128,2048]{2,1,0:T(8,128)(2,1)S(1)}, bf16[2,128,2048]{2,1,0:T(8,128)(2,1)S(1)}, u32[]{:S(2)}, u32[]{:S(2)}) collective-permute-start(bf16[2,128,2048]{2,1,0:T(8,128)(2,1)S(1)} %pad_maximum_fusion.refs_5_), channel_id=1, source_target_pairs={{0,32},{32,0},{64,96},{96,64},{128,160},{160,128},{192,224},{224,1... | collective-permute-start | bytes 3145736 | tf_op jit(solution)/shard_map/ppermute | solution.py:541
  39.8 17.5 %collective-permute-start.9 = (bf16[1024,256]{1,0:T(8,128)(2,1)S(1)}, bf16[1024,256]{1,0:T(8,128)(2,1)S(1)}, u32[]{:S(2)}, u32[]{:S(2)}) collective-permute-start(bf16[1024,256]{1,0:T(8,128)(2,1)S(1)} %collective-permute-done.1.refs_0_), channel_id=1, source_target_pairs={{0,4},{4,8},{8,12},{12,16},{16,20},{20,24},{24,28},{28,0},{1,5},{5... | collective-permute-start | bytes 1572872 | tf_op jit(solution)/shard_map/ppermute | solution.py:476
  39.8 17.5 %collective-permute-start.10 = (bf16[1024,256]{1,0:T(8,128)(2,1)S(1)}, bf16[1024,256]{1,0:T(8,128)(2,1)S(1)}, u32[]{:S(2)}, u32[]{:S(2)}) collective-permute-start(bf16[1024,256]{1,0:T(8,128)(2,1)S(1)} %collective-permute-done.3.refs_4_), channel_id=1, source_target_pairs={{0,28},{4,0},{8,4},{12,8},{16,12},{20,16},{24,20},{28,24},{1,29},{... | collective-permute-start | bytes 1572872 | tf_op jit(solution)/shard_map/ppermute | solution.py:476
  42.5 6.9 %collective-permute-start.13 = (f32[16,256]{1,0:T(8,128)S(1)}, f32[16,256]{1,0:T(8,128)S(1)}, u32[]{:S(2)}, u32[]{:S(2)}) collective-permute-start(f32[16,256]{1,0:T(8,128)S(1)} %fusion), channel_id=1, source_target_pairs={{0,128},{32,160},{64,192},{96,224},{1,129},{33,161},{65,193},{97,2... | collective-permute-start | bytes 49160 | tf_op jit(solution)/shard_map/ppermute | solution.py:480
  48.1 7.1 %collective-permute-start.12 = (bf16[64,2048]{1,0:T(8,128)(2,1)S(1)}, bf16[64,2048]{1,0:T(8,128)(2,1)S(1)}, u32[]{:S(2)}, u32[]{:S(2)}) collective-permute-start(bf16[64,2048]{1,0:T(8,128)(2,1)S(1)} %slice.37), channel_id=1, source_target_pairs={{0,3},{1,0},{2,1},{3,2},{4,7},{5,4},{6,5},{7,6},{8,11},{9,8},{10,9... | collective-permute-start | bytes 786440 | tf_op jit(solution)/shard_map/ppermute | solution.py:476
  49.5 7.8 %collective-permute-start.11 = (bf16[64,2048]{1,0:T(8,128)(2,1)S(1)}, bf16[64,2048]{1,0:T(8,128)(2,1)S(1)}, u32[]{:S(2)}, u32[]{:S(2)}) collective-permute-start(bf16[64,2048]{1,0:T(8,128)(2,1)S(1)} %slice.36), channel_id=1, source_target_pairs={{0,1},{1,2},{2,3},{3,0},{4,5},{5,6},{6,7},{7,4},{8,9},{9,10},{10,1... | collective-permute-start | bytes 786440 | tf_op jit(solution)/shard_map/ppermute | solution.py:476
  59.6 9.4 %collective-permute-start.15 = (bf16[512,256]{1,0:T(8,128)(2,1)S(1)}, bf16[512,256]{1,0:T(8,128)(2,1)S(1)}, u32[]{:S(2)}, u32[]{:S(2)}) collective-permute-start(bf16[512,256]{1,0:T(8,128)(2,1)S(1)} %slice.40), channel_id=1, source_target_pairs={{0,4},{4,8},{8,12},{12,16},{16,20},{20,24},{24,28},{28,0},{1,5},{5... | collective-permute-start | bytes 786440 | tf_op jit(solution)/shard_map/ppermute | solution.py:476
  59.9 9.1 %collective-permute-start.16 = (bf16[512,256]{1,0:T(8,128)(2,1)S(1)}, bf16[512,256]{1,0:T(8,128)(2,1)S(1)}, u32[]{:S(2)}, u32[]{:S(2)}) collective-permute-start(bf16[512,256]{1,0:T(8,128)(2,1)S(1)} %slice.41), channel_id=1, source_target_pairs={{0,28},{4,0},{8,4},{12,8},{16,12},{20,16},{24,20},{28,24},{1,29},{... | collective-permute-start | bytes 786440 | tf_op jit(solution)/shard_map/ppermute | solution.py:476
  70.3 8.9 %collective-permute-start.18 = (bf16[544,256]{1,0:T(8,128)(2,1)S(1)}, bf16[544,256]{1,0:T(8,128)(2,1)S(1)}, u32[]{:S(2)}, u32[]{:S(2)}) collective-permute-start(bf16[544,256]{1,0:T(8,128)(2,1)S(1)} %get-tuple-element.89), channel_id=1, source_target_pairs={{0,1},{1,2},{2,3},{3,0},{4,5},{5,6},{6,7},{7,4},{8,9},{9,10},{10,1... | collective-permute-start | bytes 835592 | tf_op jit(solution)/shard_map/ppermute | solution.py:476
  70.3 8.8 %collective-permute-start.19 = (bf16[544,256]{1,0:T(8,128)(2,1)S(1)}, bf16[544,256]{1,0:T(8,128)(2,1)S(1)}, u32[]{:S(2)}, u32[]{:S(2)}) collective-permute-start(bf16[544,256]{1,0:T(8,128)(2,1)S(1)} %get-tuple-element.90), channel_id=1, source_target_pairs={{0,3},{1,0},{2,1},{3,2},{4,7},{5,4},{6,5},{7,6},{8,11},{9,8},{10,9... | collective-permute-start | bytes 835592 | tf_op jit(solution)/shard_map/ppermute | solution.py:476
  76.4 8.1 %collective-permute-start.21 = (bf16[544,256]{1,0:T(8,128)(2,1)S(1)}, bf16[544,256]{1,0:T(8,128)(2,1)S(1)}, u32[]{:S(2)}, u32[]{:S(2)}) collective-permute-start(bf16[544,256]{1,0:T(8,128)(2,1)S(1)} %get-tuple-element.92), channel_id=1, source_target_pairs={{0,1},{1,2},{2,3},{3,0},{4,5},{5,6},{6,7},{7,4},{8,9},{9,10},{10,1... | collective-permute-start | bytes 835592 | tf_op jit(solution)/shard_map/ppermute | solution.py:476
  76.5 8.0 %collective-permute-start.22 = (bf16[544,256]{1,0:T(8,128)(2,1)S(1)}, bf16[544,256]{1,0:T(8,128)(2,1)S(1)}, u32[]{:S(2)}, u32[]{:S(2)}) collective-permute-start(bf16[544,256]{1,0:T(8,128)(2,1)S(1)} %get-tuple-element.93), channel_id=1, source_target_pairs={{0,3},{1,0},{2,1},{3,2},{4,7},{5,4},{6,5},{7,6},{8,11},{9,8},{10,9... | collective-permute-start | bytes 835592 | tf_op jit(solution)/shard_map/ppermute | solution.py:476
  80.0 10.5 %collective-permute-start.20 = (bf16[544,256]{1,0:T(8,128)(2,1)S(1)}, bf16[544,256]{1,0:T(8,128)(2,1)S(1)}, u32[]{:S(2)}, u32[]{:S(2)}) collective-permute-start(bf16[544,256]{1,0:T(8,128)(2,1)S(1)} %get-tuple-element.91), channel_id=1, source_target_pairs={{0,1},{1,2},{2,3},{3,0},{4,5},{5,6},{6,7},{7,4},{8,9},{9,10},{10,1... | collective-permute-start | bytes 835592 | tf_op jit(solution)/shard_map/ppermute | solution.py:476
  80.1 10.4 %collective-permute-start.23 = (bf16[544,256]{1,0:T(8,128)(2,1)S(1)}, bf16[544,256]{1,0:T(8,128)(2,1)S(1)}, u32[]{:S(2)}, u32[]{:S(2)}) collective-permute-start(bf16[544,256]{1,0:T(8,128)(2,1)S(1)} %get-tuple-element.94), channel_id=1, source_target_pairs={{0,3},{1,0},{2,1},{3,2},{4,7},{5,4},{6,5},{7,6},{8,11},{9,8},{10,9... | collective-permute-start | bytes 835592 | tf_op jit(solution)/shard_map/ppermute | solution.py:476
  94.2 10.6 %collective-permute-start.24 = (f32[48,256]{1,0:T(8,128)S(1)}, f32[48,256]{1,0:T(8,128)S(1)}, u32[]{:S(2)}, u32[]{:S(2)}) collective-permute-start(f32[48,256]{1,0:T(8,128)S(1)} %pad_maximum_fusion.1), channel_id=1, source_target_pairs={{32,0},{64,32},{96,64},{128,96},{160,128},{192,160},{224,192},{33,... | collective-permute-start | bytes 147464 | tf_op jit(solution)/shard_map/ppermute | solution.py:480
  98.4 5.8 %collective-permute-start.26 = (f32[2,8,256]{2,1,0:T(8,128)S(1)}, f32[2,8,256]{2,1,0:T(8,128)S(1)}, u32[]{:S(2)}, u32[]{:S(2)}) collective-permute-start(f32[2,8,256]{2,1,0:T(8,128)S(1)} %get-tuple-element.105), channel_id=1, source_target_pairs={{32,0},{64,32},{96,64},{128,96},{160,128},{192,160},{224,192},{33,... | collective-permute-start | bytes 49160 | tf_op jit(solution)/shard_map/ppermute | solution.py:480
  104.8 6.3 %collective-permute-start.28 = (f32[16,256]{1,0:T(8,128)S(1)}, f32[16,256]{1,0:T(8,128)S(1)}, u32[]{:S(2)}, u32[]{:S(2)}) collective-permute-start(f32[16,256]{1,0:T(8,128)S(1)} %fusion.1), channel_id=1, source_target_pairs={{160,0},{192,32},{224,64},{161,1},{193,33},{225,65},{162,2},{194,3... | collective-permute-start | bytes 49160 | tf_op jit(solution)/shard_map/ppermute | solution.py:480
  (14 other events, 168.5 us)

commit v3 on v2

--- a/solution.py
+++ b/solution.py
@@ -607,12 +607,16 @@
     after_1, last_2 = local_call(
         send_joined, [half_code, half_code], [], (after, last, up, down), tokens * width * 32
     )
+    after_1, last_2, first_kv = together((after_1, last_2, first_kv))
     after_1 = shift(after_1, "x", 1, x_count)
     last_2 = shift(last_2, "x", -1, x_count)
+    next_kv = from_behind(first_kv, "ctx", -1, ctx_count)
     (kept,) = local_call(
         keep_finish, [slab], [], (place, out_weight, kept, *on_ring[1:]), product_cost // 2
     )
-    after_1, after_2, last_1, last_2, kept = together((after_1, after_2, last_1, last_2, kept))
+    after_1, after_2, last_1, last_2, kept, next_kv = together(
+        (after_1, after_2, last_1, last_2, kept, next_kv)
+    )
     mixed_steps, starts, own_start, rim = local_call(
         back_states,
         [slab, per_part, state, floats(modes + 2 * RIM, width)],
@@ -626,8 +630,7 @@
         back_local, [slab], [], (mixed_steps, q_short, modal_poles, modal_residues), tokens * width * 64
     )
     two = from_behind(own_start, "ctx", -2, ctx_count)
-    next_kv = from_behind(first_kv, "ctx", -1, ctx_count)
-    near, two, local, next_kv = together((near, two, local, next_kv))
+    near, two, local = together((near, two, local))
     rim_size = modes + 2 * RIM
     near_rim = near[:rim_size]
     triple = own_start + decay_1 * near[rim_size:] + decay_2 * two

time: 118 us -> 115 us (0.975); the launches traced: 116 us -> 115 us
  waiting for transfers between devices: 17.9 us -> 13.9 us
  starting transfers between devices: 59.8 us -> 62.2 us
    ppermute x18, waiting for transfers between devices: 13.3 us -> 8.1 us  [shift(): lax.ppermute(block, axis, [(i, (i + distance) % size) for i in range(size)])]
    ppermute x9, starting transfers between devices: 28.1 us -> 30.6 us  [from_behind(): lax.ppermute(block, axis, [(i - distance, i) for i in range(size) if 0 <=...]
    ppermute x9, waiting for transfers between devices: 4.56 us -> 5.82 us  [from_behind(): lax.ppermute(block, axis, [(i - distance, i) for i in range(size) if 0 <=...]
where the time goes in v3:
time: 115 us
  starting transfers between devices  62.2 us (54%)
  Pallas kernels  33.6 us (29%)
  waiting for transfers between devices  13.9 us (12%)
  local copies, waits for them, and re-layouts  3.83 us (3%)
    pallas_call x12, Pallas kernels, local_call(): pl.pallas_call(kernel, out_shape=outs, in_specs=[whole if o.ndim > 1 else...  30.7 us
    ppermute x9, starting transfers between devices, from_behind(): lax.ppermute(block, axis, [(i - distance, i) for i in range(size) if 0 <=...  30.6 us
    ppermute x18, starting transfers between devices, shift(): lax.ppermute(block, axis, [(i, (i + distance) % size) for i in range(size)])  27.4 us
    ppermute x18, waiting for transfers between devices, shift(): lax.ppermute(block, axis, [(i, (i + distance) % size) for i in range(size)])  8.1 us
    ppermute x9, waiting for transfers between devices, from_behind(): lax.ppermute(block, axis, [(i - distance, i) for i in range(size) if 0 <=...  5.82 us
  transfers between devices with their start and end apart: 29, of which 9 were waited for; matrix products, arithmetic and copies ran while one was open for 1% of the time, Pallas kernels for 20%

profile of v3, /device:TPU:1, one launch (start us, length us, event | category | flops | bytes accessed | tf_op | source)
XLA Modules:
  0.0 114.9 jit_solution(16356129773113235731)
XLA Ops:
  0.7 2.5 %collective-permute-start = (bf16[1024,256]{1,0:T(8,128)(2,1)}, bf16[1024,256]{1,0:T(8,128)(2,1)S(1)}, u32[]{:S(2)}, u32[]{:S(2)}) collective-permute-start(bf16[1024,256]{1,0:T(8,128)(2,1)} %refs_2_.1), channel_id=1, source_target_pairs={{0,4},{4,8},{8,12},{12,16},{16,20},{20,24},{24,28},{28,0},{1,5},{5... | collective-permute-start | bytes 1572872 | tf_op jit(solution)/shard_map/ppermute | solution.py:476
  3.2 4.0 %collective-permute-start.2 = (bf16[1024,256]{1,0:T(8,128)(2,1)}, bf16[1024,256]{1,0:T(8,128)(2,1)S(1)}, u32[]{:S(2)}, u32[]{:S(2)}) collective-permute-start(bf16[1024,256]{1,0:T(8,128)(2,1)} %refs_2_.1), channel_id=1, source_target_pairs={{0,28},{4,0},{8,4},{12,8},{16,12},{20,16},{24,20},{28,24},{1,29},{... | collective-permute-start | bytes 1572872 | tf_op jit(solution)/shard_map/ppermute | solution.py:476
  8.6 4.0 %collective-permute-start.4 = (bf16[3,16,256]{2,1,0:T(8,128)(2,1)S(1)}, bf16[3,16,256]{2,1,0:T(8,128)(2,1)S(1)}, u32[]{:S(2)}, u32[]{:S(2)}) collective-permute-start(bf16[3,16,256]{2,1,0:T(8,128)(2,1)S(1)} %pad_maximum_fusion.2), channel_id=1, source_target_pairs={{0,32},{32,64},{64,96},{96,128},{128,160},{160,192},{192,224},{1,3... | collective-permute-start | bytes 73736 | tf_op jit(solution)/shard_map/ppermute | solution.py:480
  13.6 2.2 %copy-done = bf16[256,8192]{1,0:T(8,128)(2,1)S(1)} copy-done((bf16[256,8192]{1,0:T(8,128)(2,1)S(1)}, bf16[256,8192]{1,0:T(8,128)(2,1)}, u32[]{:S(2)}) %copy-start) | copy-done | bytes 4194328
  19.8 2.7 %collective-permute-start.3 = (bf16[1024,256]{1,0:T(8,128)(2,1)S(1)}, bf16[1024,256]{1,0:T(8,128)(2,1)S(1)}, u32[]{:S(2)}, u32[]{:S(2)}) collective-permute-start(bf16[1024,256]{1,0:T(8,128)(2,1)S(1)} %collective-permute-done.2.refs_3_), channel_id=1, source_target_pairs={{0,28},{4,0},{8,4},{12,8},{16,12},{20,16},{24,20},{28,24},{1,29},{... | collective-permute-start | bytes 1572872 | tf_op jit(solution)/shard_map/ppermute | solution.py:476
  22.5 4.7 %shard_map.111 = (f32[1024,256]{1,0:T(8,128)S(1)}, f32[1024,256]{1,0:T(8,128)S(1)}, f32[1024,256]{1,0:T(8,128)S(1)}, f32[16,8,256]{2,1,0:T(8,128)S(1)}, f32[16,256]{1,0:T(8,128)S(1)}, /*index=5*/f32[2,8,256]{2,1,0:T(8,128)S(1)}) custom-call(bf16[1024,256]{1,0:T(8,128)(2,1)S(1)} %copy-done.3, bf16[1024,256]{1,0:T(8,128)(2,1)S(1)} %copy-done.4, ...), custom_call_target="tpu_custom_call" | custom-call | flops 20971520 | bytes 327680 | tf_op jit(solution)/shard_map/pallas_call | solution.py:460
  27.2 5.3 %collective-permute-start.5 = (f32[16,256]{1,0:T(8,128)S(1)}, f32[16,256]{1,0:T(8,128)S(1)}, u32[]{:S(2)}, u32[]{:S(2)}) collective-permute-start(f32[16,256]{1,0:T(8,128)S(1)} %get-tuple-element.64), channel_id=1, source_target_pairs={{0,32},{32,64},{64,96},{96,128},{128,160},{160,192},{192,224},{1,3... | collective-permute-start | bytes 49160 | tf_op jit(solution)/shard_map/ppermute | solution.py:480
  33.5 3.2 %collective-permute-start.6 = (f32[16,256]{1,0:T(8,128)S(1)}, f32[16,256]{1,0:T(8,128)S(1)}, u32[]{:S(2)}, u32[]{:S(2)}) collective-permute-start(f32[16,256]{1,0:T(8,128)S(1)} %multiply_add_fusion.2), channel_id=1, source_target_pairs={{0,64},{32,96},{64,128},{96,160},{128,192},{160,224},{1,65},{33,97... | collective-permute-start | bytes 49160 | tf_op jit(solution)/shard_map/ppermute | solution.py:480
  39.8 2.7 %collective-permute-start.10 = (bf16[1024,256]{1,0:T(8,128)(2,1)S(1)}, bf16[1024,256]{1,0:T(8,128)(2,1)S(1)}, u32[]{:S(2)}, u32[]{:S(2)}) collective-permute-start(bf16[1024,256]{1,0:T(8,128)(2,1)S(1)} %collective-permute-done.3.refs_4_), channel_id=1, source_target_pairs={{0,28},{4,0},{8,4},{12,8},{16,12},{20,16},{24,20},{28,24},{1,29},{... | collective-permute-start | bytes 1572872 | tf_op jit(solution)/shard_map/ppermute | solution.py:476
  42.5 5.5 %collective-permute-start.13 = (f32[16,256]{1,0:T(8,128)S(1)}, f32[16,256]{1,0:T(8,128)S(1)}, u32[]{:S(2)}, u32[]{:S(2)}) collective-permute-start(f32[16,256]{1,0:T(8,128)S(1)} %fusion), channel_id=1, source_target_pairs={{0,128},{32,160},{64,192},{96,224},{1,129},{33,161},{65,193},{97,2... | collective-permute-start | bytes 49160 | tf_op jit(solution)/shard_map/ppermute | solution.py:480
  51.4 3.9 %shard_map.114 = (f32[1024,256]{1,0:T(8,128)S(1)}, bf16[1024,256]{1,0:T(8,128)(2,1)}) custom-call(f32[1024,256]{1,0:T(8,128)S(1)} %get-tuple-element.74.qs_ref, f32[1024,256]{1,0:T(8,128)S(1)} %get-tuple-element.75.ks_ref, f32[1024,256]{1,0:T(8,128)S(1)} %get-tuple-element.76.vs_ref, f32[16,8,256]{2,1,0:T(8,128)S(1)} %get-tuple-element.77.ends_ref, ...), custom_call_target="tpu_custom_call" | custom-call | flops 18350080 | bytes 286720 | tf_op jit(solution)/shard_map/pallas_call | solution.py:460
  57.3 2.2 %collective-permute-start.17 = (bf16[128,2048]{1,0:T(8,128)(2,1)S(1)}, bf16[128,2048]{1,0:T(8,128)(2,1)S(1)}, u32[]{:S(2)}, u32[]{:S(2)}) collective-permute-start(bf16[128,2048]{1,0:T(8,128)(2,1)S(1)} %constant_dynamic-update-slice_fusion.refs_3_.share_ref), channel_id=1, source_target_pairs={{0,32},{32,0},{64,96},{96,64},{128,160},{160,128},{192,224},{224,1... | collective-permute-start | bytes 1572872 | tf_op jit(solution)/shard_map/ppermute | solution.py:572
  59.9 2.7 %collective-permute-start.16 = (bf16[512,256]{1,0:T(8,128)(2,1)S(1)}, bf16[512,256]{1,0:T(8,128)(2,1)S(1)}, u32[]{:S(2)}, u32[]{:S(2)}) collective-permute-start(bf16[512,256]{1,0:T(8,128)(2,1)S(1)} %slice.41), channel_id=1, source_target_pairs={{0,28},{4,0},{8,4},{12,8},{16,12},{20,16},{24,20},{28,24},{1,29},{... | collective-permute-start | bytes 786440 | tf_op jit(solution)/shard_map/ppermute | solution.py:476
  64.3 4.7 %collective-permute-done.15.refs_3_.middle_up_ref.refs_2_ = bf16[512,256]{1,0:T(8,128)(2,1)S(1)} collective-permute-done((bf16[512,256]{1,0:T(8,128)(2,1)S(1)}, bf16[512,256]{1,0:T(8,128)(2,1)S(1)}, u32[]{:S(2)}, u32[]{:S(2)}) %collective-permute-start.15) | collective-permute-done | bytes 262176 | tf_op jit(solution)/shard_map/ppermute | solution.py:476
  70.3 2.7 %collective-permute-start.19 = (bf16[544,256]{1,0:T(8,128)(2,1)S(1)}, bf16[544,256]{1,0:T(8,128)(2,1)S(1)}, u32[]{:S(2)}, u32[]{:S(2)}) collective-permute-start(bf16[544,256]{1,0:T(8,128)(2,1)S(1)} %get-tuple-element.93), channel_id=1, source_target_pairs={{0,3},{1,0},{2,1},{3,2},{4,7},{5,4},{6,5},{7,6},{8,11},{9,8},{10,9... | collective-permute-start | bytes 835592 | tf_op jit(solution)/shard_map/ppermute | solution.py:476
  73.0 3.0 %shard_map.116 = (f32[1024,256]{1,0:T(8,128)S(1)}, f32[1024,256]{1,0:T(8,128)S(1)}) custom-call(s32[4]{0:T(128)S(1)} %pad_add_fusion.place_ref, bf16[5,1024,256]{2,1,0:T(8,128)(2,1)S(1)} %get-tuple-element.81.refs_0_, bf16[1024,256]{1,0:T(8,128)(2,1)S(1)} %collective-permute-done.10.refs_1_.refs_0_, ...), custom_call_target="tpu_custom_call" | custom-call | flops 2147483648 | bytes 33554432 | tf_op jit(solution)/shard_map/pallas_call | solution.py:460
  76.5 2.7 %collective-permute-start.22 = (bf16[544,256]{1,0:T(8,128)(2,1)S(1)}, bf16[544,256]{1,0:T(8,128)(2,1)S(1)}, u32[]{:S(2)}, u32[]{:S(2)}) collective-permute-start(bf16[544,256]{1,0:T(8,128)(2,1)S(1)} %get-tuple-element.99), channel_id=1, source_target_pairs={{0,3},{1,0},{2,1},{3,2},{4,7},{5,4},{6,5},{7,6},{8,11},{9,8},{10,9... | collective-permute-start | bytes 835592 | tf_op jit(solution)/shard_map/ppermute | solution.py:476
  80.1 2.7 %collective-permute-start.23 = (bf16[544,256]{1,0:T(8,128)(2,1)S(1)}, bf16[544,256]{1,0:T(8,128)(2,1)S(1)}, u32[]{:S(2)}, u32[]{:S(2)}) collective-permute-start(bf16[544,256]{1,0:T(8,128)(2,1)S(1)} %get-tuple-element.100), channel_id=1, source_target_pairs={{0,3},{1,0},{2,1},{3,2},{4,7},{5,4},{6,5},{7,6},{8,11},{9,8},{10,9... | collective-permute-start | bytes 835592 | tf_op jit(solution)/shard_map/ppermute | solution.py:476
  82.8 4.4 %collective-permute-start.24 = (f32[2,8,256]{2,1,0:T(8,128)S(1)}, f32[2,8,256]{2,1,0:T(8,128)S(1)}, u32[]{:S(2)}, u32[]{:S(2)}) collective-permute-start(f32[2,8,256]{2,1,0:T(8,128)S(1)} %get-tuple-element.102), channel_id=1, source_target_pairs={{32,0},{64,32},{96,64},{128,96},{160,128},{192,160},{224,192},{33,... | collective-permute-start | bytes 49160 | tf_op jit(solution)/shard_map/ppermute | solution.py:480
  90.5 3.7 %shard_map.121 = (f32[1024,256]{1,0:T(8,128)S(1)}, f32[16,8,256]{2,1,0:T(8,128)S(1)}, f32[16,256]{1,0:T(8,128)S(1)}, f32[32,256]{1,0:T(8,128)S(1)}) custom-call(f32[1024,256]{1,0:T(8,128)S(1)} %shard_map.120.kept_ref, bf16[544,256]{1,0:T(8,128)(2,1)S(1)} %collective-permute-done.20.one_up_ref, bf16[544,256]{1,0:T(8,128)(2,1)S(1)} %collective-permute-done.21.one_down_ref, ...), custom_call_target="tpu_custom_call" | custom-call | flops 10485760 | bytes 163840 | tf_op jit(solution)/shard_map/pallas_call | solution.py:460
  94.2 4.2 %collective-permute-start.25 = (f32[48,256]{1,0:T(8,128)S(1)}, f32[48,256]{1,0:T(8,128)S(1)}, u32[]{:S(2)}, u32[]{:S(2)}) collective-permute-start(f32[48,256]{1,0:T(8,128)S(1)} %pad_maximum_fusion.1), channel_id=1, source_target_pairs={{32,0},{64,32},{96,64},{128,96},{160,128},{192,160},{224,192},{33,... | collective-permute-start | bytes 147464 | tf_op jit(solution)/shard_map/ppermute | solution.py:480
  99.7 2.6 %shard_map.122.local_ref = f32[1024,256]{1,0:T(8,128)S(1)} custom-call(f32[1024,256]{1,0:T(8,128)S(1)} %get-tuple-element.111.mixed_ref, f32[1024,256]{1,0:T(8,128)S(1)} %get-tuple-element.74.qs_ref, f32[16,256]{1,0:T(8,128)S(1)} %copy-done.2, f32[16,256]{1,0:T(8,128)S(1)} %copy-done.8), custom_call_target="tpu_custom_call" | custom-call | flops 16777216 | bytes 262144 | tf_op jit(solution)/shard_map/pallas_call | solution.py:460
  105.7 2.2 %shard_map.123 = bf16[1024,256]{1,0:T(8,128)(2,1)} custom-call(f32[1024,256]{1,0:T(8,128)S(1)} %get-tuple-element.111.mixed_ref, f32[1024,256]{1,0:T(8,128)S(1)} %get-tuple-element.108.long_ref, f32[32,256]{1,0:T(8,128)S(1)} %slice.43.next_ref, f32[3,7,256]{2,1,0:T(8,128)S(1)} %copy-done.7), custom_call_target="tpu_custom_call" | custom-call | flops 5242880 | bytes 81920 | tf_op jit(solution)/shard_map/pallas_call | solution.py:460
  109.7 5.2 %shard_map.124 = (bf16[1024,256]{1,0:T(8,128)(2,1)}, bf16[1024,256]{1,0:T(8,128)(2,1)}) custom-call(f32[1024,256]{1,0:T(8,128)S(1)} %shard_map.122.local_ref, f32[1024,256]{1,0:T(8,128)S(1)} %get-tuple-element.75.ks_ref, f32[1024,256]{1,0:T(8,128)S(1)} %get-tuple-element.76.vs_ref, f32[16,8,256]{2,1,0:T(8,128)S(1)} %get-tuple-element.116.starts_ref, ...), custom_call_target="tpu_custom_call" | custom-call | flops 20971520 | bytes 327680 | tf_op jit(solution)/shard_map/pallas_call | solution.py:460
  (86 shorter events, 30.2 us)
Async XLA Ops:
  0.7 19.2 %collective-permute-start = (bf16[1024,256]{1,0:T(8,128)(2,1)}, bf16[1024,256]{1,0:T(8,128)(2,1)S(1)}, u32[]{:S(2)}, u32[]{:S(2)}) collective-permute-start(bf16[1024,256]{1,0:T(8,128)(2,1)} %refs_2_.1), channel_id=1, source_target_pairs={{0,4},{4,8},{8,12},{12,16},{16,20},{20,24},{24,28},{28,0},{1,5},{5... | collective-permute-start | bytes 1572872 | tf_op jit(solution)/shard_map/ppermute | solution.py:476
  3.2 16.6 %collective-permute-start.2 = (bf16[1024,256]{1,0:T(8,128)(2,1)}, bf16[1024,256]{1,0:T(8,128)(2,1)S(1)}, u32[]{:S(2)}, u32[]{:S(2)}) collective-permute-start(bf16[1024,256]{1,0:T(8,128)(2,1)} %refs_2_.1), channel_id=1, source_target_pairs={{0,28},{4,0},{8,4},{12,8},{16,12},{20,16},{24,20},{28,24},{1,29},{... | collective-permute-start | bytes 1572872 | tf_op jit(solution)/shard_map/ppermute | solution.py:476
  17.0 20.5 %collective-permute-start.7 = (bf16[192,2048]{1,0:T(8,128)(2,1)S(1)}, bf16[192,2048]{1,0:T(8,128)(2,1)S(1)}, u32[]{:S(2)}, u32[]{:S(2)}) collective-permute-start(bf16[192,2048]{1,0:T(8,128)(2,1)S(1)} %get-tuple-element.66), channel_id=1, source_target_pairs={{0,1},{1,2},{2,3},{3,0},{4,5},{5,6},{6,7},{7,4},{8,9},{9,10},{10,1... | collective-permute-start | bytes 2359304 | tf_op jit(solution)/shard_map/ppermute | solution.py:476
  18.3 19.2 %collective-permute-start.8 = (bf16[192,2048]{1,0:T(8,128)(2,1)S(1)}, bf16[192,2048]{1,0:T(8,128)(2,1)S(1)}, u32[]{:S(2)}, u32[]{:S(2)}) collective-permute-start(bf16[192,2048]{1,0:T(8,128)(2,1)S(1)} %get-tuple-element.67), channel_id=1, source_target_pairs={{0,3},{1,0},{2,1},{3,2},{4,7},{5,4},{6,5},{7,6},{8,11},{9,8},{10,9... | collective-permute-start | bytes 2359304 | tf_op jit(solution)/shard_map/ppermute | solution.py:476
  19.8 17.7 %collective-permute-start.1 = (bf16[1024,256]{1,0:T(8,128)(2,1)S(1)}, bf16[1024,256]{1,0:T(8,128)(2,1)S(1)}, u32[]{:S(2)}, u32[]{:S(2)}) collective-permute-start(bf16[1024,256]{1,0:T(8,128)(2,1)S(1)} %collective-permute-done.refs_1_), channel_id=1, source_target_pairs={{0,4},{4,8},{8,12},{12,16},{16,20},{20,24},{24,28},{28,0},{1,5},{5... | collective-permute-start | bytes 1572872 | tf_op jit(solution)/shard_map/ppermute | solution.py:476
  19.8 17.7 %collective-permute-start.3 = (bf16[1024,256]{1,0:T(8,128)(2,1)S(1)}, bf16[1024,256]{1,0:T(8,128)(2,1)S(1)}, u32[]{:S(2)}, u32[]{:S(2)}) collective-permute-start(bf16[1024,256]{1,0:T(8,128)(2,1)S(1)} %collective-permute-done.2.refs_3_), channel_id=1, source_target_pairs={{0,28},{4,0},{8,4},{12,8},{16,12},{20,16},{24,20},{28,24},{1,29},{... | collective-permute-start | bytes 1572872 | tf_op jit(solution)/shard_map/ppermute | solution.py:476
  27.2 6.2 %collective-permute-start.5 = (f32[16,256]{1,0:T(8,128)S(1)}, f32[16,256]{1,0:T(8,128)S(1)}, u32[]{:S(2)}, u32[]{:S(2)}) collective-permute-start(f32[16,256]{1,0:T(8,128)S(1)} %get-tuple-element.64), channel_id=1, source_target_pairs={{0,32},{32,64},{64,96},{96,128},{128,160},{160,192},{192,224},{1,3... | collective-permute-start | bytes 49160 | tf_op jit(solution)/shard_map/ppermute | solution.py:480
  37.7 19.5 %collective-permute-start.14 = (bf16[2,128,2048]{2,1,0:T(8,128)(2,1)S(1)}, bf16[2,128,2048]{2,1,0:T(8,128)(2,1)S(1)}, u32[]{:S(2)}, u32[]{:S(2)}) collective-permute-start(bf16[2,128,2048]{2,1,0:T(8,128)(2,1)S(1)} %pad_maximum_fusion.refs_5_), channel_id=1, source_target_pairs={{0,32},{32,0},{64,96},{96,64},{128,160},{160,128},{192,224},{224,1... | collective-permute-start | bytes 3145736 | tf_op jit(solution)/shard_map/ppermute | solution.py:541
  39.8 17.5 %collective-permute-start.9 = (bf16[1024,256]{1,0:T(8,128)(2,1)S(1)}, bf16[1024,256]{1,0:T(8,128)(2,1)S(1)}, u32[]{:S(2)}, u32[]{:S(2)}) collective-permute-start(bf16[1024,256]{1,0:T(8,128)(2,1)S(1)} %collective-permute-done.1.refs_0_), channel_id=1, source_target_pairs={{0,4},{4,8},{8,12},{12,16},{16,20},{20,24},{24,28},{28,0},{1,5},{5... | collective-permute-start | bytes 1572872 | tf_op jit(solution)/shard_map/ppermute | solution.py:476
  39.8 17.5 %collective-permute-start.10 = (bf16[1024,256]{1,0:T(8,128)(2,1)S(1)}, bf16[1024,256]{1,0:T(8,128)(2,1)S(1)}, u32[]{:S(2)}, u32[]{:S(2)}) collective-permute-start(bf16[1024,256]{1,0:T(8,128)(2,1)S(1)} %collective-permute-done.3.refs_4_), channel_id=1, source_target_pairs={{0,28},{4,0},{8,4},{12,8},{16,12},{20,16},{24,20},{28,24},{1,29},{... | collective-permute-start | bytes 1572872 | tf_op jit(solution)/shard_map/ppermute | solution.py:476
  42.5 6.9 %collective-permute-start.13 = (f32[16,256]{1,0:T(8,128)S(1)}, f32[16,256]{1,0:T(8,128)S(1)}, u32[]{:S(2)}, u32[]{:S(2)}) collective-permute-start(f32[16,256]{1,0:T(8,128)S(1)} %fusion), channel_id=1, source_target_pairs={{0,128},{32,160},{64,192},{96,224},{1,129},{33,161},{65,193},{97,2... | collective-permute-start | bytes 49160 | tf_op jit(solution)/shard_map/ppermute | solution.py:480
  48.1 7.1 %collective-permute-start.12 = (bf16[64,2048]{1,0:T(8,128)(2,1)S(1)}, bf16[64,2048]{1,0:T(8,128)(2,1)S(1)}, u32[]{:S(2)}, u32[]{:S(2)}) collective-permute-start(bf16[64,2048]{1,0:T(8,128)(2,1)S(1)} %slice.37), channel_id=1, source_target_pairs={{0,3},{1,0},{2,1},{3,2},{4,7},{5,4},{6,5},{7,6},{8,11},{9,8},{10,9... | collective-permute-start | bytes 786440 | tf_op jit(solution)/shard_map/ppermute | solution.py:476
  49.5 7.8 %collective-permute-start.11 = (bf16[64,2048]{1,0:T(8,128)(2,1)S(1)}, bf16[64,2048]{1,0:T(8,128)(2,1)S(1)}, u32[]{:S(2)}, u32[]{:S(2)}) collective-permute-start(bf16[64,2048]{1,0:T(8,128)(2,1)S(1)} %slice.36), channel_id=1, source_target_pairs={{0,1},{1,2},{2,3},{3,0},{4,5},{5,6},{6,7},{7,4},{8,9},{9,10},{10,1... | collective-permute-start | bytes 786440 | tf_op jit(solution)/shard_map/ppermute | solution.py:476
  59.6 9.4 %collective-permute-start.15 = (bf16[512,256]{1,0:T(8,128)(2,1)S(1)}, bf16[512,256]{1,0:T(8,128)(2,1)S(1)}, u32[]{:S(2)}, u32[]{:S(2)}) collective-permute-start(bf16[512,256]{1,0:T(8,128)(2,1)S(1)} %slice.40), channel_id=1, source_target_pairs={{0,4},{4,8},{8,12},{12,16},{16,20},{20,24},{24,28},{28,0},{1,5},{5... | collective-permute-start | bytes 786440 | tf_op jit(solution)/shard_map/ppermute | solution.py:476
  59.9 9.1 %collective-permute-start.16 = (bf16[512,256]{1,0:T(8,128)(2,1)S(1)}, bf16[512,256]{1,0:T(8,128)(2,1)S(1)}, u32[]{:S(2)}, u32[]{:S(2)}) collective-permute-start(bf16[512,256]{1,0:T(8,128)(2,1)S(1)} %slice.41), channel_id=1, source_target_pairs={{0,28},{4,0},{8,4},{12,8},{16,12},{20,16},{24,20},{28,24},{1,29},{... | collective-permute-start | bytes 786440 | tf_op jit(solution)/shard_map/ppermute | solution.py:476
  70.3 8.9 %collective-permute-start.18 = (bf16[544,256]{1,0:T(8,128)(2,1)S(1)}, bf16[544,256]{1,0:T(8,128)(2,1)S(1)}, u32[]{:S(2)}, u32[]{:S(2)}) collective-permute-start(bf16[544,256]{1,0:T(8,128)(2,1)S(1)} %get-tuple-element.92), channel_id=1, source_target_pairs={{0,1},{1,2},{2,3},{3,0},{4,5},{5,6},{6,7},{7,4},{8,9},{9,10},{10,1... | collective-permute-start | bytes 835592 | tf_op jit(solution)/shard_map/ppermute | solution.py:476
  70.3 8.8 %collective-permute-start.19 = (bf16[544,256]{1,0:T(8,128)(2,1)S(1)}, bf16[544,256]{1,0:T(8,128)(2,1)S(1)}, u32[]{:S(2)}, u32[]{:S(2)}) collective-permute-start(bf16[544,256]{1,0:T(8,128)(2,1)S(1)} %get-tuple-element.93), channel_id=1, source_target_pairs={{0,3},{1,0},{2,1},{3,2},{4,7},{5,4},{6,5},{7,6},{8,11},{9,8},{10,9... | collective-permute-start | bytes 835592 | tf_op jit(solution)/shard_map/ppermute | solution.py:476
  76.4 11.9 %collective-permute-start.21 = (bf16[544,256]{1,0:T(8,128)(2,1)S(1)}, bf16[544,256]{1,0:T(8,128)(2,1)S(1)}, u32[]{:S(2)}, u32[]{:S(2)}) collective-permute-start(bf16[544,256]{1,0:T(8,128)(2,1)S(1)} %get-tuple-element.98), channel_id=1, source_target_pairs={{0,1},{1,2},{2,3},{3,0},{4,5},{5,6},{6,7},{7,4},{8,9},{9,10},{10,1... | collective-permute-start | bytes 835592 | tf_op jit(solution)/shard_map/ppermute | solution.py:476
  76.5 11.8 %collective-permute-start.22 = (bf16[544,256]{1,0:T(8,128)(2,1)S(1)}, bf16[544,256]{1,0:T(8,128)(2,1)S(1)}, u32[]{:S(2)}, u32[]{:S(2)}) collective-permute-start(bf16[544,256]{1,0:T(8,128)(2,1)S(1)} %get-tuple-element.99), channel_id=1, source_target_pairs={{0,3},{1,0},{2,1},{3,2},{4,7},{5,4},{6,5},{7,6},{8,11},{9,8},{10,9... | collective-permute-start | bytes 835592 | tf_op jit(solution)/shard_map/ppermute | solution.py:476
  80.0 10.5 %collective-permute-start.20 = (bf16[544,256]{1,0:T(8,128)(2,1)S(1)}, bf16[544,256]{1,0:T(8,128)(2,1)S(1)}, u32[]{:S(2)}, u32[]{:S(2)}) collective-permute-start(bf16[544,256]{1,0:T(8,128)(2,1)S(1)} %get-tuple-element.97), channel_id=1, source_target_pairs={{0,1},{1,2},{2,3},{3,0},{4,5},{5,6},{6,7},{7,4},{8,9},{9,10},{10,1... | collective-permute-start | bytes 835592 | tf_op jit(solution)/shard_map/ppermute | solution.py:476
  80.1 10.4 %collective-permute-start.23 = (bf16[544,256]{1,0:T(8,128)(2,1)S(1)}, bf16[544,256]{1,0:T(8,128)(2,1)S(1)}, u32[]{:S(2)}, u32[]{:S(2)}) collective-permute-start(bf16[544,256]{1,0:T(8,128)(2,1)S(1)} %get-tuple-element.100), channel_id=1, source_target_pairs={{0,3},{1,0},{2,1},{3,2},{4,7},{5,4},{6,5},{7,6},{8,11},{9,8},{10,9... | collective-permute-start | bytes 835592 | tf_op jit(solution)/shard_map/ppermute | solution.py:476
  82.8 6.4 %collective-permute-start.24 = (f32[2,8,256]{2,1,0:T(8,128)S(1)}, f32[2,8,256]{2,1,0:T(8,128)S(1)}, u32[]{:S(2)}, u32[]{:S(2)}) collective-permute-start(f32[2,8,256]{2,1,0:T(8,128)S(1)} %get-tuple-element.102), channel_id=1, source_target_pairs={{32,0},{64,32},{96,64},{128,96},{160,128},{192,160},{224,192},{33,... | collective-permute-start | bytes 49160 | tf_op jit(solution)/shard_map/ppermute | solution.py:480
  94.2 8.8 %collective-permute-start.25 = (f32[48,256]{1,0:T(8,128)S(1)}, f32[48,256]{1,0:T(8,128)S(1)}, u32[]{:S(2)}, u32[]{:S(2)}) collective-permute-start(f32[48,256]{1,0:T(8,128)S(1)} %pad_maximum_fusion.1), channel_id=1, source_target_pairs={{32,0},{64,32},{96,64},{128,96},{160,128},{192,160},{224,192},{33,... | collective-permute-start | bytes 147464 | tf_op jit(solution)/shard_map/ppermute | solution.py:480
  103.1 6.6 %collective-permute-start.28 = (f32[16,256]{1,0:T(8,128)S(1)}, f32[16,256]{1,0:T(8,128)S(1)}, u32[]{:S(2)}, u32[]{:S(2)}) collective-permute-start(f32[16,256]{1,0:T(8,128)S(1)} %fusion.1), channel_id=1, source_target_pairs={{160,0},{192,32},{224,64},{161,1},{193,33},{225,65},{162,2},{194,3... | collective-permute-start | bytes 49160 | tf_op jit(solution)/shard_map/ppermute | solution.py:480
  (14 other events, 169.0 us)

commit v4 on v3

--- a/solution.py
+++ b/solution.py
@@ -76,7 +76,7 @@
             return tuple(p * s + fresh for p, s in zip(poles, states))
 
         zero = jnp.zeros((PARTS, LANES), jnp.float32)
-        states = lax.fori_loop(0, steps, state_step, (zero,) * modes, unroll=4)
+        states = lax.fori_loop(0, steps, state_step, (zero,) * modes, unroll=8)
         for m in range(modes):
             ends_ref[m, :, lanes] = states[m]
     part_decay = power(poles_ref[...], steps)
@@ -112,7 +112,7 @@
             natural[block, pl.ds(i, PARTS, stride=steps), :] = total * qs_ref[rows, lanes]
             return states
 
-        lax.fori_loop(0, steps, step, tuple(first[m, :, lanes] for m in range(modes)), unroll=4)
+        lax.fori_loop(0, steps, step, tuple(first[m, :, lanes] for m in range(modes)), unroll=8)
     for block, lanes in lane_blocks(width):
         gated_ref[:, lanes] = natural[block].astype(gated_ref.dtype)
 
@@ -159,10 +159,10 @@
             return tuple(p * s + fresh for p, s in zip(poles, states))
 
         zero = jnp.zeros((PARTS, LANES), jnp.float32)
-        states = lax.fori_loop(0, steps - RIM, step, (zero,) * modes, unroll=4)
+        states = lax.fori_loop(0, steps - RIM, step, (zero,) * modes, unroll=8)
         for m in range(modes):
             rim_starts[m, :, lanes] = states[m]
-        states = lax.fori_loop(steps - RIM, steps, step, states, unroll=4)
+        states = lax.fori_loop(steps - RIM, steps, step, states, unroll=8)
         for m in range(modes):
             starts_ref[m, :, lanes] = states[m]
     part_decay = power(poles_ref[...], steps)
@@ -194,7 +194,7 @@
             return states
 
         zero = jnp.zeros((PARTS, LANES), jnp.float32)
-        lax.fori_loop(0, steps, step, (zero,) * modes, unroll=4)
+        lax.fori_loop(0, steps, step, (zero,) * modes, unroll=8)
 
 
 def short_back(value, rim, taps_ref, which, target, natural):
@@ -263,7 +263,7 @@
             product[rows, lanes] = local_ref[rows, lanes] + added(fading)
             return fading
 
-        lax.fori_loop(0, steps, step, tuple(last[m, :, lanes] for m in range(modes)), unroll=4)
+        lax.fori_loop(0, steps, step, tuple(last[m, :, lanes] for m in range(modes)), unroll=8)
     for which, other, target in ((1, vs_ref, gk_ref), (2, ks_ref, gv_ref)):
         short_back(
             lambda rows, lanes: product[rows, lanes] * other[rows, lanes],

time: 115 us -> 115 us (level)
  transfers between devices with their start and end apart: 29 -> 29, of which waited for: 9 -> 10; matrix products, arithmetic and copies ran while one was open for 1% -> 1% of each run, Pallas kernels for 20% -> 20%
where the time goes in v4:
time: 115 us; the launch traced here: 114 us
  starting transfers between devices  62.2 us (54%)
  Pallas kernels  32.8 us (29%)
  waiting for transfers between devices  14.3 us (12%)
  local copies, waits for them, and re-layouts  3.83 us (3%)
    ppermute x9, starting transfers between devices, from_behind(): lax.ppermute(block, axis, [(i - distance, i) for i in range(size) if 0 <=...  30.5 us
    pallas_call x12, Pallas kernels, local_call(): pl.pallas_call(kernel, out_shape=outs, in_specs=[whole if o.ndim > 1 else...  29.9 us
    ppermute x18, starting transfers between devices, shift(): lax.ppermute(block, axis, [(i, (i + distance) % size) for i in range(size)])  27.4 us
    ppermute x18, waiting for transfers between devices, shift(): lax.ppermute(block, axis, [(i, (i + distance) % size) for i in range(size)])  8.35 us
    ppermute x9, waiting for transfers between devices, from_behind(): lax.ppermute(block, axis, [(i - distance, i) for i in range(size) if 0 <=...  5.99 us
  transfers between devices with their start and end apart: 29, of which 10 were waited for; matrix products, arithmetic and copies ran while one was open for 1% of the time, Pallas kernels for 20%

profile of v4, /device:TPU:1, one launch (start us, length us, event | category | flops | bytes accessed | tf_op | source)
XLA Modules:
  0.0 114.5 jit_solution(15236427086256087211)
XLA Ops:
  0.7 2.5 %collective-permute-start = (bf16[1024,256]{1,0:T(8,128)(2,1)}, bf16[1024,256]{1,0:T(8,128)(2,1)S(1)}, u32[]{:S(2)}, u32[]{:S(2)}) collective-permute-start(bf16[1024,256]{1,0:T(8,128)(2,1)} %refs_2_.1), channel_id=1, source_target_pairs={{0,4},{4,8},{8,12},{12,16},{16,20},{20,24},{24,28},{28,0},{1,5},{5... | collective-permute-start | bytes 1572872 | tf_op jit(solution)/shard_map/ppermute | solution.py:476
  3.2 4.0 %collective-permute-start.2 = (bf16[1024,256]{1,0:T(8,128)(2,1)}, bf16[1024,256]{1,0:T(8,128)(2,1)S(1)}, u32[]{:S(2)}, u32[]{:S(2)}) collective-permute-start(bf16[1024,256]{1,0:T(8,128)(2,1)} %refs_2_.1), channel_id=1, source_target_pairs={{0,28},{4,0},{8,4},{12,8},{16,12},{20,16},{24,20},{28,24},{1,29},{... | collective-permute-start | bytes 1572872 | tf_op jit(solution)/shard_map/ppermute | solution.py:476
  8.6 4.0 %collective-permute-start.4 = (bf16[3,16,256]{2,1,0:T(8,128)(2,1)S(1)}, bf16[3,16,256]{2,1,0:T(8,128)(2,1)S(1)}, u32[]{:S(2)}, u32[]{:S(2)}) collective-permute-start(bf16[3,16,256]{2,1,0:T(8,128)(2,1)S(1)} %pad_maximum_fusion.2), channel_id=1, source_target_pairs={{0,32},{32,64},{64,96},{96,128},{128,160},{160,192},{192,224},{1,3... | collective-permute-start | bytes 73736 | tf_op jit(solution)/shard_map/ppermute | solution.py:480
  13.6 2.2 %copy-done = bf16[256,8192]{1,0:T(8,128)(2,1)S(1)} copy-done((bf16[256,8192]{1,0:T(8,128)(2,1)S(1)}, bf16[256,8192]{1,0:T(8,128)(2,1)}, u32[]{:S(2)}) %copy-start) | copy-done | bytes 4194328
  19.8 2.7 %collective-permute-start.3 = (bf16[1024,256]{1,0:T(8,128)(2,1)S(1)}, bf16[1024,256]{1,0:T(8,128)(2,1)S(1)}, u32[]{:S(2)}, u32[]{:S(2)}) collective-permute-start(bf16[1024,256]{1,0:T(8,128)(2,1)S(1)} %collective-permute-done.2.refs_3_), channel_id=1, source_target_pairs={{0,28},{4,0},{8,4},{12,8},{16,12},{20,16},{24,20},{28,24},{1,29},{... | collective-permute-start | bytes 1572872 | tf_op jit(solution)/shard_map/ppermute | solution.py:476
  22.5 4.6 %shard_map.111 = (f32[1024,256]{1,0:T(8,128)S(1)}, f32[1024,256]{1,0:T(8,128)S(1)}, f32[1024,256]{1,0:T(8,128)S(1)}, f32[16,8,256]{2,1,0:T(8,128)S(1)}, f32[16,256]{1,0:T(8,128)S(1)}, /*index=5*/f32[2,8,256]{2,1,0:T(8,128)S(1)}) custom-call(bf16[1024,256]{1,0:T(8,128)(2,1)S(1)} %copy-done.3, bf16[1024,256]{1,0:T(8,128)(2,1)S(1)} %copy-done.4, ...), custom_call_target="tpu_custom_call" | custom-call | flops 20971520 | bytes 327680 | tf_op jit(solution)/shard_map/pallas_call | solution.py:460
  27.1 5.3 %collective-permute-start.5 = (f32[16,256]{1,0:T(8,128)S(1)}, f32[16,256]{1,0:T(8,128)S(1)}, u32[]{:S(2)}, u32[]{:S(2)}) collective-permute-start(f32[16,256]{1,0:T(8,128)S(1)} %get-tuple-element.64), channel_id=1, source_target_pairs={{0,32},{32,64},{64,96},{96,128},{128,160},{160,192},{192,224},{1,3... | collective-permute-start | bytes 49160 | tf_op jit(solution)/shard_map/ppermute | solution.py:480
  33.3 3.2 %collective-permute-start.6 = (f32[16,256]{1,0:T(8,128)S(1)}, f32[16,256]{1,0:T(8,128)S(1)}, u32[]{:S(2)}, u32[]{:S(2)}) collective-permute-start(f32[16,256]{1,0:T(8,128)S(1)} %multiply_add_fusion.2), channel_id=1, source_target_pairs={{0,64},{32,96},{64,128},{96,160},{128,192},{160,224},{1,65},{33,97... | collective-permute-start | bytes 49160 | tf_op jit(solution)/shard_map/ppermute | solution.py:480
  39.7 2.7 %collective-permute-start.10 = (bf16[1024,256]{1,0:T(8,128)(2,1)S(1)}, bf16[1024,256]{1,0:T(8,128)(2,1)S(1)}, u32[]{:S(2)}, u32[]{:S(2)}) collective-permute-start(bf16[1024,256]{1,0:T(8,128)(2,1)S(1)} %collective-permute-done.3.refs_4_), channel_id=1, source_target_pairs={{0,28},{4,0},{8,4},{12,8},{16,12},{20,16},{24,20},{28,24},{1,29},{... | collective-permute-start | bytes 1572872 | tf_op jit(solution)/shard_map/ppermute | solution.py:476
  42.4 5.5 %collective-permute-start.13 = (f32[16,256]{1,0:T(8,128)S(1)}, f32[16,256]{1,0:T(8,128)S(1)}, u32[]{:S(2)}, u32[]{:S(2)}) collective-permute-start(f32[16,256]{1,0:T(8,128)S(1)} %fusion), channel_id=1, source_target_pairs={{0,128},{32,160},{64,192},{96,224},{1,129},{33,161},{65,193},{97,2... | collective-permute-start | bytes 49160 | tf_op jit(solution)/shard_map/ppermute | solution.py:480
  51.2 3.6 %shard_map.114 = (f32[1024,256]{1,0:T(8,128)S(1)}, bf16[1024,256]{1,0:T(8,128)(2,1)}) custom-call(f32[1024,256]{1,0:T(8,128)S(1)} %get-tuple-element.74.qs_ref, f32[1024,256]{1,0:T(8,128)S(1)} %get-tuple-element.75.ks_ref, f32[1024,256]{1,0:T(8,128)S(1)} %get-tuple-element.76.vs_ref, f32[16,8,256]{2,1,0:T(8,128)S(1)} %get-tuple-element.77.ends_ref, ...), custom_call_target="tpu_custom_call" | custom-call | flops 18350080 | bytes 286720 | tf_op jit(solution)/shard_map/pallas_call | solution.py:460
  57.2 2.2 %collective-permute-start.17 = (bf16[128,2048]{1,0:T(8,128)(2,1)S(1)}, bf16[128,2048]{1,0:T(8,128)(2,1)S(1)}, u32[]{:S(2)}, u32[]{:S(2)}) collective-permute-start(bf16[128,2048]{1,0:T(8,128)(2,1)S(1)} %constant_dynamic-update-slice_fusion.refs_3_.share_ref), channel_id=1, source_target_pairs={{0,32},{32,0},{64,96},{96,64},{128,160},{160,128},{192,224},{224,1... | collective-permute-start | bytes 1572872 | tf_op jit(solution)/shard_map/ppermute | solution.py:572
  59.7 2.7 %collective-permute-start.16 = (bf16[512,256]{1,0:T(8,128)(2,1)S(1)}, bf16[512,256]{1,0:T(8,128)(2,1)S(1)}, u32[]{:S(2)}, u32[]{:S(2)}) collective-permute-start(bf16[512,256]{1,0:T(8,128)(2,1)S(1)} %slice.41), channel_id=1, source_target_pairs={{0,28},{4,0},{8,4},{12,8},{16,12},{20,16},{24,20},{28,24},{1,29},{... | collective-permute-start | bytes 786440 | tf_op jit(solution)/shard_map/ppermute | solution.py:476
  64.2 4.7 %collective-permute-done.15.refs_3_.middle_up_ref.refs_2_ = bf16[512,256]{1,0:T(8,128)(2,1)S(1)} collective-permute-done((bf16[512,256]{1,0:T(8,128)(2,1)S(1)}, bf16[512,256]{1,0:T(8,128)(2,1)S(1)}, u32[]{:S(2)}, u32[]{:S(2)}) %collective-permute-start.15) | collective-permute-done | bytes 262176 | tf_op jit(solution)/shard_map/ppermute | solution.py:476
  70.2 2.7 %collective-permute-start.19 = (bf16[544,256]{1,0:T(8,128)(2,1)S(1)}, bf16[544,256]{1,0:T(8,128)(2,1)S(1)}, u32[]{:S(2)}, u32[]{:S(2)}) collective-permute-start(bf16[544,256]{1,0:T(8,128)(2,1)S(1)} %get-tuple-element.93), channel_id=1, source_target_pairs={{0,3},{1,0},{2,1},{3,2},{4,7},{5,4},{6,5},{7,6},{8,11},{9,8},{10,9... | collective-permute-start | bytes 835592 | tf_op jit(solution)/shard_map/ppermute | solution.py:476
  72.9 3.0 %shard_map.116 = (f32[1024,256]{1,0:T(8,128)S(1)}, f32[1024,256]{1,0:T(8,128)S(1)}) custom-call(s32[4]{0:T(128)S(1)} %pad_add_fusion.place_ref, bf16[5,1024,256]{2,1,0:T(8,128)(2,1)S(1)} %get-tuple-element.81.refs_0_, bf16[1024,256]{1,0:T(8,128)(2,1)S(1)} %collective-permute-done.10.refs_1_.refs_0_, ...), custom_call_target="tpu_custom_call" | custom-call | flops 2147483648 | bytes 33554432 | tf_op jit(solution)/shard_map/pallas_call | solution.py:460
  76.4 2.7 %collective-permute-start.22 = (bf16[544,256]{1,0:T(8,128)(2,1)S(1)}, bf16[544,256]{1,0:T(8,128)(2,1)S(1)}, u32[]{:S(2)}, u32[]{:S(2)}) collective-permute-start(bf16[544,256]{1,0:T(8,128)(2,1)S(1)} %get-tuple-element.99), channel_id=1, source_target_pairs={{0,3},{1,0},{2,1},{3,2},{4,7},{5,4},{6,5},{7,6},{8,11},{9,8},{10,9... | collective-permute-start | bytes 835592 | tf_op jit(solution)/shard_map/ppermute | solution.py:476
  80.0 2.7 %collective-permute-start.23 = (bf16[544,256]{1,0:T(8,128)(2,1)S(1)}, bf16[544,256]{1,0:T(8,128)(2,1)S(1)}, u32[]{:S(2)}, u32[]{:S(2)}) collective-permute-start(bf16[544,256]{1,0:T(8,128)(2,1)S(1)} %get-tuple-element.100), channel_id=1, source_target_pairs={{0,3},{1,0},{2,1},{3,2},{4,7},{5,4},{6,5},{7,6},{8,11},{9,8},{10,9... | collective-permute-start | bytes 835592 | tf_op jit(solution)/shard_map/ppermute | solution.py:476
  82.6 4.4 %collective-permute-start.24 = (f32[2,8,256]{2,1,0:T(8,128)S(1)}, f32[2,8,256]{2,1,0:T(8,128)S(1)}, u32[]{:S(2)}, u32[]{:S(2)}) collective-permute-start(f32[2,8,256]{2,1,0:T(8,128)S(1)} %get-tuple-element.102), channel_id=1, source_target_pairs={{32,0},{64,32},{96,64},{128,96},{160,128},{192,160},{224,192},{33,... | collective-permute-start | bytes 49160 | tf_op jit(solution)/shard_map/ppermute | solution.py:480
  90.3 3.4 %shard_map.121 = (f32[1024,256]{1,0:T(8,128)S(1)}, f32[16,8,256]{2,1,0:T(8,128)S(1)}, f32[16,256]{1,0:T(8,128)S(1)}, f32[32,256]{1,0:T(8,128)S(1)}) custom-call(f32[1024,256]{1,0:T(8,128)S(1)} %shard_map.120.kept_ref, bf16[544,256]{1,0:T(8,128)(2,1)S(1)} %collective-permute-done.20.one_up_ref, bf16[544,256]{1,0:T(8,128)(2,1)S(1)} %collective-permute-done.21.one_down_ref, ...), custom_call_target="tpu_custom_call" | custom-call | flops 10485760 | bytes 163840 | tf_op jit(solution)/shard_map/pallas_call | solution.py:460
  93.7 4.2 %collective-permute-start.25 = (f32[48,256]{1,0:T(8,128)S(1)}, f32[48,256]{1,0:T(8,128)S(1)}, u32[]{:S(2)}, u32[]{:S(2)}) collective-permute-start(f32[48,256]{1,0:T(8,128)S(1)} %pad_maximum_fusion.1), channel_id=1, source_target_pairs={{32,0},{64,32},{96,64},{128,96},{160,128},{192,160},{224,192},{33,... | collective-permute-start | bytes 147464 | tf_op jit(solution)/shard_map/ppermute | solution.py:480
  99.2 2.4 %shard_map.122.local_ref = f32[1024,256]{1,0:T(8,128)S(1)} custom-call(f32[1024,256]{1,0:T(8,128)S(1)} %get-tuple-element.111.mixed_ref, f32[1024,256]{1,0:T(8,128)S(1)} %get-tuple-element.74.qs_ref, f32[16,256]{1,0:T(8,128)S(1)} %copy-done.2, f32[16,256]{1,0:T(8,128)S(1)} %copy-done.8), custom_call_target="tpu_custom_call" | custom-call | flops 16777216 | bytes 262144 | tf_op jit(solution)/shard_map/pallas_call | solution.py:460
  105.2 2.2 %shard_map.123 = bf16[1024,256]{1,0:T(8,128)(2,1)} custom-call(f32[1024,256]{1,0:T(8,128)S(1)} %get-tuple-element.111.mixed_ref, f32[1024,256]{1,0:T(8,128)S(1)} %get-tuple-element.108.long_ref, f32[32,256]{1,0:T(8,128)S(1)} %slice.43.next_ref, f32[3,7,256]{2,1,0:T(8,128)S(1)} %copy-done.7), custom_call_target="tpu_custom_call" | custom-call | flops 5242880 | bytes 81920 | tf_op jit(solution)/shard_map/pallas_call | solution.py:460
  109.2 5.3 %shard_map.124 = (bf16[1024,256]{1,0:T(8,128)(2,1)}, bf16[1024,256]{1,0:T(8,128)(2,1)}) custom-call(f32[1024,256]{1,0:T(8,128)S(1)} %shard_map.122.local_ref, f32[1024,256]{1,0:T(8,128)S(1)} %get-tuple-element.75.ks_ref, f32[1024,256]{1,0:T(8,128)S(1)} %get-tuple-element.76.vs_ref, f32[16,8,256]{2,1,0:T(8,128)S(1)} %get-tuple-element.116.starts_ref, ...), custom_call_target="tpu_custom_call" | custom-call | flops 20971520 | bytes 327680 | tf_op jit(solution)/shard_map/pallas_call | solution.py:460
  (86 shorter events, 30.6 us)
Async XLA Ops:
  0.7 19.2 %collective-permute-start = (bf16[1024,256]{1,0:T(8,128)(2,1)}, bf16[1024,256]{1,0:T(8,128)(2,1)S(1)}, u32[]{:S(2)}, u32[]{:S(2)}) collective-permute-start(bf16[1024,256]{1,0:T(8,128)(2,1)} %refs_2_.1), channel_id=1, source_target_pairs={{0,4},{4,8},{8,12},{12,16},{16,20},{20,24},{24,28},{28,0},{1,5},{5... | collective-permute-start | bytes 1572872 | tf_op jit(solution)/shard_map/ppermute | solution.py:476
  3.2 16.6 %collective-permute-start.2 = (bf16[1024,256]{1,0:T(8,128)(2,1)}, bf16[1024,256]{1,0:T(8,128)(2,1)S(1)}, u32[]{:S(2)}, u32[]{:S(2)}) collective-permute-start(bf16[1024,256]{1,0:T(8,128)(2,1)} %refs_2_.1), channel_id=1, source_target_pairs={{0,28},{4,0},{8,4},{12,8},{16,12},{20,16},{24,20},{28,24},{1,29},{... | collective-permute-start | bytes 1572872 | tf_op jit(solution)/shard_map/ppermute | solution.py:476
  17.0 20.3 %collective-permute-start.7 = (bf16[192,2048]{1,0:T(8,128)(2,1)S(1)}, bf16[192,2048]{1,0:T(8,128)(2,1)S(1)}, u32[]{:S(2)}, u32[]{:S(2)}) collective-permute-start(bf16[192,2048]{1,0:T(8,128)(2,1)S(1)} %get-tuple-element.66), channel_id=1, source_target_pairs={{0,1},{1,2},{2,3},{3,0},{4,5},{5,6},{6,7},{7,4},{8,9},{9,10},{10,1... | collective-permute-start | bytes 2359304 | tf_op jit(solution)/shard_map/ppermute | solution.py:476
  18.3 19.0 %collective-permute-start.8 = (bf16[192,2048]{1,0:T(8,128)(2,1)S(1)}, bf16[192,2048]{1,0:T(8,128)(2,1)S(1)}, u32[]{:S(2)}, u32[]{:S(2)}) collective-permute-start(bf16[192,2048]{1,0:T(8,128)(2,1)S(1)} %get-tuple-element.67), channel_id=1, source_target_pairs={{0,3},{1,0},{2,1},{3,2},{4,7},{5,4},{6,5},{7,6},{8,11},{9,8},{10,9... | collective-permute-start | bytes 2359304 | tf_op jit(solution)/shard_map/ppermute | solution.py:476
  19.8 17.6 %collective-permute-start.1 = (bf16[1024,256]{1,0:T(8,128)(2,1)S(1)}, bf16[1024,256]{1,0:T(8,128)(2,1)S(1)}, u32[]{:S(2)}, u32[]{:S(2)}) collective-permute-start(bf16[1024,256]{1,0:T(8,128)(2,1)S(1)} %collective-permute-done.refs_1_), channel_id=1, source_target_pairs={{0,4},{4,8},{8,12},{12,16},{16,20},{20,24},{24,28},{28,0},{1,5},{5... | collective-permute-start | bytes 1572872 | tf_op jit(solution)/shard_map/ppermute | solution.py:476
  19.8 17.6 %collective-permute-start.3 = (bf16[1024,256]{1,0:T(8,128)(2,1)S(1)}, bf16[1024,256]{1,0:T(8,128)(2,1)S(1)}, u32[]{:S(2)}, u32[]{:S(2)}) collective-permute-start(bf16[1024,256]{1,0:T(8,128)(2,1)S(1)} %collective-permute-done.2.refs_3_), channel_id=1, source_target_pairs={{0,28},{4,0},{8,4},{12,8},{16,12},{20,16},{24,20},{28,24},{1,29},{... | collective-permute-start | bytes 1572872 | tf_op jit(solution)/shard_map/ppermute | solution.py:476
  27.1 6.2 %collective-permute-start.5 = (f32[16,256]{1,0:T(8,128)S(1)}, f32[16,256]{1,0:T(8,128)S(1)}, u32[]{:S(2)}, u32[]{:S(2)}) collective-permute-start(f32[16,256]{1,0:T(8,128)S(1)} %get-tuple-element.64), channel_id=1, source_target_pairs={{0,32},{32,64},{64,96},{96,128},{128,160},{160,192},{192,224},{1,3... | collective-permute-start | bytes 49160 | tf_op jit(solution)/shard_map/ppermute | solution.py:480
  37.6 19.5 %collective-permute-start.14 = (bf16[2,128,2048]{2,1,0:T(8,128)(2,1)S(1)}, bf16[2,128,2048]{2,1,0:T(8,128)(2,1)S(1)}, u32[]{:S(2)}, u32[]{:S(2)}) collective-permute-start(bf16[2,128,2048]{2,1,0:T(8,128)(2,1)S(1)} %pad_maximum_fusion.refs_5_), channel_id=1, source_target_pairs={{0,32},{32,0},{64,96},{96,64},{128,160},{160,128},{192,224},{224,1... | collective-permute-start | bytes 3145736 | tf_op jit(solution)/shard_map/ppermute | solution.py:541
  39.7 17.5 %collective-permute-start.9 = (bf16[1024,256]{1,0:T(8,128)(2,1)S(1)}, bf16[1024,256]{1,0:T(8,128)(2,1)S(1)}, u32[]{:S(2)}, u32[]{:S(2)}) collective-permute-start(bf16[1024,256]{1,0:T(8,128)(2,1)S(1)} %collective-permute-done.1.refs_0_), channel_id=1, source_target_pairs={{0,4},{4,8},{8,12},{12,16},{16,20},{20,24},{24,28},{28,0},{1,5},{5... | collective-permute-start | bytes 1572872 | tf_op jit(solution)/shard_map/ppermute | solution.py:476
  39.7 17.5 %collective-permute-start.10 = (bf16[1024,256]{1,0:T(8,128)(2,1)S(1)}, bf16[1024,256]{1,0:T(8,128)(2,1)S(1)}, u32[]{:S(2)}, u32[]{:S(2)}) collective-permute-start(bf16[1024,256]{1,0:T(8,128)(2,1)S(1)} %collective-permute-done.3.refs_4_), channel_id=1, source_target_pairs={{0,28},{4,0},{8,4},{12,8},{16,12},{20,16},{24,20},{28,24},{1,29},{... | collective-permute-start | bytes 1572872 | tf_op jit(solution)/shard_map/ppermute | solution.py:476
  42.4 6.9 %collective-permute-start.13 = (f32[16,256]{1,0:T(8,128)S(1)}, f32[16,256]{1,0:T(8,128)S(1)}, u32[]{:S(2)}, u32[]{:S(2)}) collective-permute-start(f32[16,256]{1,0:T(8,128)S(1)} %fusion), channel_id=1, source_target_pairs={{0,128},{32,160},{64,192},{96,224},{1,129},{33,161},{65,193},{97,2... | collective-permute-start | bytes 49160 | tf_op jit(solution)/shard_map/ppermute | solution.py:480
  48.0 7.0 %collective-permute-start.12 = (bf16[64,2048]{1,0:T(8,128)(2,1)S(1)}, bf16[64,2048]{1,0:T(8,128)(2,1)S(1)}, u32[]{:S(2)}, u32[]{:S(2)}) collective-permute-start(bf16[64,2048]{1,0:T(8,128)(2,1)S(1)} %slice.37), channel_id=1, source_target_pairs={{0,3},{1,0},{2,1},{3,2},{4,7},{5,4},{6,5},{7,6},{8,11},{9,8},{10,9... | collective-permute-start | bytes 786440 | tf_op jit(solution)/shard_map/ppermute | solution.py:476
  49.3 7.8 %collective-permute-start.11 = (bf16[64,2048]{1,0:T(8,128)(2,1)S(1)}, bf16[64,2048]{1,0:T(8,128)(2,1)S(1)}, u32[]{:S(2)}, u32[]{:S(2)}) collective-permute-start(bf16[64,2048]{1,0:T(8,128)(2,1)S(1)} %slice.36), channel_id=1, source_target_pairs={{0,1},{1,2},{2,3},{3,0},{4,5},{5,6},{6,7},{7,4},{8,9},{9,10},{10,1... | collective-permute-start | bytes 786440 | tf_op jit(solution)/shard_map/ppermute | solution.py:476
  59.5 9.4 %collective-permute-start.15 = (bf16[512,256]{1,0:T(8,128)(2,1)S(1)}, bf16[512,256]{1,0:T(8,128)(2,1)S(1)}, u32[]{:S(2)}, u32[]{:S(2)}) collective-permute-start(bf16[512,256]{1,0:T(8,128)(2,1)S(1)} %slice.40), channel_id=1, source_target_pairs={{0,4},{4,8},{8,12},{12,16},{16,20},{20,24},{24,28},{28,0},{1,5},{5... | collective-permute-start | bytes 786440 | tf_op jit(solution)/shard_map/ppermute | solution.py:476
  59.7 9.1 %collective-permute-start.16 = (bf16[512,256]{1,0:T(8,128)(2,1)S(1)}, bf16[512,256]{1,0:T(8,128)(2,1)S(1)}, u32[]{:S(2)}, u32[]{:S(2)}) collective-permute-start(bf16[512,256]{1,0:T(8,128)(2,1)S(1)} %slice.41), channel_id=1, source_target_pairs={{0,28},{4,0},{8,4},{12,8},{16,12},{20,16},{24,20},{28,24},{1,29},{... | collective-permute-start | bytes 786440 | tf_op jit(solution)/shard_map/ppermute | solution.py:476
  70.1 8.9 %collective-permute-start.18 = (bf16[544,256]{1,0:T(8,128)(2,1)S(1)}, bf16[544,256]{1,0:T(8,128)(2,1)S(1)}, u32[]{:S(2)}, u32[]{:S(2)}) collective-permute-start(bf16[544,256]{1,0:T(8,128)(2,1)S(1)} %get-tuple-element.92), channel_id=1, source_target_pairs={{0,1},{1,2},{2,3},{3,0},{4,5},{5,6},{6,7},{7,4},{8,9},{9,10},{10,1... | collective-permute-start | bytes 835592 | tf_op jit(solution)/shard_map/ppermute | solution.py:476
  70.2 8.8 %collective-permute-start.19 = (bf16[544,256]{1,0:T(8,128)(2,1)S(1)}, bf16[544,256]{1,0:T(8,128)(2,1)S(1)}, u32[]{:S(2)}, u32[]{:S(2)}) collective-permute-start(bf16[544,256]{1,0:T(8,128)(2,1)S(1)} %get-tuple-element.93), channel_id=1, source_target_pairs={{0,3},{1,0},{2,1},{3,2},{4,7},{5,4},{6,5},{7,6},{8,11},{9,8},{10,9... | collective-permute-start | bytes 835592 | tf_op jit(solution)/shard_map/ppermute | solution.py:476
  76.3 11.9 %collective-permute-start.21 = (bf16[544,256]{1,0:T(8,128)(2,1)S(1)}, bf16[544,256]{1,0:T(8,128)(2,1)S(1)}, u32[]{:S(2)}, u32[]{:S(2)}) collective-permute-start(bf16[544,256]{1,0:T(8,128)(2,1)S(1)} %get-tuple-element.98), channel_id=1, source_target_pairs={{0,1},{1,2},{2,3},{3,0},{4,5},{5,6},{6,7},{7,4},{8,9},{9,10},{10,1... | collective-permute-start | bytes 835592 | tf_op jit(solution)/shard_map/ppermute | solution.py:476
  76.4 11.8 %collective-permute-start.22 = (bf16[544,256]{1,0:T(8,128)(2,1)S(1)}, bf16[544,256]{1,0:T(8,128)(2,1)S(1)}, u32[]{:S(2)}, u32[]{:S(2)}) collective-permute-start(bf16[544,256]{1,0:T(8,128)(2,1)S(1)} %get-tuple-element.99), channel_id=1, source_target_pairs={{0,3},{1,0},{2,1},{3,2},{4,7},{5,4},{6,5},{7,6},{8,11},{9,8},{10,9... | collective-permute-start | bytes 835592 | tf_op jit(solution)/shard_map/ppermute | solution.py:476
  79.9 10.5 %collective-permute-start.20 = (bf16[544,256]{1,0:T(8,128)(2,1)S(1)}, bf16[544,256]{1,0:T(8,128)(2,1)S(1)}, u32[]{:S(2)}, u32[]{:S(2)}) collective-permute-start(bf16[544,256]{1,0:T(8,128)(2,1)S(1)} %get-tuple-element.97), channel_id=1, source_target_pairs={{0,1},{1,2},{2,3},{3,0},{4,5},{5,6},{6,7},{7,4},{8,9},{9,10},{10,1... | collective-permute-start | bytes 835592 | tf_op jit(solution)/shard_map/ppermute | solution.py:476
  80.0 10.4 %collective-permute-start.23 = (bf16[544,256]{1,0:T(8,128)(2,1)S(1)}, bf16[544,256]{1,0:T(8,128)(2,1)S(1)}, u32[]{:S(2)}, u32[]{:S(2)}) collective-permute-start(bf16[544,256]{1,0:T(8,128)(2,1)S(1)} %get-tuple-element.100), channel_id=1, source_target_pairs={{0,3},{1,0},{2,1},{3,2},{4,7},{5,4},{6,5},{7,6},{8,11},{9,8},{10,9... | collective-permute-start | bytes 835592 | tf_op jit(solution)/shard_map/ppermute | solution.py:476
  82.6 6.4 %collective-permute-start.24 = (f32[2,8,256]{2,1,0:T(8,128)S(1)}, f32[2,8,256]{2,1,0:T(8,128)S(1)}, u32[]{:S(2)}, u32[]{:S(2)}) collective-permute-start(f32[2,8,256]{2,1,0:T(8,128)S(1)} %get-tuple-element.102), channel_id=1, source_target_pairs={{32,0},{64,32},{96,64},{128,96},{160,128},{192,160},{224,192},{33,... | collective-permute-start | bytes 49160 | tf_op jit(solution)/shard_map/ppermute | solution.py:480
  93.7 8.8 %collective-permute-start.25 = (f32[48,256]{1,0:T(8,128)S(1)}, f32[48,256]{1,0:T(8,128)S(1)}, u32[]{:S(2)}, u32[]{:S(2)}) collective-permute-start(f32[48,256]{1,0:T(8,128)S(1)} %pad_maximum_fusion.1), channel_id=1, source_target_pairs={{32,0},{64,32},{96,64},{128,96},{160,128},{192,160},{224,192},{33,... | collective-permute-start | bytes 147464 | tf_op jit(solution)/shard_map/ppermute | solution.py:480
  102.6 6.6 %collective-permute-start.28 = (f32[16,256]{1,0:T(8,128)S(1)}, f32[16,256]{1,0:T(8,128)S(1)}, u32[]{:S(2)}, u32[]{:S(2)}) collective-permute-start(f32[16,256]{1,0:T(8,128)S(1)} %fusion.1), channel_id=1, source_target_pairs={{160,0},{192,32},{224,64},{161,1},{193,33},{225,65},{162,2},{194,3... | collective-permute-start | bytes 49160 | tf_op jit(solution)/shard_map/ppermute | solution.py:480
  (14 other events, 168.7 us)
